TPU v7x, 32 devices: a whole 2x2x4 slice. The times are simulated.
32 devices in a mesh: grp: 8 (over z, x), row: 4 (over y, core).
Axes of the slice: x: 2, y: 2, z: 4, core: 2. Of those that a mesh axis runs over, the one named last changes fastest.
Arguments:
- features: bfloat16 [262144, 512], P(('grp', 'row')), may hold values from -6 to 6
- precinct: int32 [262144], P(('grp', 'row')), may hold values from 0 to 1023
- outcome: int32 [262144], P(('grp', 'row')), may hold values from 0 to 7
- row_counts: int32 [8, 4], P('grp', 'row'), may hold values from 2048 to 8192, as said below
- beta: float32 [512], replicated, may hold values from -0.125 to 0.125
- nation_coef: float32 [4, 512], replicated, may hold values from -0.125 to 0.125
- state_coef: float32 [64, 512], replicated, may hold values from -0.125 to 0.125
- county_coef: float32 [2048, 512], P('grp'), may hold values from -0.125 to 0.125
- precinct_coef: float32 [8192], P('grp'), may hold values from -3 to 3
- precinct_county: int32 [8192], P('grp'), may hold values from 0 to 255, as said below
- county_state: int32 [2048], replicated, may hold values from 0 to 63, as said below
- state_nation: int32 [64], replicated, may hold values from 0 to 3, as said below
Outputs:
- county_grad: float32 [2048, 512], P(('grp', 'row'))
- precinct_grad: float32 [8192], P('grp')
- state_grad: float32 [64, 512], replicated
- nation_grad: float32 [4, 512], replicated
- beta_grad: float32 [512], replicated
Inputs may be any that keep to these rules, and one draw needn't show every extreme that they name: `precinct_county`: non-decreasing within each block of 1024 precincts; each block has 0 first and 255 last. `county_state`: non-decreasing, 0 first and 63 last. `state_nation`: non-decreasing, 0 first and 3 last. `row_counts`: some device block is full and some other holds exactly 2048 live rows.
All inputs are finite; a program needn't handle non-finite values.
Results may differ from a plain program's by a relative error of at most 0.006.
Values sent between devices are 32-bit elements; how exact they have to be, the bound alone decides.
No kernel may reach another device: no remote copies, remote signals or barrier semaphores. Data moves between devices by JAX's collectives and lax.ppermute only.
A program may use at most 64 MiB of HBM per device.

v0:
```python
import jax
import jax.numpy as jnp
from jax import lax
from jax.sharding import PartitionSpec as P


def on_device(
    features,
    precinct,
    outcome,
    row_counts,
    beta,
    nation_coef,
    state_coef,
    county_coef,
    precinct_coef,
    precinct_county,
    county_state,
    state_nation,
):
    rows_here = features.shape[0]
    cnt_here = county_coef.shape[0]
    prec_here = precinct_coef.shape[0]
    n_states = state_coef.shape[0]
    n_nations = nation_coef.shape[0]
    grp_index = lax.axis_index("grp")
    row_index = lax.axis_index("row")
    row_split = lax.axis_size("row")
    share_rows = cnt_here // row_split
    high = lax.Precision.HIGHEST
    local_states = lax.dynamic_slice_in_dim(county_state, grp_index * cnt_here, cnt_here, 0)
    state_hot = (local_states[:, None] == jnp.arange(n_states, dtype=jnp.int32)[None, :]).astype(
        jnp.float32
    )
    nation_hot = (state_nation[:, None] == jnp.arange(n_nations, dtype=jnp.int32)[None, :]).astype(
        jnp.float32
    )
    upper_coef = state_coef + jnp.dot(nation_hot, nation_coef, precision=high)
    coef_table = (
        county_coef + jnp.dot(state_hot, upper_coef, precision=high) + beta[None, :]
    ).astype(jnp.bfloat16)
    prec_equal = precinct[:, None] == jnp.arange(prec_here, dtype=jnp.int32)[None, :]
    prec_hot = prec_equal.astype(jnp.bfloat16)
    map_hot = (precinct_county[:, None] == jnp.arange(cnt_here, dtype=jnp.int32)[None, :]).astype(
        jnp.bfloat16
    )
    county_hot = jnp.dot(prec_hot, map_hot, preferred_element_type=jnp.float32).astype(jnp.bfloat16)
    scores = lax.dot_general(
        features, coef_table, (((1,), (1,)), ((), ())), preferred_element_type=jnp.float32
    )
    intercept = jnp.sum(jnp.where(prec_equal, precinct_coef[None, :], jnp.float32(0.0)), axis=1)
    linear = jnp.sum(scores * county_hot.astype(jnp.float32), axis=1) + intercept
    live_rows = jnp.arange(rows_here, dtype=jnp.int32) < row_counts[0, 0]
    residual = jnp.where(live_rows, outcome.astype(jnp.float32) - jnp.exp(linear), jnp.float32(0.0))
    residual_b = residual.astype(jnp.bfloat16)
    weighted = county_hot * residual_b[:, None]
    county_local = lax.dot_general(
        weighted, features, (((0,), (0,)), ((), ())), preferred_element_type=jnp.float32
    )
    prec_local = jnp.sum(jnp.where(prec_equal, residual[:, None], jnp.float32(0.0)), axis=0)
    county_sum, prec_sum = lax.psum((county_local, prec_local), "row")
    county_share = lax.dynamic_slice_in_dim(county_sum, row_index * share_rows, share_rows, 0)
    hot_share = lax.dynamic_slice_in_dim(state_hot, row_index * share_rows, share_rows, 0)
    state_part = lax.dot_general(hot_share, county_share, (((0,), (0,)), ((), ())), precision=high)
    state_total = lax.psum(state_part, ("grp", "row"))
    nation_total = lax.dot_general(
        nation_hot, state_total, (((0,), (0,)), ((), ())), precision=high
    )
    beta_total = jnp.sum(nation_total, axis=0)
    own_coef = lax.dynamic_slice_in_dim(county_coef, row_index * share_rows, share_rows, 0)
    return (
        county_share - own_coef,
        prec_sum - precinct_coef,
        state_total - state_coef,
        nation_total - nation_coef,
        beta_total - beta,
    )


def solution(mesh):
    placed = (
        P(("grp", "row"), None),
        P(("grp", "row")),
        P(("grp", "row")),
        P("grp", "row"),
        P(),
        P(),
        P(),
        P("grp", None),
        P("grp"),
        P("grp"),
        P(),
        P(),
    )
    return jax.shard_map(
        on_device,
        mesh=mesh,
        in_specs=placed,
        out_specs=(P(("grp", "row"), None), P("grp"), P(), P(), P()),
        check_vma=False,
    )
```

profile of v0, /device:TPU:0, one launch (start us, length us, event | category | flops | bytes accessed | tf_op | source)
XLA Modules:
  0.0 212.0 jit_solution(17141826107697574952)
XLA Ops:
  7.2 0.0 all-reduce.3.cloned.1.call-start
  7.2 0.9 iota_compare_fusion.18
  8.1 0.0 copy-start.5
  8.1 0.0 copy-start.7
  8.1 0.0 copy-start.1
  8.2 0.0 copy-start.2
  8.2 0.0 copy-start.4
  8.2 9.9 %fusion.3 = bf16[8192,256]{0,1:T(8,128)(2,1)} fusion(s32[8192]{0:T(1024)} %param.13, pred[1024,256]{1,0:T(32,128)(4,1)S(1)} %iota_compare_fusion.18), kind=kOutput, calls=%fused_computation.7 | convolution fusion | flops 4305453056 | bytes 4489216 | tf_op jit(solution)/shard_map/dot_general | solution.py:47
  18.1 5.3 %select_reduce_fusion.1 = f32[8192]{0:T(1024)S(1)} fusion(f32[1024]{0:T(1024)S(1)} %copy-done.5, s32[8192]{0:T(1024)S(1)} %copy-done.7), kind=kLoop, calls=%fused_computation.1 | loop fusion | flops 25157632 | bytes 69632 | tf_op jit(solution)/shard_map/reduce_sum | solution.py:51
  24.1 0.8 dynamic_slice.12
  24.8 0.2 convolution_add_fusion.1
  25.1 0.0 copy-start.3
  25.1 0.0 slice-start
  25.1 0.4 fusion.9
  25.6 0.0 slice-start.1
  25.6 7.5 %fusion.6 = f32[8192]{0:T(1024)S(1)} fusion(bf16[8192,256]{0,1:T(8,128)(2,1)} %fusion.3, bf16[256,512]{1,0:T(8,128)(2,1)S(1)} %fusion.9, bf16[8192,512]{1,0:T(8,128)(2,1)} %param.12), kind=kOutput, calls=%fused_computation.10 | convolution fusion | flops 2153766912 | bytes 12877824 | tf_op jit(solution)/shard_map/dot_general | solution.py:48
  33.1 0.4 slice-done.1
  33.5 3.1 %fusion.4 = f32[256,512]{1,0:T(8,128)} fusion(bf16[8192,512]{1,0:T(8,128)(2,1)S(1)} %bitcast.16, bf16[8192,256]{0,1:T(8,128)(2,1)S(1)} %copy-done.8, bf16[8192]{0:T(1024)(128)(2,1)S(1)} %get-tuple-element.5), kind=kOutput, calls=%fused_computation.8 | convolution fusion | flops 2149580800 | bytes 13123584 | tf_op jit(solution)/shard_map/dot_general | solution.py:57
  36.6 0.0 all-reduce.3.cloned.1.call-update
  36.6 0.0 all-reduce.5.cloned.1.call-start
  36.7 4.5 %select_reduce_fusion = f32[1024]{0:T(1024)S(1)} fusion(f32[8192]{0:T(1024)S(1)} %get-tuple-element.6, s32[8192]{0:T(1024)S(1)} %copy-done.7), kind=kLoop, calls=%fused_computation | loop fusion | flops 25164800 | bytes 69632 | tf_op jit(solution)/shard_map/reduce_sum | solution.py:60
  41.2 8.5 %psum.22 = f32[1024]{0:T(1024)S(1)} all-reduce(f32[1024]{0:T(1024)S(1)} %select_reduce_fusion), channel_id=1, replica_groups=mesh['grp'=8,'row'=4] {'row'}, use_global_device_ids=true, to_apply=%region_4.5 | all-reduce | flops 1024 | bytes 8192 | tf_op jit(solution)/shard_map/psum | solution.py:61
  49.7 0.6 sub.20
  50.3 0.1 iota_compare_fusion.6
  50.4 22.3 %all-reduce.3.cloned.1.call-done = f32[256,512]{1,0:T(8,128)} async-done(((f32[256,512]{1,0:T(8,128)}), f32[256,512]{1,0:T(8,128)}) %all-reduce.3.cloned.1.call-update) | async-done | bytes 524304 | tf_op jit(solution)/shard_map/psum | solution.py:61
  72.6 1.8 fusion.11
  74.5 0.0 all-reduce.5.cloned.1.call-update
  74.5 1.6 dynamic-slice_subtract_fusion
  76.1 125.1 %all-reduce.5.cloned.1.call-done = f32[64,512]{1,0:T(8,128)} async-done(((f32[64,512]{1,0:T(8,128)}), f32[64,512]{1,0:T(8,128)}) %all-reduce.5.cloned.1.call-update) | async-done | bytes 131088 | tf_op jit(solution)/shard_map/psum | solution.py:65
  201.2 1.8 fusion.19
  203.0 0.6 sub.23
  203.5 1.6 sub.21
  (15 shorter events, 0.0 us)
Async XLA Ops:
  7.2 65.5 %all-reduce.3.cloned.1.call-start = ((), (), s32[]{:S(2)}) async-start(), calls=%async_computation | async-start | bytes 1048576 | tf_op jit(solution)/shard_map/psum | solution.py:61
  8.1 10.0 %copy-start.5 = (f32[1024]{0:T(1024)S(1)}, f32[1024]{0:T(1024)}, u32[]{:S(2)}) copy-start(f32[1024]{0:T(1024)} %param.20) | copy-start | bytes 12292
  8.1 10.0 %copy-start.7 = (s32[8192]{0:T(1024)S(1)}, s32[8192]{0:T(1024)}, u32[]{:S(2)}) copy-start(s32[8192]{0:T(1024)} %param.13) | copy-start | bytes 98308
  8.1 16.7 %copy-start.1 = (f32[64,512]{1,0:T(8,128)S(1)}, f32[64,512]{1,0:T(8,128)}, u32[]{:S(2)}) copy-start(f32[64,512]{1,0:T(8,128)} %param.18) | copy-start | bytes 393220
  8.2 16.7 %copy-start.2 = (f32[4,512]{1,0:T(4,128)S(1)}, f32[4,512]{1,0:T(4,128)}, u32[]{:S(2)}) copy-start(f32[4,512]{1,0:T(4,128)} %param.17) | copy-start | bytes 24580
  8.2 16.7 %copy-start.6 = (s32[64]{0:T(128)S(1)}, s32[64]{0:T(128)}, u32[]{:S(2)}) copy-start(s32[64]{0:T(128)} %param.23) | copy-start | bytes 772
  8.2 16.9 %copy-start = (f32[256,512]{1,0:T(8,128)S(1)}, f32[256,512]{1,0:T(8,128)}, u32[]{:S(2)}) copy-start(f32[256,512]{1,0:T(8,128)} %param.19) | copy-start | bytes 1572868
  8.2 16.9 %copy-start.4 = (f32[512]{0:T(512)S(1)}, f32[512]{0:T(512)}, u32[]{:S(2)}) copy-start(f32[512]{0:T(512)} %param.16) | copy-start | bytes 6148
  25.1 8.0 %copy-start.3 = (s32[8192]{0:T(1024)S(1)}, s32[8192]{0:T(1024)}, u32[]{:S(2)}) copy-start(s32[8192]{0:T(1024)} %param.14) | copy-start | bytes 98308
  25.1 8.0 %slice-start = ((s8[8388608]{0:T(1024)(128)(4,1)}), s8[4194304]{0:T(1024)(128)(4,1)S(1)}, s32[]{:S(2)}) async-start(s8[8388608]{0:T(1024)(128)(4,1)} %bitcast.15), calls=%async_computation.2 | async-start | bytes 8388608
  25.1 8.0 %copy-start.8 = (bf16[8192,256]{0,1:T(8,128)(2,1)S(1)}, bf16[8192,256]{0,1:T(8,128)(2,1)}, u32[]{:S(2)}) copy-start(bf16[8192,256]{0,1:T(8,128)(2,1)} %fusion.3) | copy-start | bytes 12582916
  25.6 7.9 %slice-start.1 = ((s8[8388608]{0:T(1024)(128)(4,1)}), s8[4194304]{0:T(1024)(128)(4,1)S(1)}, s32[]{:S(2)}) async-start(s8[8388608]{0:T(1024)(128)(4,1)} %bitcast.15), calls=%async_computation.3 | async-start | bytes 8388608
  36.6 164.5 %all-reduce.5.cloned.1.call-start = ((), (), s32[]{:S(2)}) async-start(), calls=%async_computation.1 | async-start | bytes 262144 | tf_op jit(solution)/shard_map/psum | solution.py:65
Sparse Core Ops, SparseCore 0:
  36.8 35.8 all-reduce.2
  78.7 122.3 all-reduce.4
where the time goes:
time: 212 us
  waiting for transfers between devices  147 us (69%)
  matrix products  24.8 us (12%)
  other arithmetic  15.1 us (7%)
  between operations  14.9 us (7%)
  blocking collectives  8.5 us (4%)
    psum x1, waiting for transfers between devices, on_device(): state_total = lax.psum(state_part, ('grp', 'row'))  125 us
    psum x1, waiting for transfers between devices, on_device(): county_sum, prec_sum = lax.psum((county_local, prec_local), 'row')  22.3 us
    dot_general x1, matrix products, on_device(): jnp.dot(prec_hot, map_hot, preferred_element_type=jnp.float32)  9.92 us
    psum x1, blocking collectives, on_device(): county_sum, prec_sum = lax.psum((county_local, prec_local), 'row')  8.5 us
    dot_general x1, matrix products, on_device(): lax.dot_general(features, coef_table, (((1,), (1,)), ((), ())), preferred...  7.48 us
    reduce_sum x1, other arithmetic, on_device(): jnp.sum(jnp.where(prec_equal, precinct_coef[None, :], jnp.float32(0.0)),...  5.27 us
    reduce_sum x1, other arithmetic, on_device(): jnp.sum(jnp.where(prec_equal, residual[:, None], jnp.float32(0.0)), axis=0)  4.46 us
  transfers between devices with their start and end apart: 2, of which 2 were waited for; matrix products, arithmetic and copies ran while one was open for 3% of the time, Pallas kernels for 0%

commit v1 on v0

v1 whole, which is shorter than its diff:
```python
import functools

import jax
import jax.numpy as jnp
from jax import lax
from jax.experimental import pallas as pl
from jax.experimental.pallas import tpu as pltpu
from jax.sharding import PartitionSpec as P

LANES = 128
ROW_STEP = 1024
ROW_CHUNK = 512
F32 = jnp.float32
BF16 = jnp.bfloat16


def split3(x):
    a = x.astype(BF16)
    r = x - a.astype(F32)
    b = r.astype(BF16)
    c = (r - b.astype(F32)).astype(BF16)
    return a, b, c


def hot_dot(hot, x, dims):
    out = None
    for part in reversed(split3(x)):
        term = lax.dot_general(hot, part, (dims, ((), ())), preferred_element_type=F32)
        out = term if out is None else out + term
    return out


def iota_rows(n):
    return lax.broadcasted_iota(jnp.int32, (n, 1), 0)


def main_kernel(
    count_ref,
    features_ref,
    precinct_ref,
    outcome_ref,
    beta_ref,
    nation_ref,
    state_ref,
    county_ref,
    prec_ref,
    map_ref,
    county_state_ref,
    state_nation_ref,
    county_out,
    state_out,
    table,
    lookup,
    county_acc,
    prec_acc,
):
    step = pl.program_id(0)
    steps = pl.num_programs(0)
    n_states = state_ref.shape[0]
    n_nations = nation_ref.shape[0]
    n_cnt, p_size = county_ref.shape
    n_hi = prec_ref.shape[0]
    group = lax.axis_index("grp")
    states = county_state_ref[group]
    state_hot = (iota_rows(n_states) == states).astype(F32).astype(BF16)

    @pl.when(step == 0)
    def _():
        nation_hot = (iota_rows(n_nations) == state_nation_ref[...]).astype(F32).astype(BF16)
        upper = state_ref[...] + hot_dot(nation_hot, nation_ref[...], ((0,), (0,)))
        table[...] = (
            county_ref[...] + hot_dot(state_hot, upper, ((0,), (0,))) + beta_ref[...]
        ).astype(BF16)
        lookup[...] = jnp.concatenate(
            [x.astype(F32) for x in split3(prec_ref[...])] + [map_ref[...].astype(F32)], axis=0
        ).astype(BF16)
        county_acc[...] = jnp.zeros_like(county_acc)
        prec_acc[...] = jnp.zeros_like(prec_acc)

    chunk = ROW_CHUNK
    for at in range(0, ROW_STEP, chunk):
        feats = features_ref[at : at + chunk, :]
        prec = precinct_ref[0, :, at : at + chunk]
        count = outcome_ref[0, :, at : at + chunk].astype(F32)
        low = jnp.bitwise_and(prec, LANES - 1)
        high = jnp.right_shift(prec, 7)
        low_hot = (iota_rows(LANES) == low).astype(F32).astype(BF16)
        high_hot = iota_rows(n_hi) == high
        found = jnp.dot(lookup[...], low_hot, preferred_element_type=F32)
        coef = found[:n_hi] + found[n_hi : 2 * n_hi] + found[2 * n_hi : 3 * n_hi]
        intercept = jnp.sum(jnp.where(high_hot, coef, 0.0), axis=0, keepdims=True)
        county = jnp.sum(
            jnp.where(high_hot, found[3 * n_hi :], 0.0), axis=0, keepdims=True
        ).astype(jnp.int32)
        county_hot = iota_rows(n_cnt) == county
        scores = lax.dot_general(
            table[...], feats, (((1,), (1,)), ((), ())), preferred_element_type=F32
        )
        linear = jnp.sum(jnp.where(county_hot, scores, 0.0), axis=0, keepdims=True) + intercept
        row = step * ROW_STEP + at + lax.broadcasted_iota(jnp.int32, (1, chunk), 1)
        residual = jnp.where(row < count_ref[0, 0], count - jnp.exp(linear), 0.0)
        rounded = residual.astype(BF16).astype(F32)
        weighted = jnp.where(county_hot, rounded, 0.0).astype(BF16)
        county_acc[...] += jnp.dot(weighted, feats, preferred_element_type=F32)
        by_high = jnp.concatenate(
            [jnp.where(high_hot, x.astype(F32), 0.0) for x in split3(residual)], axis=0
        ).astype(BF16)
        prec_acc[...] += lax.dot_general(
            by_high, low_hot, (((1,), (1,)), ((), ())), preferred_element_type=F32
        )

    @pl.when(step == steps - 1)
    def _():
        n_row, padded, _ = county_out.shape
        share = n_cnt // n_row
        total = county_acc[...]
        prec_sum = prec_acc[:n_hi] + prec_acc[n_hi : 2 * n_hi] + prec_acc[2 * n_hi :]
        for r in range(n_row):
            county_out[r, :share, :] = total[r * share : (r + 1) * share, :]
            county_out[r, share:, :LANES] = prec_sum
            county_out[r, share:, LANES:] = jnp.zeros((padded - share, p_size - LANES), F32)
        state_sum = hot_dot(state_hot, total, ((1,), (0,)))
        pieces, per, _ = state_out.shape
        blocks = p_size // LANES
        for k in range(pieces):
            top = k // blocks * per
            left = k % blocks * LANES
            state_out[k] = state_sum[top : top + per, left : left + LANES]


def end_kernel(
    state_nation_ref, gathered_ref, state_ref, nation_ref, beta_ref, state_out, nation_out, beta_out, total
):
    pieces, per, _ = gathered_ref.shape
    blocks = total.shape[1] // LANES
    for k in range(pieces):
        top = k // blocks * per
        left = k % blocks * LANES
        total[top : top + per, left : left + LANES] = gathered_ref[k]
    n_nations = nation_ref.shape[0]
    nation_hot = (iota_rows(n_nations) == state_nation_ref[...]).astype(F32).astype(BF16)
    sums = total[...]
    nation_total = hot_dot(nation_hot, sums, ((1,), (0,)))
    state_out[...] = sums - state_ref[...]
    nation_out[...] = nation_total - nation_ref[...]
    beta_out[...] = jnp.sum(nation_total, axis=0, keepdims=True) - beta_ref[...]


def whole(shape):
    return pl.BlockSpec(shape, lambda i: (0,) * len(shape))


def on_device(
    features,
    precinct,
    outcome,
    row_counts,
    beta,
    nation_coef,
    state_coef,
    county_coef,
    precinct_coef,
    precinct_county,
    county_state,
    state_nation,
):
    rows_here, p_size = features.shape
    cnt_here = county_coef.shape[0]
    prec_here = precinct_coef.shape[0]
    n_states = state_coef.shape[0]
    n_row = lax.axis_size("row")
    n_grp = lax.axis_size("grp")
    row_index = lax.axis_index("row")
    share = cnt_here // n_row
    n_hi = prec_here // LANES
    steps = rows_here // ROW_STEP
    pieces = n_row * n_grp
    per = n_states * p_size // LANES // pieces
    nations = nation_coef.shape[0]

    precinct3 = precinct.reshape(steps, 1, ROW_STEP)
    outcome3 = outcome.reshape(steps, 1, ROW_STEP)
    states3 = county_state.reshape(n_grp, 1, cnt_here)
    prec2 = precinct_coef.reshape(n_hi, LANES)
    map2 = precinct_county.reshape(n_hi, LANES)
    beta2 = beta.reshape(1, p_size)
    nation_row = state_nation.reshape(1, n_states)

    county_pack, state_pack = pl.pallas_call(
        main_kernel,
        grid=(steps,),
        in_specs=[
            pl.BlockSpec(memory_space=pltpu.SMEM),
            pl.BlockSpec((ROW_STEP, p_size), lambda i: (i, 0)),
            pl.BlockSpec((1, 1, ROW_STEP), lambda i: (i, 0, 0)),
            pl.BlockSpec((1, 1, ROW_STEP), lambda i: (i, 0, 0)),
            whole(beta2.shape),
            whole(nation_coef.shape),
            whole(state_coef.shape),
            whole(county_coef.shape),
            whole(prec2.shape),
            whole(map2.shape),
            whole(states3.shape),
            whole(nation_row.shape),
        ],
        out_specs=[whole((n_row, share + n_hi, p_size)), whole((pieces, per, LANES))],
        out_shape=[
            jax.ShapeDtypeStruct((n_row, share + n_hi, p_size), F32),
            jax.ShapeDtypeStruct((pieces, per, LANES), F32),
        ],
        scratch_shapes=[
            pltpu.VMEM((cnt_here, p_size), BF16),
            pltpu.VMEM((4 * n_hi, LANES), BF16),
            pltpu.VMEM((cnt_here, p_size), F32),
            pltpu.VMEM((3 * n_hi, LANES), F32),
        ],
        compiler_params=pltpu.CompilerParams(vmem_limit_bytes=32 * 1024 * 1024),
        name="local_sums",
    )(
        row_counts,
        features,
        precinct3,
        outcome3,
        beta2,
        nation_coef,
        state_coef,
        county_coef,
        prec2,
        map2,
        states3,
        nation_row,
    )

    state_parts = lax.all_to_all(state_pack, ("grp", "row"), 0, 0, tiled=True)
    county_parts = lax.all_to_all(county_pack, "row", 0, 0, tiled=True)
    state_piece = jnp.sum(state_parts, axis=0, keepdims=True)
    gathered = lax.all_gather(state_piece, ("grp", "row"), axis=0, tiled=True)
    county_sum = jnp.sum(county_parts, axis=0)
    own_coef = lax.dynamic_slice_in_dim(county_coef, row_index * share, share, 0)
    county_grad = county_sum[:share] - own_coef
    precinct_grad = county_sum[share:, :LANES].reshape(prec_here) - precinct_coef

    state_grad, nation_grad, beta_grad = pl.pallas_call(
        end_kernel,
        out_shape=[
            jax.ShapeDtypeStruct(state_coef.shape, F32),
            jax.ShapeDtypeStruct(nation_coef.shape, F32),
            jax.ShapeDtypeStruct((1, p_size), F32),
        ],
        scratch_shapes=[pltpu.VMEM(state_coef.shape, F32)],
        name="upper_totals",
    )(nation_row, gathered, state_coef, nation_coef, beta2)
    return county_grad, precinct_grad, state_grad, nation_grad, beta_grad.reshape(p_size)


def solution(mesh):
    placed = (
        P(("grp", "row"), None),
        P(("grp", "row")),
        P(("grp", "row")),
        P("grp", "row"),
        P(),
        P(),
        P(),
        P("grp", None),
        P("grp"),
        P("grp"),
        P(),
        P(),
    )
    return jax.shard_map(
        on_device,
        mesh=mesh,
        in_specs=placed,
        out_specs=(P(("grp", "row"), None), P("grp"), P(), P(), P()),
        check_vma=False,
    )
```

time: 212 us -> 90.3 us (0.43)
  waiting for transfers between devices: 147 us -> 0.01 us
  blocking collectives: 8.5 us -> 57.6 us
  matrix products: 24.8 us -> 0 us
  Pallas kernels: 0 us -> 13.9 us
  between operations: 14.9 us -> 1.35 us
  other arithmetic: 15.1 us -> 2.26 us
  local copies, waits for them, and re-layouts: 1.19 us -> 10.9 us
  starting transfers between devices: 0.08 us -> 3.48 us
    psum x2 -> x0, waiting for transfers between devices: 147 us -> none  [the longest x1 125 us: on_device(): state_total = lax.psum(state_part, ('grp', 'row'))]
    all_gather x0 -> x1, blocking collectives: none -> 42.3 us  [on_device(): gathered = lax.all_gather(state_piece, ('grp', 'row'), axis=0, tiled=True)]
    dot_general x7 -> x0, matrix products: 24.8 us -> none  [the longest x1 9.92 us: on_device(): jnp.dot(prec_hot, map_hot, preferred_element_type=jnp.float32)]
    all_to_all x0 -> x1, blocking collectives: none -> 15.3 us  [on_device(): state_parts = lax.all_to_all(state_pack, ('grp', 'row'), 0, 0, tiled=True)]
    pallas_call x0 -> x2, Pallas kernels: none -> 13.9 us  [the longest x1 12.2 us: on_device(): pl.pallas_call(main_kernel, grid=(steps,), in_specs=[pl.BlockSpec(memory_...]
    unnamed x22 -> x24, local copies, waits for them, and re-layouts: 0.42 us -> 10.9 us
    reduce_sum x2, other arithmetic: 9.72 us -> 0.08 us  [the longest x1 0.04 us: on_device(): county_sum = jnp.sum(county_parts, axis=0)]
    psum x1 -> x0, blocking collectives: 8.5 us -> none  [on_device(): county_sum, prec_sum = lax.psum((county_local, prec_local), 'row')]
  transfers between devices with their start and end apart: 2 -> 1, of which waited for: 2 -> 0; matrix products, arithmetic and copies ran while one was open for 3% -> 0% of each run, Pallas kernels for 0% -> 2%
where the time goes in v1:
time: 90.3 us; the launch traced here: 89.6 us
  blocking collectives  57.6 us (64%)
  Pallas kernels  13.9 us (15%)
  local copies, waits for them, and re-layouts  10.9 us (12%)
  starting transfers between devices  3.48 us (4%)
  other arithmetic  2.26 us (3%)
  between operations  1.35 us (1%)
    all_gather x1, blocking collectives, on_device(): gathered = lax.all_gather(state_piece, ('grp', 'row'), axis=0, tiled=True)  42.3 us
    all_to_all x1, blocking collectives, on_device(): state_parts = lax.all_to_all(state_pack, ('grp', 'row'), 0, 0, tiled=True)  15.3 us
    pallas_call x1, Pallas kernels, on_device(): pl.pallas_call(main_kernel, grid=(steps,), in_specs=[pl.BlockSpec(memory_...  12.2 us
    unnamed x24, local copies, waits for them, and re-layouts  10.9 us
    all_to_all x1, starting transfers between devices, on_device(): county_parts = lax.all_to_all(county_pack, 'row', 0, 0, tiled=True)  3.48 us
  transfers between devices with their start and end apart: 1, of which 0 were waited for; matrix products, arithmetic and copies ran while one was open for 0% of the time, Pallas kernels for 2%

profile of v1, /device:TPU:0, one launch (start us, length us, event | category | flops | bytes accessed | tf_op | source)
XLA Modules:
  0.0 89.6 jit_solution(1761508688700453430)
XLA Ops:
  0.6 0.0 copy-start.7
  1.3 0.0 copy-start
  1.3 3.4 %copy-done = bf16[8192,512]{1,0:T(8,128)(2,1)S(1)} copy-done((bf16[8192,512]{1,0:T(8,128)(2,1)S(1)}, bf16[8192,512]{1,0:T(8,128)(2,1)}, u32[]{:S(2)}) %copy-start) | copy-done | bytes 8388632
  4.7 0.0 copy-start.1
  4.7 1.0 %copy-done.1 = f32[256,512]{1,0:T(8,128)S(1)} copy-done((f32[256,512]{1,0:T(8,128)S(1)}, f32[256,512]{1,0:T(8,128)}, u32[]{:S(2)}) %copy-start.1) | copy-done | bytes 524312
  5.7 0.0 copy-start.2
  5.7 0.9 %copy-done.2 = f32[64,512]{1,0:T(8,128)S(1)} copy-done((f32[64,512]{1,0:T(8,128)S(1)}, f32[64,512]{1,0:T(8,128)}, u32[]{:S(2)}) %copy-start.2) | copy-done | bytes 131096
  6.6 0.0 copy-start.3
  6.6 0.8 copy-done.3
  7.4 0.0 copy-start.4
  7.4 0.8 copy-done.4
  8.1 0.0 copy-start.5
  8.2 0.7 copy-done.5
  8.8 0.0 copy-start.6
  8.8 0.7 copy-done.6
  9.5 0.0 copy-start.8
  9.5 0.7 copy-done.8
  10.2 0.0 copy-start.9
  10.2 0.7 copy-done.9
  10.9 0.0 copy-start.10
  10.9 0.7 copy-done.10
  11.6 0.0 copy-start.11
  11.6 0.7 copy-done.11
  12.3 12.2 %local_sums.1 = (f32[4,72,512]{2,1,0:T(8,128)}, f32[32,8,128]{2,1,0:T(8,128)S(1)}) custom-call(s32[1,1]{1,0:T(1,128)S(6)} %copy.17.count_ref, bf16[8192,512]{1,0:T(8,128)(2,1)S(1)} %copy-done, s32[8,1,1024]{2,1,0:T(1,128)S(1)} %bitcast.13, s32[8,1,1024]{2,1,0:T(1,128)S(1)} %bitcast.14, f32[1,512]{1,0:T(1,128)S(1)} %bitcast.18, f32[4,512]{1,0:T(4,128)S(1)} %copy-done.5, ...), custom_call_target="tpu_custom_call" | custom-call | tf_op jit(solution)/shard_map/local_sums/pallas_call | solution.py:189
  24.4 15.3 %all_to_all.10 = f32[32,8,128]{2,1,0:T(8,128)S(1)} all-to-all(f32[32,8,128]{2,1,0:T(8,128)S(1)} %get-tuple-element.11), channel_id=1, replica_groups=mesh['grp'=8,'row'=4] {'grp','row'}, dimensions={0} | all-to-all | bytes 262144 | tf_op jit(solution)/shard_map/all_to_all | solution.py:234
  39.7 3.5 %all-to-all-start = ((f32[4,72,512]{2,1,0:T(8,128)}), f32[4,72,512]{2,1,0:T(8,128)S(1)}, u32[]{:S(2)}, u32[]{:S(2)}) async-start(f32[4,72,512]{2,1,0:T(8,128)} %get-tuple-element.10), calls=%async_computation | async-start | bytes 1179648 | tf_op jit(solution)/shard_map/all_to_all | solution.py:235
  43.3 42.3 %all-gather = f32[256,128]{1,0:T(8,128)} all-gather(f32[8,128]{1,0:T(8,128)S(1)} %reduce_sum.19), channel_id=2, replica_groups=mesh['grp'=8,'row'=4] {'grp','row'}, dimensions={0}, use_global_device_ids=true | all-gather | bytes 135168 | tf_op jit(solution)/shard_map/all_gather | solution.py:237
  85.6 1.8 %upper_totals.1 = (f32[64,512]{1,0:T(8,128)}, f32[4,512]{1,0:T(4,128)}, f32[1,512]{1,0:T(1,128)}) custom-call(s32[1,64]{1,0:T(1,128)} %bitcast.20, f32[32,8,128]{2,1,0:T(8,128)} %bitcast.22, f32[64,512]{1,0:T(8,128)} %state_ref.3, f32[4,512]{1,0:T(4,128)} %nation_ref.3, f32[1,512]{1,0:T(1,128)} %bitcast.17), custom_call_target="tpu_custom_call" | custom-call | tf_op jit(solution)/shard_map/upper_totals/pallas_call | solution.py:243
  87.4 0.0 all-to-all-done
  87.4 0.0 copy-done.7
  87.4 0.6 fusion
  88.0 1.6 %slice_subtract_fusion = f32[64,512]{1,0:T(8,128)} fusion(f32[72,512]{1,0:T(8,128)S(1)} %reduce_sum.18, f32[256,512]{1,0:T(8,128)} %county_ref.1, s32[]{:T(128)S(6)} %select_n.3), kind=kLoop, calls=%fused_computation | loop fusion | flops 32768 | bytes 393220 | tf_op jit(solution)/shard_map/sub | solution.py:240
  (2 shorter events, 0.1 us)
Async XLA Ops:
  0.6 86.8 %copy-start.7 = (f32[1024]{0:T(1024)S(1)}, f32[1024]{0:T(1024)}, u32[]{:S(2)}) copy-start(f32[1024]{0:T(1024)} %param.20) | copy-start | bytes 12292
  1.3 3.4 %copy-start = (bf16[8192,512]{1,0:T(8,128)(2,1)S(1)}, bf16[8192,512]{1,0:T(8,128)(2,1)}, u32[]{:S(2)}) copy-start(bf16[8192,512]{1,0:T(8,128)(2,1)} %features_ref.1) | copy-start | bytes 25165828
  4.7 1.0 %copy-start.1 = (f32[256,512]{1,0:T(8,128)S(1)}, f32[256,512]{1,0:T(8,128)}, u32[]{:S(2)}) copy-start(f32[256,512]{1,0:T(8,128)} %county_ref.1) | copy-start | bytes 1572868
  5.7 0.9 %copy-start.2 = (f32[64,512]{1,0:T(8,128)S(1)}, f32[64,512]{1,0:T(8,128)}, u32[]{:S(2)}) copy-start(f32[64,512]{1,0:T(8,128)} %state_ref.3) | copy-start | bytes 393220
  6.6 0.8 copy-start.3
  7.4 0.8 copy-start.4
  8.1 0.7 copy-start.5
  8.8 0.7 copy-start.6
  9.5 0.7 copy-start.8
  10.2 0.7 copy-start.9
  10.9 0.7 copy-start.10
  11.6 0.7 copy-start.11
  39.7 47.6 %all-to-all-start = ((f32[4,72,512]{2,1,0:T(8,128)}), f32[4,72,512]{2,1,0:T(8,128)S(1)}, u32[]{:S(2)}, u32[]{:S(2)}) async-start(f32[4,72,512]{2,1,0:T(8,128)} %get-tuple-element.10), calls=%async_computation | async-start | bytes 1179648 | tf_op jit(solution)/shard_map/all_to_all | solution.py:235

commit v2 on v1

--- a/solution.py
+++ b/solution.py
@@ -10,6 +10,7 @@
 LANES = 128
 ROW_STEP = 1024
 ROW_CHUNK = 512
+VMEM_LIMIT = 60 * 1024 * 1024
 F32 = jnp.float32
 BF16 = jnp.bfloat16
 
@@ -47,13 +48,11 @@
     map_ref,
     county_state_ref,
     state_nation_ref,
-    county_out,
-    state_out,
-    table,
-    lookup,
-    county_acc,
-    prec_acc,
+    *rest,
 ):
+    *outs, table, lookup, county_acc, prec_acc, state_acc = rest
+    n_row = len(outs) // 2
+    state_outs, county_outs = outs[:n_row], outs[n_row:]
     step = pl.program_id(0)
     steps = pl.num_programs(0)
     n_states = state_ref.shape[0]
@@ -111,32 +110,26 @@
 
     @pl.when(step == steps - 1)
     def _():
-        n_row, padded, _ = county_out.shape
+        me = lax.axis_index("row")
         share = n_cnt // n_row
-        total = county_acc[...]
+        per = n_states // n_row
         prec_sum = prec_acc[:n_hi] + prec_acc[n_hi : 2 * n_hi] + prec_acc[2 * n_hi :]
-        for r in range(n_row):
-            county_out[r, :share, :] = total[r * share : (r + 1) * share, :]
-            county_out[r, share:, :LANES] = prec_sum
-            county_out[r, share:, LANES:] = jnp.zeros((padded - share, p_size - LANES), F32)
-        state_sum = hot_dot(state_hot, total, ((1,), (0,)))
-        pieces, per, _ = state_out.shape
-        blocks = p_size // LANES
-        for k in range(pieces):
-            top = k // blocks * per
-            left = k % blocks * LANES
-            state_out[k] = state_sum[top : top + per, left : left + LANES]
-
-
-def end_kernel(
-    state_nation_ref, gathered_ref, state_ref, nation_ref, beta_ref, state_out, nation_out, beta_out, total
-):
-    pieces, per, _ = gathered_ref.shape
-    blocks = total.shape[1] // LANES
-    for k in range(pieces):
-        top = k // blocks * per
-        left = k % blocks * LANES
-        total[top : top + per, left : left + LANES] = gathered_ref[k]
+        state_acc[...] = hot_dot(state_hot, county_acc[...], ((1,), (0,)))
+        for d in range(n_row):
+            peer = jnp.bitwise_xor(me, d)
+            state_outs[d][...] = state_acc[pl.ds(pl.multiple_of(peer * per, per), per), :]
+            county_outs[d][:share, :] = county_acc[pl.ds(pl.multiple_of(peer * share, share), share), :]
+            county_outs[d][share:, :LANES] = prec_sum
+            county_outs[d][share:, LANES:] = jnp.zeros((n_hi, p_size - LANES), F32)
+
+
+def end_kernel(*refs):
+    state_nation_ref, *gathered, state_ref, nation_ref, beta_ref, state_out, nation_out, beta_out, total = refs
+    me = lax.axis_index("row")
+    per = gathered[0].shape[0]
+    for d, part in enumerate(gathered):
+        peer = jnp.bitwise_xor(me, d)
+        total[pl.ds(pl.multiple_of(peer * per, per), per), :] = part[...]
     n_nations = nation_ref.shape[0]
     nation_hot = (iota_rows(n_nations) == state_nation_ref[...]).astype(F32).astype(BF16)
     sums = total[...]
@@ -144,6 +137,21 @@
     state_out[...] = sums - state_ref[...]
     nation_out[...] = nation_total - nation_ref[...]
     beta_out[...] = jnp.sum(nation_total, axis=0, keepdims=True) - beta_ref[...]
+
+
+def swap(x, axis, d):
+    n = lax.axis_size(axis)
+    return lax.ppermute(x, axis, [(i, i ^ d) for i in range(n)])
+
+
+def gather_by(x, axis):
+    return [x] + [swap(x, axis, d) for d in range(1, lax.axis_size(axis))]
+
+
+def total_of(parts):
+    while len(parts) > 1:
+        parts = [sum(parts[i : i + 2][1:], parts[i]) for i in range(0, len(parts), 2)]
+    return parts[0]
 
 
 def whole(shape):
@@ -174,9 +182,7 @@
     share = cnt_here // n_row
     n_hi = prec_here // LANES
     steps = rows_here // ROW_STEP
-    pieces = n_row * n_grp
-    per = n_states * p_size // LANES // pieces
-    nations = nation_coef.shape[0]
+    per = n_states // n_row
 
     precinct3 = precinct.reshape(steps, 1, ROW_STEP)
     outcome3 = outcome.reshape(steps, 1, ROW_STEP)
@@ -186,7 +192,7 @@
     beta2 = beta.reshape(1, p_size)
     nation_row = state_nation.reshape(1, n_states)
 
-    county_pack, state_pack = pl.pallas_call(
+    outs = pl.pallas_call(
         main_kernel,
         grid=(steps,),
         in_specs=[
@@ -203,18 +209,17 @@
             whole(states3.shape),
             whole(nation_row.shape),
         ],
-        out_specs=[whole((n_row, share + n_hi, p_size)), whole((pieces, per, LANES))],
-        out_shape=[
-            jax.ShapeDtypeStruct((n_row, share + n_hi, p_size), F32),
-            jax.ShapeDtypeStruct((pieces, per, LANES), F32),
-        ],
+        out_specs=[whole((per, p_size))] * n_row + [whole((share + n_hi, p_size))] * n_row,
+        out_shape=[jax.ShapeDtypeStruct((per, p_size), F32)] * n_row
+        + [jax.ShapeDtypeStruct((share + n_hi, p_size), F32)] * n_row,
         scratch_shapes=[
             pltpu.VMEM((cnt_here, p_size), BF16),
             pltpu.VMEM((4 * n_hi, LANES), BF16),
             pltpu.VMEM((cnt_here, p_size), F32),
             pltpu.VMEM((3 * n_hi, LANES), F32),
+            pltpu.VMEM(state_coef.shape, F32),
         ],
-        compiler_params=pltpu.CompilerParams(vmem_limit_bytes=32 * 1024 * 1024),
+        compiler_params=pltpu.CompilerParams(vmem_limit_bytes=VMEM_LIMIT),
         name="local_sums",
     )(
         row_counts,
@@ -231,11 +236,12 @@
         nation_row,
     )
 
-    state_parts = lax.all_to_all(state_pack, ("grp", "row"), 0, 0, tiled=True)
-    county_parts = lax.all_to_all(county_pack, "row", 0, 0, tiled=True)
-    state_piece = jnp.sum(state_parts, axis=0, keepdims=True)
-    gathered = lax.all_gather(state_piece, ("grp", "row"), axis=0, tiled=True)
-    county_sum = jnp.sum(county_parts, axis=0)
+    state_parts = [outs[0]] + [swap(outs[d], "row", d) for d in range(1, n_row)]
+    state_piece = total_of(state_parts)
+    state_piece = total_of(gather_by(state_piece, "grp"))
+    gathered = gather_by(state_piece, "row")
+    county_parts = [outs[n_row]] + [swap(outs[n_row + d], "row", d) for d in range(1, n_row)]
+    county_sum = total_of(county_parts)
     own_coef = lax.dynamic_slice_in_dim(county_coef, row_index * share, share, 0)
     county_grad = county_sum[:share] - own_coef
     precinct_grad = county_sum[share:, :LANES].reshape(prec_here) - precinct_coef
@@ -249,7 +255,7 @@
         ],
         scratch_shapes=[pltpu.VMEM(state_coef.shape, F32)],
         name="upper_totals",
-    )(nation_row, gathered, state_coef, nation_coef, beta2)
+    )(nation_row, *gathered, state_coef, nation_coef, beta2)
     return county_grad, precinct_grad, state_grad, nation_grad, beta_grad.reshape(p_size)
 
 

time: 90.3 us -> 50.4 us (0.56)
  blocking collectives: 57.6 us -> 0 us
  starting transfers between devices: 3.48 us -> 18.7 us
  local copies, waits for them, and re-layouts: 10.9 us -> 1.21 us
  waiting for transfers between devices: 0.01 us -> 9.24 us
  Pallas kernels: 13.9 us -> 15.7 us
  other arithmetic: 2.26 us -> 3.92 us
    all_gather x1 -> x0, blocking collectives: 42.3 us -> none  [on_device(): gathered = lax.all_gather(state_piece, ('grp', 'row'), axis=0, tiled=True)]
    ppermute x0 -> x16, starting transfers between devices: none -> 18.7 us  [swap(): return lax.ppermute(x, axis, [(i, i ^ d) for i in range(n)])]
    all_to_all x1 -> x0, blocking collectives: 15.3 us -> none  [on_device(): state_parts = lax.all_to_all(state_pack, ('grp', 'row'), 0, 0, tiled=True)]
    unnamed x24 -> x10, local copies, waits for them, and re-layouts: 10.9 us -> 1.21 us
    ppermute x0 -> x16, waiting for transfers between devices: none -> 9.24 us  [swap(): return lax.ppermute(x, axis, [(i, i ^ d) for i in range(n)])]
    all_to_all x1 -> x0, starting transfers between devices: 3.48 us -> none  [on_device(): county_parts = lax.all_to_all(county_pack, 'row', 0, 0, tiled=True)]
    pallas_call x1, Pallas kernels: 12.2 us -> 13.9 us  [on_device(): pl.pallas_call(main_kernel, grid=(steps,), in_specs=[pl.BlockSpec(memory_...]
    add x0 -> x3, other arithmetic: none -> 1.75 us  [total_of(): parts = [sum(parts[i:i + 2][1:], parts[i]) for i in range(0, len(parts), 2)]]
  transfers between devices with their start and end apart: 1 -> 16, of which waited for: 0 -> 5; matrix products, arithmetic and copies ran while one was open for 0% -> 0% of each run, Pallas kernels for 2% -> 3%
where the time goes in v2:
time: 50.4 us; the launch traced here: 50.1 us
  starting transfers between devices  18.7 us (37%)
  Pallas kernels  15.7 us (31%)
  waiting for transfers between devices  9.24 us (18%)
  other arithmetic  3.92 us (8%)
  between operations  1.37 us (3%)
  local copies, waits for them, and re-layouts  1.21 us (2%)
    ppermute x16, starting transfers between devices, swap(): return lax.ppermute(x, axis, [(i, i ^ d) for i in range(n)])  18.7 us
    pallas_call x1, Pallas kernels, on_device(): pl.pallas_call(main_kernel, grid=(steps,), in_specs=[pl.BlockSpec(memory_...  13.9 us
    ppermute x16, waiting for transfers between devices, swap(): return lax.ppermute(x, axis, [(i, i ^ d) for i in range(n)])  9.24 us
    add x3, other arithmetic, total_of(): parts = [sum(parts[i:i + 2][1:], parts[i]) for i in range(0, len(parts), 2)]  1.75 us
    pallas_call x1, Pallas kernels, on_device(): pl.pallas_call(end_kernel, out_shape=[jax.ShapeDtypeStruct(state_coef.sha...  1.73 us
    sub x1, other arithmetic, on_device(): county_grad = county_sum[:share] - own_coef  1.58 us
    unnamed x10, local copies, waits for them, and re-layouts  1.21 us
  transfers between devices with their start and end apart: 16, of which 5 were waited for; matrix products, arithmetic and copies ran while one was open for 0% of the time, Pallas kernels for 3%

profile of v2, /device:TPU:0, one launch (start us, length us, event | category | flops | bytes accessed | tf_op | source)
XLA Modules:
  0.0 50.1 jit_solution(995533533572325311)
XLA Ops:
  1.3 13.9 %local_sums.1 = (f32[16,512]{1,0:T(8,128)}, f32[16,512]{1,0:T(8,128)}, f32[16,512]{1,0:T(8,128)}, f32[16,512]{1,0:T(8,128)}, f32[72,512]{1,0:T(8,128)}, /*index=...) custom-call(s32[1,1]{1,0:T(1,128)S(6)} %copy.17.count_ref, bf16[8192,512]{1,0:T(8,128)(2,1)} %features_ref.1, ...), custom_call_target="tpu_custom_call" | custom-call | tf_op jit(solution)/shard_map/local_sums/pallas_call | solution.py:195
  15.2 3.0 %collective-permute-start.4 = (f32[16,512]{1,0:T(8,128)}, f32[16,512]{1,0:T(8,128)S(1)}, u32[]{:S(2)}, u32[]{:S(2)}) collective-permute-start(f32[16,512]{1,0:T(8,128)} %get-tuple-element.22), channel_id=1, source_target_pairs={{0,2},{1,3},{2,0},{3,1},{4,6},{5,7},{6,4},{7,5},{8,10},{9,11},{10,... | collective-permute-start | bytes 98312 | tf_op jit(solution)/shard_map/ppermute | solution.py:144
  18.3 0.2 collective-permute-start.3
  18.4 1.9 %collective-permute-done.4 = f32[16,512]{1,0:T(8,128)S(1)} collective-permute-done((f32[16,512]{1,0:T(8,128)}, f32[16,512]{1,0:T(8,128)S(1)}, u32[]{:S(2)}, u32[]{:S(2)}) %collective-permute-start.4) | collective-permute-done | bytes 32800 | tf_op jit(solution)/shard_map/ppermute | solution.py:144
  20.4 1.5 %collective-permute-done.5 = f32[16,512]{1,0:T(8,128)S(1)} collective-permute-done((f32[16,512]{1,0:T(8,128)}, f32[16,512]{1,0:T(8,128)S(1)}, u32[]{:S(2)}, u32[]{:S(2)}) %collective-permute-start.5) | collective-permute-done | bytes 32800 | tf_op jit(solution)/shard_map/ppermute | solution.py:144
  21.9 0.8 %add_add_fusion.2 = f32[16,512]{1,0:T(8,128)S(1)} fusion(f32[16,512]{1,0:T(8,128)S(1)} %collective-permute-done.4, f32[16,512]{1,0:T(8,128)S(1)} %collective-permute-done.5, f32[16,512]{1,0:T(8,128)} %get-tuple-element.20, f32[16,512]{1,0:T(8,128)S(1)} %collective-permute-done.3), kind=kLoop, calls=%fused_computation.3 | loop fusion | flops 24576 | bytes 163840 | tf_op jit(solution)/shard_map/add | solution.py:153
  22.6 3.7 %collective-permute-start.11 = (f32[16,512]{1,0:T(8,128)S(1)}, f32[16,512]{1,0:T(8,128)S(1)}, u32[]{:S(2)}, u32[]{:S(2)}) collective-permute-start(f32[16,512]{1,0:T(8,128)S(1)} %add_add_fusion.2), channel_id=1, source_target_pairs={{0,24},{4,28},{8,16},{12,20},{16,8},{20,12},{24,0},{28,4},{1,25},{... | collective-permute-start | bytes 98312 | tf_op jit(solution)/shard_map/ppermute | solution.py:144
  26.3 1.2 %collective-permute-start.12 = (f32[16,512]{1,0:T(8,128)S(1)}, f32[16,512]{1,0:T(8,128)S(1)}, u32[]{:S(2)}, u32[]{:S(2)}) collective-permute-start(f32[16,512]{1,0:T(8,128)S(1)} %add_add_fusion.2), channel_id=1, source_target_pairs={{0,28},{4,24},{8,20},{12,16},{16,12},{20,8},{24,4},{28,0},{1,29},{... | collective-permute-start | bytes 98312 | tf_op jit(solution)/shard_map/ppermute | solution.py:144
  27.5 0.8 %collective-permute-start.9 = (f32[16,512]{1,0:T(8,128)S(1)}, f32[16,512]{1,0:T(8,128)S(1)}, u32[]{:S(2)}, u32[]{:S(2)}) collective-permute-start(f32[16,512]{1,0:T(8,128)S(1)} %add_add_fusion.2), channel_id=1, source_target_pairs={{0,16},{4,20},{8,24},{12,28},{16,0},{20,4},{24,8},{28,12},{1,17},{... | collective-permute-start | bytes 98312 | tf_op jit(solution)/shard_map/ppermute | solution.py:144
  28.3 2.1 %collective-permute-start.10 = (f32[16,512]{1,0:T(8,128)S(1)}, f32[16,512]{1,0:T(8,128)S(1)}, u32[]{:S(2)}, u32[]{:S(2)}) collective-permute-start(f32[16,512]{1,0:T(8,128)S(1)} %add_add_fusion.2), channel_id=1, source_target_pairs={{0,20},{4,16},{8,28},{12,24},{16,4},{20,0},{24,12},{28,8},{1,21},{... | collective-permute-start | bytes 98312 | tf_op jit(solution)/shard_map/ppermute | solution.py:144
  30.4 1.3 %collective-permute-start.7 = (f32[16,512]{1,0:T(8,128)S(1)}, f32[16,512]{1,0:T(8,128)S(1)}, u32[]{:S(2)}, u32[]{:S(2)}) collective-permute-start(f32[16,512]{1,0:T(8,128)S(1)} %add_add_fusion.2), channel_id=1, source_target_pairs={{0,8},{4,12},{8,0},{12,4},{16,24},{20,28},{24,16},{28,20},{1,9},{5... | collective-permute-start | bytes 98312 | tf_op jit(solution)/shard_map/ppermute | solution.py:144
  31.6 0.0 collective-permute-done.11
  31.6 1.7 %collective-permute-start.8 = (f32[16,512]{1,0:T(8,128)S(1)}, f32[16,512]{1,0:T(8,128)S(1)}, u32[]{:S(2)}, u32[]{:S(2)}) collective-permute-start(f32[16,512]{1,0:T(8,128)S(1)} %add_add_fusion.2), channel_id=1, source_target_pairs={{0,12},{4,8},{8,4},{12,0},{16,28},{20,24},{24,20},{28,16},{1,13},{... | collective-permute-start | bytes 98312 | tf_op jit(solution)/shard_map/ppermute | solution.py:144
  33.3 1.1 %collective-permute-start.6 = (f32[16,512]{1,0:T(8,128)S(1)}, f32[16,512]{1,0:T(8,128)S(1)}, u32[]{:S(2)}, u32[]{:S(2)}) collective-permute-start(f32[16,512]{1,0:T(8,128)S(1)} %add_add_fusion.2), channel_id=1, source_target_pairs={{0,4},{4,0},{8,12},{12,8},{16,20},{20,16},{24,28},{28,24},{1,5},{5... | collective-permute-start | bytes 98312 | tf_op jit(solution)/shard_map/ppermute | solution.py:144
  34.4 0.0 collective-permute-done.9
  34.5 0.8 %collective-permute-start.1 = (f32[72,512]{1,0:T(8,128)}, f32[72,512]{1,0:T(8,128)S(1)}, u32[]{:S(2)}, u32[]{:S(2)}) collective-permute-start(f32[72,512]{1,0:T(8,128)} %get-tuple-element.18), channel_id=1, source_target_pairs={{0,2},{1,3},{2,0},{3,1},{4,6},{5,7},{6,4},{7,5},{8,10},{9,11},{10,... | collective-permute-start | bytes 442376 | tf_op jit(solution)/shard_map/ppermute | solution.py:144
  35.3 0.0 collective-permute-done.10
  35.3 0.0 collective-permute-start.2
  35.3 1.3 %collective-permute-start = (f32[72,512]{1,0:T(8,128)}, f32[72,512]{1,0:T(8,128)S(1)}, u32[]{:S(2)}, u32[]{:S(2)}) collective-permute-start(f32[72,512]{1,0:T(8,128)} %get-tuple-element.17), channel_id=1, source_target_pairs={{0,1},{1,0},{2,3},{3,2},{4,5},{5,4},{6,7},{7,6},{8,9},{9,8},{10,11... | collective-permute-start | bytes 442376 | tf_op jit(solution)/shard_map/ppermute | solution.py:144
  36.6 0.6 %collective-permute-done.6 = f32[16,512]{1,0:T(8,128)S(1)} collective-permute-done((f32[16,512]{1,0:T(8,128)S(1)}, f32[16,512]{1,0:T(8,128)S(1)}, u32[]{:S(2)}, u32[]{:S(2)}) %collective-permute-start.6) | collective-permute-done | bytes 32800 | tf_op jit(solution)/shard_map/ppermute | solution.py:144
  37.3 0.0 copy-start
  37.3 0.1 collective-permute-start.13
  37.4 0.8 %collective-permute-start.14 = (f32[16,512]{1,0:T(8,128)S(1)}, f32[16,512]{1,0:T(8,128)S(1)}, u32[]{:S(2)}, u32[]{:S(2)}) collective-permute-start(f32[16,512]{1,0:T(8,128)S(1)} %add_add_fusion.1.refs_1_), channel_id=1, source_target_pairs={{0,2},{1,3},{2,0},{3,1},{4,6},{5,7},{6,4},{7,5},{8,10},{9,11},{10,... | collective-permute-start | bytes 98312 | tf_op jit(solution)/shard_map/ppermute | solution.py:144
  38.2 0.4 collective-permute-done.13.refs_2_
  38.6 0.7 %collective-permute-start.15 = (f32[16,512]{1,0:T(8,128)S(1)}, f32[16,512]{1,0:T(8,128)S(1)}, u32[]{:S(2)}, u32[]{:S(2)}) collective-permute-start(f32[16,512]{1,0:T(8,128)S(1)} %add_add_fusion.1.refs_1_), channel_id=1, source_target_pairs={{0,3},{1,2},{2,1},{3,0},{4,7},{5,6},{6,5},{7,4},{8,11},{9,10},{10,... | collective-permute-start | bytes 98312 | tf_op jit(solution)/shard_map/ppermute | solution.py:144
  39.2 4.8 %collective-permute-done.14.refs_3_ = f32[16,512]{1,0:T(8,128)S(1)} collective-permute-done((f32[16,512]{1,0:T(8,128)S(1)}, f32[16,512]{1,0:T(8,128)S(1)}, u32[]{:S(2)}, u32[]{:S(2)}) %collective-permute-start.14) | collective-permute-done | bytes 32800 | tf_op jit(solution)/shard_map/ppermute | solution.py:144
  44.0 0.6 %copy-done.2 = f32[16,512]{1,0:T(8,128)} copy-done((f32[16,512]{1,0:T(8,128)}, f32[16,512]{1,0:T(8,128)S(1)}, u32[]{:S(2)}) %copy-start.2) | copy-done | bytes 32792
  44.6 0.6 %copy-done.3 = f32[16,512]{1,0:T(8,128)} copy-done((f32[16,512]{1,0:T(8,128)}, f32[16,512]{1,0:T(8,128)S(1)}, u32[]{:S(2)}) %copy-start.3) | copy-done | bytes 32792
  45.2 1.7 %upper_totals.1 = (f32[64,512]{1,0:T(8,128)}, f32[4,512]{1,0:T(4,128)}, f32[1,512]{1,0:T(1,128)}) custom-call(s32[1,64]{1,0:T(1,128)} %bitcast.20, f32[16,512]{1,0:T(8,128)} %copy-done, f32[16,512]{1,0:T(8,128)} %copy-done.1, f32[16,512]{1,0:T(8,128)} %copy-done.2, f32[16,512]{1,0:T(8,128)} %copy-done.3, f32[64,512]{1,0:T(8,128)} %refs_5_.1, ...), custom_call_target="tpu_custom_call" | custom-call | tf_op jit(solution)/shard_map/upper_totals/pallas_call | solution.py:249
  47.0 1.0 %add_add_fusion = f32[72,512]{1,0:T(8,128)S(1)} fusion(f32[72,512]{1,0:T(8,128)S(1)} %collective-permute-done.1, f32[72,512]{1,0:T(8,128)S(1)} %collective-permute-done.2, f32[72,512]{1,0:T(8,128)} %get-tuple-element.16, f32[72,512]{1,0:T(8,128)S(1)} %collective-permute-done), kind=kLoop, calls=%fused_computation | loop fusion | flops 110592 | bytes 737280 | tf_op jit(solution)/shard_map/add | solution.py:153
  48.0 0.6 %fusion = f32[1024]{0:T(1024)} fusion(f32[1024]{0:T(1024)S(1)} %copy-done.4, f32[72,512]{1,0:T(8,128)S(1)} %add_add_fusion), kind=kLoop, calls=%fused_computation.5 | loop fusion | flops 1024 | bytes 12288 | tf_op jit(solution)/shard_map/sub | solution.py:247
  48.5 1.6 %slice_subtract_fusion = f32[64,512]{1,0:T(8,128)} fusion(f32[72,512]{1,0:T(8,128)S(1)} %add_add_fusion, f32[256,512]{1,0:T(8,128)} %county_ref.1, s32[]{:T(128)S(6)} %select_n.3), kind=kLoop, calls=%fused_computation.1 | loop fusion | flops 32768 | bytes 393220 | tf_op jit(solution)/shard_map/sub | solution.py:246
  (17 shorter events, 0.1 us)
Async XLA Ops:
  0.6 47.3 %copy-start.4 = (f32[1024]{0:T(1024)S(1)}, f32[1024]{0:T(1024)}, u32[]{:S(2)}) copy-start(f32[1024]{0:T(1024)} %param.20) | copy-start | bytes 12292
  15.2 5.1 %collective-permute-start.4 = (f32[16,512]{1,0:T(8,128)}, f32[16,512]{1,0:T(8,128)S(1)}, u32[]{:S(2)}, u32[]{:S(2)}) collective-permute-start(f32[16,512]{1,0:T(8,128)} %get-tuple-element.22), channel_id=1, source_target_pairs={{0,2},{1,3},{2,0},{3,1},{4,6},{5,7},{6,4},{7,5},{8,10},{9,11},{10,... | collective-permute-start | bytes 98312 | tf_op jit(solution)/shard_map/ppermute | solution.py:144
  18.2 3.6 %collective-permute-start.5 = (f32[16,512]{1,0:T(8,128)}, f32[16,512]{1,0:T(8,128)S(1)}, u32[]{:S(2)}, u32[]{:S(2)}) collective-permute-start(f32[16,512]{1,0:T(8,128)} %get-tuple-element.23), channel_id=1, source_target_pairs={{0,3},{1,2},{2,1},{3,0},{4,7},{5,6},{6,5},{7,4},{8,11},{9,10},{10,... | collective-permute-start | bytes 98312 | tf_op jit(solution)/shard_map/ppermute | solution.py:144
  18.3 3.6 %collective-permute-start.3 = (f32[16,512]{1,0:T(8,128)}, f32[16,512]{1,0:T(8,128)S(1)}, u32[]{:S(2)}, u32[]{:S(2)}) collective-permute-start(f32[16,512]{1,0:T(8,128)} %get-tuple-element.21), channel_id=1, source_target_pairs={{0,1},{1,0},{2,3},{3,2},{4,5},{5,4},{6,7},{7,6},{8,9},{9,8},{10,11... | collective-permute-start | bytes 98312 | tf_op jit(solution)/shard_map/ppermute | solution.py:144
  22.6 9.0 %collective-permute-start.11 = (f32[16,512]{1,0:T(8,128)S(1)}, f32[16,512]{1,0:T(8,128)S(1)}, u32[]{:S(2)}, u32[]{:S(2)}) collective-permute-start(f32[16,512]{1,0:T(8,128)S(1)} %add_add_fusion.2), channel_id=1, source_target_pairs={{0,24},{4,28},{8,16},{12,20},{16,8},{20,12},{24,0},{28,4},{1,25},{... | collective-permute-start | bytes 98312 | tf_op jit(solution)/shard_map/ppermute | solution.py:144
  26.3 7.0 %collective-permute-start.12 = (f32[16,512]{1,0:T(8,128)S(1)}, f32[16,512]{1,0:T(8,128)S(1)}, u32[]{:S(2)}, u32[]{:S(2)}) collective-permute-start(f32[16,512]{1,0:T(8,128)S(1)} %add_add_fusion.2), channel_id=1, source_target_pairs={{0,28},{4,24},{8,20},{12,16},{16,12},{20,8},{24,4},{28,0},{1,29},{... | collective-permute-start | bytes 98312 | tf_op jit(solution)/shard_map/ppermute | solution.py:144
  27.5 7.0 %collective-permute-start.9 = (f32[16,512]{1,0:T(8,128)S(1)}, f32[16,512]{1,0:T(8,128)S(1)}, u32[]{:S(2)}, u32[]{:S(2)}) collective-permute-start(f32[16,512]{1,0:T(8,128)S(1)} %add_add_fusion.2), channel_id=1, source_target_pairs={{0,16},{4,20},{8,24},{12,28},{16,0},{20,4},{24,8},{28,12},{1,17},{... | collective-permute-start | bytes 98312 | tf_op jit(solution)/shard_map/ppermute | solution.py:144
  28.3 7.0 %collective-permute-start.10 = (f32[16,512]{1,0:T(8,128)S(1)}, f32[16,512]{1,0:T(8,128)S(1)}, u32[]{:S(2)}, u32[]{:S(2)}) collective-permute-start(f32[16,512]{1,0:T(8,128)S(1)} %add_add_fusion.2), channel_id=1, source_target_pairs={{0,20},{4,16},{8,28},{12,24},{16,4},{20,0},{24,12},{28,8},{1,21},{... | collective-permute-start | bytes 98312 | tf_op jit(solution)/shard_map/ppermute | solution.py:144
  30.4 4.9 %collective-permute-start.7 = (f32[16,512]{1,0:T(8,128)S(1)}, f32[16,512]{1,0:T(8,128)S(1)}, u32[]{:S(2)}, u32[]{:S(2)}) collective-permute-start(f32[16,512]{1,0:T(8,128)S(1)} %add_add_fusion.2), channel_id=1, source_target_pairs={{0,8},{4,12},{8,0},{12,4},{16,24},{20,28},{24,16},{28,20},{1,9},{5... | collective-permute-start | bytes 98312 | tf_op jit(solution)/shard_map/ppermute | solution.py:144
  31.6 5.0 %collective-permute-start.8 = (f32[16,512]{1,0:T(8,128)S(1)}, f32[16,512]{1,0:T(8,128)S(1)}, u32[]{:S(2)}, u32[]{:S(2)}) collective-permute-start(f32[16,512]{1,0:T(8,128)S(1)} %add_add_fusion.2), channel_id=1, source_target_pairs={{0,12},{4,8},{8,4},{12,0},{16,28},{20,24},{24,20},{28,16},{1,13},{... | collective-permute-start | bytes 98312 | tf_op jit(solution)/shard_map/ppermute | solution.py:144
  33.3 3.9 %collective-permute-start.6 = (f32[16,512]{1,0:T(8,128)S(1)}, f32[16,512]{1,0:T(8,128)S(1)}, u32[]{:S(2)}, u32[]{:S(2)}) collective-permute-start(f32[16,512]{1,0:T(8,128)S(1)} %add_add_fusion.2), channel_id=1, source_target_pairs={{0,4},{4,0},{8,12},{12,8},{16,20},{20,16},{24,28},{28,24},{1,5},{5... | collective-permute-start | bytes 98312 | tf_op jit(solution)/shard_map/ppermute | solution.py:144
  34.5 12.5 %collective-permute-start.1 = (f32[72,512]{1,0:T(8,128)}, f32[72,512]{1,0:T(8,128)S(1)}, u32[]{:S(2)}, u32[]{:S(2)}) collective-permute-start(f32[72,512]{1,0:T(8,128)} %get-tuple-element.18), channel_id=1, source_target_pairs={{0,2},{1,3},{2,0},{3,1},{4,6},{5,7},{6,4},{7,5},{8,10},{9,11},{10,... | collective-permute-start | bytes 442376 | tf_op jit(solution)/shard_map/ppermute | solution.py:144
  35.3 11.7 %collective-permute-start.2 = (f32[72,512]{1,0:T(8,128)}, f32[72,512]{1,0:T(8,128)S(1)}, u32[]{:S(2)}, u32[]{:S(2)}) collective-permute-start(f32[72,512]{1,0:T(8,128)} %get-tuple-element.19), channel_id=1, source_target_pairs={{0,3},{1,2},{2,1},{3,0},{4,7},{5,6},{6,5},{7,4},{8,11},{9,10},{10,... | collective-permute-start | bytes 442376 | tf_op jit(solution)/shard_map/ppermute | solution.py:144
  35.3 11.7 %collective-permute-start = (f32[72,512]{1,0:T(8,128)}, f32[72,512]{1,0:T(8,128)S(1)}, u32[]{:S(2)}, u32[]{:S(2)}) collective-permute-start(f32[72,512]{1,0:T(8,128)} %get-tuple-element.17), channel_id=1, source_target_pairs={{0,1},{1,0},{2,3},{3,2},{4,5},{5,4},{6,7},{7,6},{8,9},{9,8},{10,11... | collective-permute-start | bytes 442376 | tf_op jit(solution)/shard_map/ppermute | solution.py:144
  37.3 6.8 %copy-start = (f32[16,512]{1,0:T(8,128)}, f32[16,512]{1,0:T(8,128)S(1)}, u32[]{:S(2)}) copy-start(f32[16,512]{1,0:T(8,128)S(1)} %add_add_fusion.1.refs_1_) | copy-start | bytes 98308
  37.3 1.3 %collective-permute-start.13 = (f32[16,512]{1,0:T(8,128)S(1)}, f32[16,512]{1,0:T(8,128)S(1)}, u32[]{:S(2)}, u32[]{:S(2)}) collective-permute-start(f32[16,512]{1,0:T(8,128)S(1)} %add_add_fusion.1.refs_1_), channel_id=1, source_target_pairs={{0,1},{1,0},{2,3},{3,2},{4,5},{5,4},{6,7},{7,6},{8,9},{9,8},{10,11... | collective-permute-start | bytes 98312 | tf_op jit(solution)/shard_map/ppermute | solution.py:144
  37.4 6.7 %collective-permute-start.14 = (f32[16,512]{1,0:T(8,128)S(1)}, f32[16,512]{1,0:T(8,128)S(1)}, u32[]{:S(2)}, u32[]{:S(2)}) collective-permute-start(f32[16,512]{1,0:T(8,128)S(1)} %add_add_fusion.1.refs_1_), channel_id=1, source_target_pairs={{0,2},{1,3},{2,0},{3,1},{4,6},{5,7},{6,4},{7,5},{8,10},{9,11},{10,... | collective-permute-start | bytes 98312 | tf_op jit(solution)/shard_map/ppermute | solution.py:144
  38.6 5.5 %copy-start.1 = (f32[16,512]{1,0:T(8,128)}, f32[16,512]{1,0:T(8,128)S(1)}, u32[]{:S(2)}) copy-start(f32[16,512]{1,0:T(8,128)S(1)} %collective-permute-done.13.refs_2_) | copy-start | bytes 98308
  38.6 5.5 %collective-permute-start.15 = (f32[16,512]{1,0:T(8,128)S(1)}, f32[16,512]{1,0:T(8,128)S(1)}, u32[]{:S(2)}, u32[]{:S(2)}) collective-permute-start(f32[16,512]{1,0:T(8,128)S(1)} %add_add_fusion.1.refs_1_), channel_id=1, source_target_pairs={{0,3},{1,2},{2,1},{3,0},{4,7},{5,6},{6,5},{7,4},{8,11},{9,10},{10,... | collective-permute-start | bytes 98312 | tf_op jit(solution)/shard_map/ppermute | solution.py:144
  44.0 0.6 %copy-start.2 = (f32[16,512]{1,0:T(8,128)}, f32[16,512]{1,0:T(8,128)S(1)}, u32[]{:S(2)}) copy-start(f32[16,512]{1,0:T(8,128)S(1)} %collective-permute-done.14.refs_3_) | copy-start | bytes 98308
  44.6 0.6 %copy-start.3 = (f32[16,512]{1,0:T(8,128)}, f32[16,512]{1,0:T(8,128)S(1)}, u32[]{:S(2)}) copy-start(f32[16,512]{1,0:T(8,128)S(1)} %collective-permute-done.15.refs_4_) | copy-start | bytes 98308

commit v3 on v2

v3 whole, which is shorter than its diff:
```python
import functools

import jax
import jax.numpy as jnp
from jax import lax
from jax.experimental import pallas as pl
from jax.experimental.pallas import tpu as pltpu
from jax.sharding import PartitionSpec as P

LANES = 128
ROW_STEP = 1024
VMEM_LIMIT = 60 * 1024 * 1024
F32 = jnp.float32
BF16 = jnp.bfloat16


def split3(x):
    a = x.astype(BF16)
    r = x - a.astype(F32)
    b = r.astype(BF16)
    c = (r - b.astype(F32)).astype(BF16)
    return a, b, c


def hot_dot(hot, x, dims):
    out = None
    for part in reversed(split3(x)):
        term = lax.dot_general(hot, part, (dims, ((), ())), preferred_element_type=F32)
        out = term if out is None else out + term
    return out


def iota_rows(n):
    return lax.broadcasted_iota(jnp.int32, (n, 1), 0)


def pick(values, low, high_hot):
    found = []
    for at in range(0, low.shape[1], LANES):
        index = jnp.broadcast_to(low[:, at : at + LANES], values.shape)
        found.append(jnp.take_along_axis(values, index, axis=1, mode="promise_in_bounds"))
    return jnp.sum(
        jnp.where(high_hot, jnp.concatenate(found, axis=1), jnp.zeros((), values.dtype)),
        axis=0,
        keepdims=True,
    )


def main_kernel(
    count_ref,
    features_ref,
    precinct_ref,
    outcome_ref,
    beta_ref,
    nation_ref,
    state_ref,
    county_ref,
    prec_ref,
    map_ref,
    county_state_ref,
    state_nation_ref,
    *rest,
):
    *outs, feats, table, s0, s1, h0, h1, b0, b1, r0, r1, w0, w1, county_acc, prec_acc, state_acc, sems = rest
    scores, hot_rows, bases, residuals, weights = (s0, s1), (h0, h1), (b0, b1), (r0, r1), (w0, w1)
    n_row = len(outs) // 2
    state_outs, county_outs = outs[:n_row], outs[n_row:]
    n_states = state_ref.shape[0]
    n_nations = nation_ref.shape[0]
    n_cnt, p_size = county_ref.shape
    n_hi = prec_ref.shape[0]
    chunks = precinct_ref.shape[0]
    size = precinct_ref.shape[2]

    def fetch(j):
        rows = pl.ds(pl.multiple_of(j * size, size), size)
        return pltpu.make_async_copy(features_ref.at[rows], feats.at[rows], sems.at[j])

    for j in range(chunks):
        fetch(j).start()

    states = county_state_ref[lax.axis_index("grp")]
    state_hot = (iota_rows(n_states) == states).astype(F32).astype(BF16)
    nation_hot = (iota_rows(n_nations) == state_nation_ref[...]).astype(F32).astype(BF16)
    upper = state_ref[...] + hot_dot(nation_hot, nation_ref[...], ((0,), (0,)))
    table[...] = (county_ref[...] + hot_dot(state_hot, upper, ((0,), (0,))) + beta_ref[...]).astype(BF16)
    county_acc[...] = jnp.zeros_like(county_acc)
    prec_acc[...] = jnp.zeros_like(prec_acc)

    def block(j):
        return feats[pl.ds(pl.multiple_of(j * size, size), size), :]

    def parts_of(j):
        prec = precinct_ref[j]
        return jnp.bitwise_and(prec, LANES - 1), iota_rows(n_hi) == jnp.right_shift(prec, 7)

    def score(j, k):
        low, high_hot = parts_of(j)
        bases[k][...] = pick(prec_ref[...], low, high_hot)
        hot_rows[k][...] = pick(map_ref[...], low, high_hot)
        scores[k][...] = lax.dot_general(
            table[...], block(j), (((1,), (1,)), ((), ())), preferred_element_type=F32
        )

    def residue(j, k):
        county_hot = iota_rows(n_cnt) == hot_rows[k][...]
        linear = jnp.sum(jnp.where(county_hot, scores[k][...], 0.0), axis=0, keepdims=True)
        linear = linear + bases[k][...]
        row = j * size + lax.broadcasted_iota(jnp.int32, (1, size), 1)
        count = outcome_ref[j].astype(F32)
        residual = jnp.where(row < count_ref[0, 0], count - jnp.exp(linear), 0.0)
        residuals[k][...] = residual
        rounded = residual.astype(BF16).astype(F32)
        weights[k][...] = jnp.where(county_hot, rounded, 0.0).astype(BF16)

    def collect(j, k):
        county_acc[...] += jnp.dot(weights[k][...], block(j), preferred_element_type=F32)
        low, high_hot = parts_of(j)
        low_hot = (iota_rows(LANES) == low).astype(F32).astype(BF16)
        by_high = jnp.concatenate(
            [jnp.where(high_hot, x.astype(F32), 0.0) for x in split3(residuals[k][...])[:2]], axis=0
        ).astype(BF16)
        prec_acc[...] += lax.dot_general(
            by_high, low_hot, (((1,), (1,)), ((), ())), preferred_element_type=F32
        )

    fetch(0).wait()
    score(0, 0)
    fetch(1).wait()
    score(1, 1)
    residue(0, 0)

    def body(t, carry):
        j = 2 * t
        fetch(j).wait()
        fetch(j + 1).wait()
        residue(j - 1, 1)
        score(j, 0)
        collect(j - 2, 0)
        residue(j, 0)
        score(j + 1, 1)
        collect(j - 1, 1)
        return carry

    lax.fori_loop(1, chunks // 2, body, 0)
    residue(chunks - 1, 1)
    collect(chunks - 2, 0)
    collect(chunks - 1, 1)

    me = lax.axis_index("row")
    share = n_cnt // n_row
    per = n_states // n_row
    prec_sum = prec_acc[:n_hi] + prec_acc[n_hi:]
    state_acc[...] = hot_dot(state_hot, county_acc[...], ((1,), (0,)))
    for d in range(n_row):
        peer = jnp.bitwise_xor(me, d)
        state_outs[d][...] = state_acc[pl.ds(pl.multiple_of(peer * per, per), per), :]
        county_outs[d][:share, :] = county_acc[pl.ds(pl.multiple_of(peer * share, share), share), :]
        county_outs[d][share:, :LANES] = prec_sum
        county_outs[d][share:, LANES:] = jnp.zeros((n_hi, p_size - LANES), F32)


def end_kernel(*refs):
    state_nation_ref, *gathered, state_ref, nation_ref, beta_ref, state_out, nation_out, beta_out, total = refs
    me = lax.axis_index("row")
    per = gathered[0].shape[0]
    for d, part in enumerate(gathered):
        peer = jnp.bitwise_xor(me, d)
        total[pl.ds(pl.multiple_of(peer * per, per), per), :] = part[...]
    n_nations = nation_ref.shape[0]
    nation_hot = (iota_rows(n_nations) == state_nation_ref[...]).astype(F32).astype(BF16)
    sums = total[...]
    nation_total = hot_dot(nation_hot, sums, ((1,), (0,)))
    state_out[...] = sums - state_ref[...]
    nation_out[...] = nation_total - nation_ref[...]
    beta_out[...] = jnp.sum(nation_total, axis=0, keepdims=True) - beta_ref[...]


def swap(x, axis, d):
    n = lax.axis_size(axis)
    return lax.ppermute(x, axis, [(i, i ^ d) for i in range(n)])


def gather_by(x, axis):
    return [x] + [swap(x, axis, d) for d in range(1, lax.axis_size(axis))]


def total_of(parts):
    while len(parts) > 1:
        parts = [sum(parts[i : i + 2][1:], parts[i]) for i in range(0, len(parts), 2)]
    return parts[0]


def on_device(
    features,
    precinct,
    outcome,
    row_counts,
    beta,
    nation_coef,
    state_coef,
    county_coef,
    precinct_coef,
    precinct_county,
    county_state,
    state_nation,
):
    rows_here, p_size = features.shape
    cnt_here = county_coef.shape[0]
    prec_here = precinct_coef.shape[0]
    n_states = state_coef.shape[0]
    n_row = lax.axis_size("row")
    n_grp = lax.axis_size("grp")
    row_index = lax.axis_index("row")
    share = cnt_here // n_row
    n_hi = prec_here // LANES
    steps = rows_here // ROW_STEP
    per = n_states // n_row

    precinct3 = precinct.reshape(steps, 1, ROW_STEP)
    outcome3 = outcome.reshape(steps, 1, ROW_STEP)
    states3 = county_state.reshape(n_grp, 1, cnt_here)
    prec2 = precinct_coef.reshape(n_hi, LANES)
    map2 = precinct_county.reshape(n_hi, LANES)
    beta2 = beta.reshape(1, p_size)
    nation_row = state_nation.reshape(1, n_states)

    outs = pl.pallas_call(
        main_kernel,
        in_specs=[pl.BlockSpec(memory_space=pltpu.SMEM), pl.BlockSpec(memory_space=pl.ANY)]
        + [pl.BlockSpec(memory_space=pltpu.VMEM)] * 10,
        out_shape=[jax.ShapeDtypeStruct((per, p_size), F32)] * n_row
        + [jax.ShapeDtypeStruct((share + n_hi, p_size), F32)] * n_row,
        scratch_shapes=[
            pltpu.VMEM((rows_here, p_size), BF16),
            pltpu.VMEM((cnt_here, p_size), BF16),
            pltpu.VMEM((cnt_here, ROW_STEP), F32),
            pltpu.VMEM((cnt_here, ROW_STEP), F32),
            pltpu.VMEM((1, ROW_STEP), jnp.int32),
            pltpu.VMEM((1, ROW_STEP), jnp.int32),
            pltpu.VMEM((1, ROW_STEP), F32),
            pltpu.VMEM((1, ROW_STEP), F32),
            pltpu.VMEM((1, ROW_STEP), F32),
            pltpu.VMEM((1, ROW_STEP), F32),
            pltpu.VMEM((cnt_here, ROW_STEP), BF16),
            pltpu.VMEM((cnt_here, ROW_STEP), BF16),
            pltpu.VMEM((cnt_here, p_size), F32),
            pltpu.VMEM((2 * n_hi, LANES), F32),
            pltpu.VMEM(state_coef.shape, F32),
            pltpu.SemaphoreType.DMA((steps,)),
        ],
        compiler_params=pltpu.CompilerParams(vmem_limit_bytes=VMEM_LIMIT),
        name="local_sums",
    )(
        row_counts,
        features,
        precinct3,
        outcome3,
        beta2,
        nation_coef,
        state_coef,
        county_coef,
        prec2,
        map2,
        states3,
        nation_row,
    )

    state_parts = [outs[0]] + [swap(outs[d], "row", d) for d in range(1, n_row)]
    state_piece = total_of(state_parts)
    copies = jnp.broadcast_to(state_piece, (n_grp,) + state_piece.shape)
    state_piece = jnp.sum(lax.all_to_all(copies, "grp", 0, 0, tiled=True), axis=0)
    gathered = gather_by(state_piece, "row")
    county_parts = [outs[n_row]] + [swap(outs[n_row + d], "row", d) for d in range(1, n_row)]
    county_sum = total_of(county_parts)
    own_coef = lax.dynamic_slice_in_dim(county_coef, row_index * share, share, 0)
    county_grad = county_sum[:share] - own_coef
    precinct_grad = county_sum[share:, :LANES].reshape(prec_here) - precinct_coef

    *gathered, county_grad, precinct_grad = lax.optimization_barrier(
        (*gathered, county_grad, precinct_grad)
    )
    state_grad, nation_grad, beta_grad = pl.pallas_call(
        end_kernel,
        out_shape=[
            jax.ShapeDtypeStruct(state_coef.shape, F32),
            jax.ShapeDtypeStruct(nation_coef.shape, F32),
            jax.ShapeDtypeStruct((1, p_size), F32),
        ],
        scratch_shapes=[pltpu.VMEM(state_coef.shape, F32)],
        compiler_params=pltpu.CompilerParams(vmem_limit_bytes=VMEM_LIMIT),
        name="upper_totals",
    )(nation_row, *gathered, state_coef, nation_coef, beta2)
    return county_grad, precinct_grad, state_grad, nation_grad, beta_grad.reshape(p_size)


def solution(mesh):
    placed = (
        P(("grp", "row"), None),
        P(("grp", "row")),
        P(("grp", "row")),
        P("grp", "row"),
        P(),
        P(),
        P(),
        P("grp", None),
        P("grp"),
        P("grp"),
        P(),
        P(),
    )
    return jax.shard_map(
        on_device,
        mesh=mesh,
        in_specs=placed,
        out_specs=(P(("grp", "row"), None), P("grp"), P(), P(), P()),
        check_vma=False,
    )
```

time: 50.4 us -> 43.3 us (0.86)
  starting transfers between devices: 18.7 us -> 13 us
  Pallas kernels: 15.7 us -> 12.7 us
  waiting for transfers between devices: 9.24 us -> 9.99 us
  local copies, waits for them, and re-layouts: 1.21 us -> 1.93 us
    ppermute x16 -> x9, starting transfers between devices: 18.7 us -> 7.18 us  [swap(): return lax.ppermute(x, axis, [(i, i ^ d) for i in range(n)])]
    all_to_all x0 -> x1, waiting for transfers between devices: none -> 6.99 us  [on_device(): lax.all_to_all(copies, 'grp', 0, 0, tiled=True)]
    ppermute x16 -> x9, waiting for transfers between devices: 9.24 us -> 2.99 us  [swap(): return lax.ppermute(x, axis, [(i, i ^ d) for i in range(n)])]
    all_to_all x0 -> x1, starting transfers between devices: none -> 5.81 us  [on_device(): lax.all_to_all(copies, 'grp', 0, 0, tiled=True)]
    pallas_call x1, Pallas kernels: 13.9 us -> 11 us  [on_device(): pl.pallas_call(main_kernel, in_specs=[pl.BlockSpec(memory_space=pltpu.SME...]
    broadcast_in_dim x0 -> x1, local copies, waits for them, and re-layouts: none -> 0.73 us  [on_device(): copies = jnp.broadcast_to(state_piece, (n_grp,) + state_piece.shape)]
    add x3 -> x2, other arithmetic: 1.75 us -> 1.72 us  [total_of(): parts = [sum(parts[i:i + 2][1:], parts[i]) for i in range(0, len(parts), 2)]]
  transfers between devices with their start and end apart: 16 -> 10, of which waited for: 5 -> 4; matrix products, arithmetic and copies ran while one was open for 0% -> 11% of each run, Pallas kernels for 3% -> 0%
where the time goes in v3:
time: 43.3 us; the launch traced here: 42.9 us
  starting transfers between devices  13 us (30%)
  Pallas kernels  12.7 us (29%)
  waiting for transfers between devices  9.99 us (23%)
  other arithmetic  3.92 us (9%)
  local copies, waits for them, and re-layouts  1.93 us (4%)
  between operations  1.37 us (3%)
    pallas_call x1, Pallas kernels, on_device(): pl.pallas_call(main_kernel, in_specs=[pl.BlockSpec(memory_space=pltpu.SME...  11 us
    ppermute x9, starting transfers between devices, swap(): return lax.ppermute(x, axis, [(i, i ^ d) for i in range(n)])  7.18 us
    all_to_all x1, waiting for transfers between devices, on_device(): lax.all_to_all(copies, 'grp', 0, 0, tiled=True)  6.99 us
    all_to_all x1, starting transfers between devices, on_device(): lax.all_to_all(copies, 'grp', 0, 0, tiled=True)  5.81 us
    ppermute x9, waiting for transfers between devices, swap(): return lax.ppermute(x, axis, [(i, i ^ d) for i in range(n)])  2.99 us
    pallas_call x1, Pallas kernels, on_device(): pl.pallas_call(end_kernel, out_shape=[jax.ShapeDtypeStruct(state_coef.sha...  1.73 us
    add x2, other arithmetic, total_of(): parts = [sum(parts[i:i + 2][1:], parts[i]) for i in range(0, len(parts), 2)]  1.72 us
    sub x1, other arithmetic, on_device(): county_grad = county_sum[:share] - own_coef  1.59 us
  transfers between devices with their start and end apart: 10, of which 4 were waited for; matrix products, arithmetic and copies ran while one was open for 11% of the time, Pallas kernels for 0%

profile of v3, /device:TPU:0, one launch (start us, length us, event | category | flops | bytes accessed | tf_op | source)
XLA Modules:
  0.0 42.9 jit_solution(4494774878070502963)
XLA Ops:
  0.6 0.0 copy-start.4
  1.3 11.0 %local_sums.1 = (f32[16,512]{1,0:T(8,128)}, f32[16,512]{1,0:T(8,128)}, f32[16,512]{1,0:T(8,128)}, f32[16,512]{1,0:T(8,128)}, f32[72,512]{1,0:T(8,128)}, /*index=...) custom-call(s32[1,1]{1,0:T(1,128)S(6)} %copy.17.count_ref, bf16[8192,512]{1,0:T(8,128)(2,1)} %features_ref.1, ...), custom_call_target="tpu_custom_call" | custom-call | tf_op jit(solution)/shard_map/local_sums/pallas_call | solution.py:228
  12.3 0.5 %collective-permute-start = (f32[16,512]{1,0:T(8,128)}, f32[16,512]{1,0:T(8,128)S(1)}, u32[]{:S(2)}, u32[]{:S(2)}) collective-permute-start(f32[16,512]{1,0:T(8,128)} %get-tuple-element.23), channel_id=1, source_target_pairs={{0,1},{1,0},{2,3},{3,2},{4,5},{5,4},{6,7},{7,6},{8,9},{9,8},{10,11... | collective-permute-start | bytes 98312 | tf_op jit(solution)/shard_map/ppermute | solution.py:181
  12.8 2.6 %collective-permute-start.1 = (f32[16,512]{1,0:T(8,128)}, f32[16,512]{1,0:T(8,128)S(1)}, u32[]{:S(2)}, u32[]{:S(2)}) collective-permute-start(f32[16,512]{1,0:T(8,128)} %get-tuple-element.24), channel_id=1, source_target_pairs={{0,2},{1,3},{2,0},{3,1},{4,6},{5,7},{6,4},{7,5},{8,10},{9,11},{10,... | collective-permute-start | bytes 98312 | tf_op jit(solution)/shard_map/ppermute | solution.py:181
  15.4 0.1 collective-permute-start.2
  15.5 0.1 collective-permute-start.6
  15.6 1.9 %collective-permute-start.7 = (f32[72,512]{1,0:T(8,128)}, f32[72,512]{1,0:T(8,128)S(1)}, u32[]{:S(2)}, u32[]{:S(2)}) collective-permute-start(f32[72,512]{1,0:T(8,128)} %get-tuple-element.28), channel_id=1, source_target_pairs={{0,2},{1,3},{2,0},{3,1},{4,6},{5,7},{6,4},{7,5},{8,10},{9,11},{10,... | collective-permute-start | bytes 442376 | tf_op jit(solution)/shard_map/ppermute | solution.py:181
  17.5 0.0 collective-permute-done
  17.5 0.0 collective-permute-start.8
  17.6 0.0 collective-permute-done.1
  17.6 1.4 %collective-permute-done.2 = f32[16,512]{1,0:T(8,128)S(1)} collective-permute-done((f32[16,512]{1,0:T(8,128)}, f32[16,512]{1,0:T(8,128)S(1)}, u32[]{:S(2)}, u32[]{:S(2)}) %collective-permute-start.2) | collective-permute-done | bytes 32800 | tf_op jit(solution)/shard_map/ppermute | solution.py:181
  19.0 0.8 %add_add_fusion.1 = f32[16,512]{1,0:T(8,128)S(1)} fusion(f32[16,512]{1,0:T(8,128)S(1)} %collective-permute-done.1, f32[16,512]{1,0:T(8,128)S(1)} %collective-permute-done.2, f32[16,512]{1,0:T(8,128)} %get-tuple-element.22, f32[16,512]{1,0:T(8,128)S(1)} %collective-permute-done), kind=kLoop, calls=%fused_computation.2 | loop fusion | flops 24576 | bytes 163840 | tf_op jit(solution)/shard_map/add | solution.py:190
  19.7 0.7 %broadcast_in_dim.3 = f32[8,16,512]{2,1,0:T(8,128)} broadcast(f32[16,512]{1,0:T(8,128)S(1)} %add_add_fusion.1), dimensions={1,2} | broadcast | bytes 294912 | tf_op jit(solution)/shard_map/broadcast_in_dim | solution.py:271
  20.5 5.8 %all-to-all-start = ((f32[8,16,512]{2,1,0:T(8,128)}), f32[8,16,512]{2,1,0:T(8,128)S(1)}, u32[]{:S(2)}, u32[]{:S(2)}) async-start(f32[8,16,512]{2,1,0:T(8,128)} %broadcast_in_dim.3), calls=%async_computation | async-start | bytes 524288 | tf_op jit(solution)/shard_map/all_to_all | solution.py:272
  26.3 0.0 collective-permute-done.6
  26.3 0.0 collective-permute-done.7
  26.3 0.0 collective-permute-done.8
  26.3 1.0 %add_add_fusion = f32[72,512]{1,0:T(8,128)S(1)} fusion(f32[72,512]{1,0:T(8,128)S(1)} %collective-permute-done.7, f32[72,512]{1,0:T(8,128)S(1)} %collective-permute-done.8, f32[72,512]{1,0:T(8,128)} %get-tuple-element.26, f32[72,512]{1,0:T(8,128)S(1)} %collective-permute-done.6), kind=kLoop, calls=%fused_computation | loop fusion | flops 110592 | bytes 737280 | tf_op jit(solution)/shard_map/add | solution.py:190
  27.2 1.6 %slice_subtract_fusion = f32[64,512]{1,0:T(8,128)} fusion(f32[72,512]{1,0:T(8,128)S(1)} %add_add_fusion, f32[256,512]{1,0:T(8,128)} %county_ref.1, s32[]{:T(128)S(6)} %select_n.3), kind=kLoop, calls=%fused_computation.1 | loop fusion | flops 32768 | bytes 393220 | tf_op jit(solution)/shard_map/sub | solution.py:277
  28.8 7.0 %all-to-all-done = f32[8,16,512]{2,1,0:T(8,128)S(1)} async-done(((f32[8,16,512]{2,1,0:T(8,128)}), f32[8,16,512]{2,1,0:T(8,128)S(1)}, u32[]{:S(2)}, u32[]{:S(2)}) %all-to-all-start) | async-done | bytes 262176 | tf_op jit(solution)/shard_map/all_to_all | solution.py:272
  35.8 0.0 copy-start
  35.9 0.1 collective-permute-start.5
  35.9 0.6 %collective-permute-start.4 = (f32[16,512]{1,0:T(8,128)S(1)}, f32[16,512]{1,0:T(8,128)S(1)}, u32[]{:S(2)}, u32[]{:S(2)}) collective-permute-start(f32[16,512]{1,0:T(8,128)S(1)} %reduce_sum.9.refs_1_), channel_id=1, source_target_pairs={{0,2},{1,3},{2,0},{3,1},{4,6},{5,7},{6,4},{7,5},{8,10},{9,11},{10,... | collective-permute-start | bytes 98312 | tf_op jit(solution)/shard_map/ppermute | solution.py:181
  36.5 1.2 %collective-permute-start.3 = (f32[16,512]{1,0:T(8,128)S(1)}, f32[16,512]{1,0:T(8,128)S(1)}, u32[]{:S(2)}, u32[]{:S(2)}) collective-permute-start(f32[16,512]{1,0:T(8,128)S(1)} %reduce_sum.9.refs_1_), channel_id=1, source_target_pairs={{0,1},{1,0},{2,3},{3,2},{4,5},{5,4},{6,7},{7,6},{8,9},{9,8},{10,11... | collective-permute-start | bytes 98312 | tf_op jit(solution)/shard_map/ppermute | solution.py:181
  37.8 0.0 copy-done.4
  37.8 0.6 %fusion = f32[1024]{0:T(1024)} fusion(f32[1024]{0:T(1024)S(1)} %copy-done.4, f32[72,512]{1,0:T(8,128)S(1)} %add_add_fusion), kind=kLoop, calls=%fused_computation.4 | loop fusion | flops 1024 | bytes 12288 | tf_op jit(solution)/shard_map/sub | solution.py:278
  38.4 0.9 %collective-permute-done.5.refs_4_ = f32[16,512]{1,0:T(8,128)S(1)} collective-permute-done((f32[16,512]{1,0:T(8,128)S(1)}, f32[16,512]{1,0:T(8,128)S(1)}, u32[]{:S(2)}, u32[]{:S(2)}) %collective-permute-start.5) | collective-permute-done | bytes 32800 | tf_op jit(solution)/shard_map/ppermute | solution.py:181
  39.3 0.7 %collective-permute-done.4.refs_3_ = f32[16,512]{1,0:T(8,128)S(1)} collective-permute-done((f32[16,512]{1,0:T(8,128)S(1)}, f32[16,512]{1,0:T(8,128)S(1)}, u32[]{:S(2)}, u32[]{:S(2)}) %collective-permute-start.4) | collective-permute-done | bytes 32800 | tf_op jit(solution)/shard_map/ppermute | solution.py:181
  40.0 0.0 collective-permute-done.3.refs_2_
  40.0 0.6 %copy-done.2 = f32[16,512]{1,0:T(8,128)} copy-done((f32[16,512]{1,0:T(8,128)}, f32[16,512]{1,0:T(8,128)S(1)}, u32[]{:S(2)}) %copy-start.2) | copy-done | bytes 32792
  40.6 0.6 %copy-done.3 = f32[16,512]{1,0:T(8,128)} copy-done((f32[16,512]{1,0:T(8,128)}, f32[16,512]{1,0:T(8,128)S(1)}, u32[]{:S(2)}) %copy-start.3) | copy-done | bytes 32792
  41.2 1.7 %upper_totals.1 = (f32[64,512]{1,0:T(8,128)}, f32[4,512]{1,0:T(4,128)}, f32[1,512]{1,0:T(1,128)}) custom-call(s32[1,64]{1,0:T(1,128)} %bitcast.20, f32[16,512]{1,0:T(8,128)} %copy-done, f32[16,512]{1,0:T(8,128)} %copy-done.3, f32[16,512]{1,0:T(8,128)} %copy-done.2, f32[16,512]{1,0:T(8,128)} %copy-done.1, f32[64,512]{1,0:T(8,128)} %refs_5_.1, ...), custom_call_target="tpu_custom_call" | custom-call | tf_op jit(solution)/shard_map/upper_totals/pallas_call | solution.py:283
  (6 shorter events, 0.0 us)
Async XLA Ops:
  0.6 37.1 %copy-start.4 = (f32[1024]{0:T(1024)S(1)}, f32[1024]{0:T(1024)}, u32[]{:S(2)}) copy-start(f32[1024]{0:T(1024)} %param.20) | copy-start | bytes 12292
  12.3 5.3 %collective-permute-start = (f32[16,512]{1,0:T(8,128)}, f32[16,512]{1,0:T(8,128)S(1)}, u32[]{:S(2)}, u32[]{:S(2)}) collective-permute-start(f32[16,512]{1,0:T(8,128)} %get-tuple-element.23), channel_id=1, source_target_pairs={{0,1},{1,0},{2,3},{3,2},{4,5},{5,4},{6,7},{7,6},{8,9},{9,8},{10,11... | collective-permute-start | bytes 98312 | tf_op jit(solution)/shard_map/ppermute | solution.py:181
  12.8 4.8 %collective-permute-start.1 = (f32[16,512]{1,0:T(8,128)}, f32[16,512]{1,0:T(8,128)S(1)}, u32[]{:S(2)}, u32[]{:S(2)}) collective-permute-start(f32[16,512]{1,0:T(8,128)} %get-tuple-element.24), channel_id=1, source_target_pairs={{0,2},{1,3},{2,0},{3,1},{4,6},{5,7},{6,4},{7,5},{8,10},{9,11},{10,... | collective-permute-start | bytes 98312 | tf_op jit(solution)/shard_map/ppermute | solution.py:181
  15.4 3.6 %collective-permute-start.2 = (f32[16,512]{1,0:T(8,128)}, f32[16,512]{1,0:T(8,128)S(1)}, u32[]{:S(2)}, u32[]{:S(2)}) collective-permute-start(f32[16,512]{1,0:T(8,128)} %get-tuple-element.25), channel_id=1, source_target_pairs={{0,3},{1,2},{2,1},{3,0},{4,7},{5,6},{6,5},{7,4},{8,11},{9,10},{10,... | collective-permute-start | bytes 98312 | tf_op jit(solution)/shard_map/ppermute | solution.py:181
  15.5 10.8 %collective-permute-start.6 = (f32[72,512]{1,0:T(8,128)}, f32[72,512]{1,0:T(8,128)S(1)}, u32[]{:S(2)}, u32[]{:S(2)}) collective-permute-start(f32[72,512]{1,0:T(8,128)} %get-tuple-element.27), channel_id=1, source_target_pairs={{0,1},{1,0},{2,3},{3,2},{4,5},{5,4},{6,7},{7,6},{8,9},{9,8},{10,11... | collective-permute-start | bytes 442376 | tf_op jit(solution)/shard_map/ppermute | solution.py:181
  15.6 10.7 %collective-permute-start.7 = (f32[72,512]{1,0:T(8,128)}, f32[72,512]{1,0:T(8,128)S(1)}, u32[]{:S(2)}, u32[]{:S(2)}) collective-permute-start(f32[72,512]{1,0:T(8,128)} %get-tuple-element.28), channel_id=1, source_target_pairs={{0,2},{1,3},{2,0},{3,1},{4,6},{5,7},{6,4},{7,5},{8,10},{9,11},{10,... | collective-permute-start | bytes 442376 | tf_op jit(solution)/shard_map/ppermute | solution.py:181
  17.5 8.7 %collective-permute-start.8 = (f32[72,512]{1,0:T(8,128)}, f32[72,512]{1,0:T(8,128)S(1)}, u32[]{:S(2)}, u32[]{:S(2)}) collective-permute-start(f32[72,512]{1,0:T(8,128)} %get-tuple-element.29), channel_id=1, source_target_pairs={{0,3},{1,2},{2,1},{3,0},{4,7},{5,6},{6,5},{7,4},{8,11},{9,10},{10,... | collective-permute-start | bytes 442376 | tf_op jit(solution)/shard_map/ppermute | solution.py:181
  20.5 15.4 %all-to-all-start = ((f32[8,16,512]{2,1,0:T(8,128)}), f32[8,16,512]{2,1,0:T(8,128)S(1)}, u32[]{:S(2)}, u32[]{:S(2)}) async-start(f32[8,16,512]{2,1,0:T(8,128)} %broadcast_in_dim.3), calls=%async_computation | async-start | bytes 524288 | tf_op jit(solution)/shard_map/all_to_all | solution.py:272
  35.8 4.1 %copy-start = (f32[16,512]{1,0:T(8,128)}, f32[16,512]{1,0:T(8,128)S(1)}, u32[]{:S(2)}) copy-start(f32[16,512]{1,0:T(8,128)S(1)} %reduce_sum.9.refs_1_) | copy-start | bytes 98308
  35.9 3.4 %collective-permute-start.5 = (f32[16,512]{1,0:T(8,128)S(1)}, f32[16,512]{1,0:T(8,128)S(1)}, u32[]{:S(2)}, u32[]{:S(2)}) collective-permute-start(f32[16,512]{1,0:T(8,128)S(1)} %reduce_sum.9.refs_1_), channel_id=1, source_target_pairs={{0,3},{1,2},{2,1},{3,0},{4,7},{5,6},{6,5},{7,4},{8,11},{9,10},{10,... | collective-permute-start | bytes 98312 | tf_op jit(solution)/shard_map/ppermute | solution.py:181
  35.9 4.0 %collective-permute-start.4 = (f32[16,512]{1,0:T(8,128)S(1)}, f32[16,512]{1,0:T(8,128)S(1)}, u32[]{:S(2)}, u32[]{:S(2)}) collective-permute-start(f32[16,512]{1,0:T(8,128)S(1)} %reduce_sum.9.refs_1_), channel_id=1, source_target_pairs={{0,2},{1,3},{2,0},{3,1},{4,6},{5,7},{6,4},{7,5},{8,10},{9,11},{10,... | collective-permute-start | bytes 98312 | tf_op jit(solution)/shard_map/ppermute | solution.py:181
  36.5 3.4 %collective-permute-start.3 = (f32[16,512]{1,0:T(8,128)S(1)}, f32[16,512]{1,0:T(8,128)S(1)}, u32[]{:S(2)}, u32[]{:S(2)}) collective-permute-start(f32[16,512]{1,0:T(8,128)S(1)} %reduce_sum.9.refs_1_), channel_id=1, source_target_pairs={{0,1},{1,0},{2,3},{3,2},{4,5},{5,4},{6,7},{7,6},{8,9},{9,8},{10,11... | collective-permute-start | bytes 98312 | tf_op jit(solution)/shard_map/ppermute | solution.py:181
  39.3 0.7 %copy-start.1 = (f32[16,512]{1,0:T(8,128)}, f32[16,512]{1,0:T(8,128)S(1)}, u32[]{:S(2)}) copy-start(f32[16,512]{1,0:T(8,128)S(1)} %collective-permute-done.5.refs_4_) | copy-start | bytes 98308
  40.0 0.6 %copy-start.2 = (f32[16,512]{1,0:T(8,128)}, f32[16,512]{1,0:T(8,128)S(1)}, u32[]{:S(2)}) copy-start(f32[16,512]{1,0:T(8,128)S(1)} %collective-permute-done.4.refs_3_) | copy-start | bytes 98308
  40.6 0.6 %copy-start.3 = (f32[16,512]{1,0:T(8,128)}, f32[16,512]{1,0:T(8,128)S(1)}, u32[]{:S(2)}) copy-start(f32[16,512]{1,0:T(8,128)S(1)} %collective-permute-done.3.refs_2_) | copy-start | bytes 98308

commit v4 on v3

--- a/solution.py
+++ b/solution.py
@@ -9,7 +9,9 @@
 
 LANES = 128
 ROW_STEP = 1024
+SMALL = 10
 VMEM_LIMIT = 60 * 1024 * 1024
+END_LIMIT = 16 * 1024 * 1024
 F32 = jnp.float32
 BF16 = jnp.bfloat16
 
@@ -46,22 +48,25 @@
     )
 
 
-def main_kernel(
-    count_ref,
-    features_ref,
-    precinct_ref,
-    outcome_ref,
-    beta_ref,
-    nation_ref,
-    state_ref,
-    county_ref,
-    prec_ref,
-    map_ref,
-    county_state_ref,
-    state_nation_ref,
-    *rest,
-):
-    *outs, feats, table, s0, s1, h0, h1, b0, b1, r0, r1, w0, w1, county_acc, prec_acc, state_acc, sems = rest
+def main_kernel(n_out, count_ref, features_ref, *args):
+    small = args[:SMALL]
+    out_refs = args[SMALL : SMALL + n_out]
+    held = args[SMALL + n_out : 2 * SMALL + n_out]
+    feats, table, s0, s1, h0, h1, b0, b1, r0, r1, w0, w1, county_acc, prec_acc, state_acc, *outs, small_sems, sems, out_sems = (
+        args[2 * SMALL + n_out :]
+    )
+    (
+        state_nation_ref,
+        nation_ref,
+        state_ref,
+        county_state_ref,
+        county_ref,
+        beta_ref,
+        precinct_ref,
+        prec_ref,
+        map_ref,
+        outcome_ref,
+    ) = held
     scores, hot_rows, bases, residuals, weights = (s0, s1), (h0, h1), (b0, b1), (r0, r1), (w0, w1)
     n_row = len(outs) // 2
     state_outs, county_outs = outs[:n_row], outs[n_row:]
@@ -76,8 +81,16 @@
         rows = pl.ds(pl.multiple_of(j * size, size), size)
         return pltpu.make_async_copy(features_ref.at[rows], feats.at[rows], sems.at[j])
 
+    small_copies = [
+        pltpu.make_async_copy(source, target, small_sems.at[k])
+        for k, (source, target) in enumerate(zip(small, held))
+    ]
+    for copy in small_copies:
+        copy.start()
     for j in range(chunks):
         fetch(j).start()
+    for copy in small_copies:
+        copy.wait()
 
     states = county_state_ref[lax.axis_index("grp")]
     state_hot = (iota_rows(n_states) == states).astype(F32).astype(BF16)
@@ -108,7 +121,7 @@
         linear = linear + bases[k][...]
         row = j * size + lax.broadcasted_iota(jnp.int32, (1, size), 1)
         count = outcome_ref[j].astype(F32)
-        residual = jnp.where(row < count_ref[0, 0], count - jnp.exp(linear), 0.0)
+        residual = jnp.where(row < count_ref[...], count - jnp.exp(linear), 0.0)
         residuals[k][...] = residual
         rounded = residual.astype(BF16).astype(F32)
         weights[k][...] = jnp.where(county_hot, rounded, 0.0).astype(BF16)
@@ -151,29 +164,57 @@
     share = n_cnt // n_row
     per = n_states // n_row
     prec_sum = prec_acc[:n_hi] + prec_acc[n_hi:]
+    own_rows = pl.ds(pl.multiple_of(me * share, share), share)
+
+    def send(k):
+        copy = pltpu.make_async_copy(outs[k], out_refs[k], out_sems.at[k])
+        copy.start()
+        return copy
+
+    copies = []
+    for d in range(n_row):
+        peer = jnp.bitwise_xor(me, d)
+        sums = county_acc[pl.ds(pl.multiple_of(peer * share, share), share), :]
+        county_outs[d][:share, :] = sums if d else sums - county_ref[own_rows, :]
+        county_outs[d][share:, :LANES] = prec_sum if d else prec_sum - prec_ref[...]
+        county_outs[d][share:, LANES:] = jnp.zeros((n_hi, p_size - LANES), F32)
+        copies.append(send(n_row + d))
     state_acc[...] = hot_dot(state_hot, county_acc[...], ((1,), (0,)))
     for d in range(n_row):
         peer = jnp.bitwise_xor(me, d)
         state_outs[d][...] = state_acc[pl.ds(pl.multiple_of(peer * per, per), per), :]
-        county_outs[d][:share, :] = county_acc[pl.ds(pl.multiple_of(peer * share, share), share), :]
-        county_outs[d][share:, :LANES] = prec_sum
-        county_outs[d][share:, LANES:] = jnp.zeros((n_hi, p_size - LANES), F32)
-
-
-def end_kernel(*refs):
-    state_nation_ref, *gathered, state_ref, nation_ref, beta_ref, state_out, nation_out, beta_out, total = refs
+        copies.append(send(d))
+    for copy in copies:
+        copy.wait()
+
+
+def county_end_kernel(state_nation_ref, state_ref, nation_ref, beta_ref, *refs):
+    *parts, county_out, prec_out, prior_out, hot_out = refs
+    share = county_out.shape[0]
+    n_states = state_ref.shape[0]
+    n_nations = nation_ref.shape[0]
+    prior_out[:n_states, :] = state_ref[...]
+    prior_out[n_states : n_states + n_nations, :] = nation_ref[...]
+    prior_out[n_states + n_nations :, :] = beta_ref[...]
+    hot_out[...] = (iota_rows(n_nations) == state_nation_ref[...]).astype(F32)
+    county_out[...] = total_of([part[:share, :] for part in parts])
+    prec_out[...] = total_of([part[share:, :LANES] for part in parts])
+
+
+def end_kernel(prior_ref, hot_ref, *refs):
+    *gathered, state_out, nation_out, beta_out, total = refs
     me = lax.axis_index("row")
     per = gathered[0].shape[0]
+    n_states = state_out.shape[0]
+    n_nations = nation_out.shape[0]
     for d, part in enumerate(gathered):
         peer = jnp.bitwise_xor(me, d)
         total[pl.ds(pl.multiple_of(peer * per, per), per), :] = part[...]
-    n_nations = nation_ref.shape[0]
-    nation_hot = (iota_rows(n_nations) == state_nation_ref[...]).astype(F32).astype(BF16)
     sums = total[...]
-    nation_total = hot_dot(nation_hot, sums, ((1,), (0,)))
-    state_out[...] = sums - state_ref[...]
-    nation_out[...] = nation_total - nation_ref[...]
-    beta_out[...] = jnp.sum(nation_total, axis=0, keepdims=True) - beta_ref[...]
+    nation_total = hot_dot(hot_ref[...].astype(BF16), sums, ((1,), (0,)))
+    state_out[...] = sums - prior_ref[:n_states, :]
+    nation_out[...] = nation_total - prior_ref[n_states : n_states + n_nations, :]
+    beta_out[...] = jnp.sum(nation_total, axis=0, keepdims=True) - prior_ref[n_states + n_nations :, :]
 
 
 def swap(x, axis, d):
@@ -181,8 +222,8 @@
     return lax.ppermute(x, axis, [(i, i ^ d) for i in range(n)])
 
 
-def gather_by(x, axis):
-    return [x] + [swap(x, axis, d) for d in range(1, lax.axis_size(axis))]
+def gather_by(x, axis, distances):
+    return [x] + [swap(x, axis, d) for d in distances]
 
 
 def total_of(parts):
@@ -211,7 +252,6 @@
     n_states = state_coef.shape[0]
     n_row = lax.axis_size("row")
     n_grp = lax.axis_size("grp")
-    row_index = lax.axis_index("row")
     share = cnt_here // n_row
     n_hi = prec_here // LANES
     steps = rows_here // ROW_STEP
@@ -225,13 +265,28 @@
     beta2 = beta.reshape(1, p_size)
     nation_row = state_nation.reshape(1, n_states)
 
+    n_nations = nation_coef.shape[0]
+    small = (
+        nation_row,
+        nation_coef,
+        state_coef,
+        states3,
+        county_coef,
+        beta2,
+        precinct3,
+        prec2,
+        map2,
+        outcome3,
+    )
     outs = pl.pallas_call(
-        main_kernel,
-        in_specs=[pl.BlockSpec(memory_space=pltpu.SMEM), pl.BlockSpec(memory_space=pl.ANY)]
-        + [pl.BlockSpec(memory_space=pltpu.VMEM)] * 10,
+        functools.partial(main_kernel, 2 * n_row),
+        in_specs=[pl.BlockSpec(memory_space=pltpu.VMEM)]
+        + [pl.BlockSpec(memory_space=pltpu.HBM)] * (SMALL + 1),
+        out_specs=[pl.BlockSpec(memory_space=pltpu.HBM)] * (2 * n_row),
         out_shape=[jax.ShapeDtypeStruct((per, p_size), F32)] * n_row
         + [jax.ShapeDtypeStruct((share + n_hi, p_size), F32)] * n_row,
-        scratch_shapes=[
+        scratch_shapes=[pltpu.VMEM(x.shape, x.dtype) for x in small]
+        + [
             pltpu.VMEM((rows_here, p_size), BF16),
             pltpu.VMEM((cnt_here, p_size), BF16),
             pltpu.VMEM((cnt_here, ROW_STEP), F32),
@@ -247,39 +302,38 @@
             pltpu.VMEM((cnt_here, p_size), F32),
             pltpu.VMEM((2 * n_hi, LANES), F32),
             pltpu.VMEM(state_coef.shape, F32),
+        ]
+        + [pltpu.VMEM((per, p_size), F32)] * n_row
+        + [pltpu.VMEM((share + n_hi, p_size), F32)] * n_row
+        + [
+            pltpu.SemaphoreType.DMA((SMALL,)),
             pltpu.SemaphoreType.DMA((steps,)),
+            pltpu.SemaphoreType.DMA((2 * n_row,)),
         ],
         compiler_params=pltpu.CompilerParams(vmem_limit_bytes=VMEM_LIMIT),
         name="local_sums",
-    )(
-        row_counts,
-        features,
-        precinct3,
-        outcome3,
-        beta2,
-        nation_coef,
-        state_coef,
-        county_coef,
-        prec2,
-        map2,
-        states3,
-        nation_row,
-    )
-
+    )(row_counts, features, *small)
+
+    near = 1 << (n_grp.bit_length() // 2 - 1)
     state_parts = [outs[0]] + [swap(outs[d], "row", d) for d in range(1, n_row)]
     state_piece = total_of(state_parts)
-    copies = jnp.broadcast_to(state_piece, (n_grp,) + state_piece.shape)
-    state_piece = jnp.sum(lax.all_to_all(copies, "grp", 0, 0, tiled=True), axis=0)
-    gathered = gather_by(state_piece, "row")
-    county_parts = [outs[n_row]] + [swap(outs[n_row + d], "row", d) for d in range(1, n_row)]
-    county_sum = total_of(county_parts)
-    own_coef = lax.dynamic_slice_in_dim(county_coef, row_index * share, share, 0)
-    county_grad = county_sum[:share] - own_coef
-    precinct_grad = county_sum[share:, :LANES].reshape(prec_here) - precinct_coef
-
-    *gathered, county_grad, precinct_grad = lax.optimization_barrier(
-        (*gathered, county_grad, precinct_grad)
-    )
+    state_piece, *county_outs = lax.optimization_barrier((state_piece, *outs[n_row:]))
+    county_parts = [county_outs[0]] + [swap(county_outs[d], "row", d) for d in range(1, n_row)]
+    state_piece = total_of(gather_by(state_piece, "grp", range(1, near)))
+    state_piece = total_of(gather_by(state_piece, "grp", range(near, n_grp, near)))
+    gathered = gather_by(state_piece, "row", range(1, n_row))
+    county_grad, precinct_grad, prior, nation_hot = pl.pallas_call(
+        county_end_kernel,
+        out_shape=[
+            jax.ShapeDtypeStruct((share, p_size), F32),
+            jax.ShapeDtypeStruct((n_hi, LANES), F32),
+            jax.ShapeDtypeStruct((n_states + n_nations + 1, p_size), F32),
+            jax.ShapeDtypeStruct((n_nations, n_states), F32),
+        ],
+        compiler_params=pltpu.CompilerParams(vmem_limit_bytes=END_LIMIT),
+        name="county_totals",
+    )(nation_row, state_coef, nation_coef, beta2, *county_parts)
+
     state_grad, nation_grad, beta_grad = pl.pallas_call(
         end_kernel,
         out_shape=[
@@ -288,10 +342,10 @@
             jax.ShapeDtypeStruct((1, p_size), F32),
         ],
         scratch_shapes=[pltpu.VMEM(state_coef.shape, F32)],
-        compiler_params=pltpu.CompilerParams(vmem_limit_bytes=VMEM_LIMIT),
+        compiler_params=pltpu.CompilerParams(vmem_limit_bytes=END_LIMIT),
         name="upper_totals",
-    )(nation_row, *gathered, state_coef, nation_coef, beta2)
-    return county_grad, precinct_grad, state_grad, nation_grad, beta_grad.reshape(p_size)
+    )(prior, nation_hot, *gathered)
+    return county_grad, precinct_grad.reshape(prec_here), state_grad, nation_grad, beta_grad.reshape(p_size)
 
 
 def solution(mesh):

time: 43.3 us -> 41.9 us (0.968)
  other arithmetic: 3.92 us -> 0.79 us
  waiting for transfers between devices: 9.99 us -> 11.4 us
  Pallas kernels: 12.7 us -> 14.1 us
  local copies, waits for them, and re-layouts: 1.93 us -> 0.92 us
    ppermute x9 -> x13, waiting for transfers between devices: 2.99 us -> 11.4 us  [swap(): return lax.ppermute(x, axis, [(i, i ^ d) for i in range(n)])]
    all_to_all x1 -> x0, waiting for transfers between devices: 6.99 us -> none  [on_device(): lax.all_to_all(copies, 'grp', 0, 0, tiled=True)]
    all_to_all x1 -> x0, starting transfers between devices: 5.81 us -> none  [on_device(): lax.all_to_all(copies, 'grp', 0, 0, tiled=True)]
    ppermute x9 -> x13, starting transfers between devices: 7.18 us -> 12.7 us  [swap(): return lax.ppermute(x, axis, [(i, i ^ d) for i in range(n)])]
    pallas_call x1 -> x2, Pallas kernels: 11 us -> 13.3 us  [the longest x1 12.6 us: on_device(): pl.pallas_call(functools.partial(main_kernel, 2 * n_row), in_specs=[pl.Bl...]
    sub x2 -> x0, other arithmetic: 2.18 us -> none  [the longest x1 1.59 us: on_device(): county_grad = county_sum[:share] - own_coef]
    pallas_call x1, Pallas kernels: 1.73 us -> 0.79 us  [on_device(): pl.pallas_call(end_kernel, out_shape=[jax.ShapeDtypeStruct(state_coef.sha...]
    add x2 -> x3, other arithmetic: 1.72 us -> 0.79 us  [total_of(): parts = [sum(parts[i:i + 2][1:], parts[i]) for i in range(0, len(parts), 2)]]
  transfers between devices with their start and end apart: 10 -> 13, of which waited for: 4 -> 7; matrix products, arithmetic and copies ran while one was open for 11% -> 0% of each run, Pallas kernels for 0% -> 2%
where the time goes in v4:
time: 41.9 us; the launch traced here: 41.2 us
  Pallas kernels  14.1 us (34%)
  starting transfers between devices  12.7 us (30%)
  waiting for transfers between devices  11.4 us (27%)
  between operations  1.41 us (3%)
  local copies, waits for them, and re-layouts  0.92 us (2%)
  other arithmetic  0.79 us (2%)
    ppermute x13, starting transfers between devices, swap(): return lax.ppermute(x, axis, [(i, i ^ d) for i in range(n)])  12.7 us
    pallas_call x1, Pallas kernels, on_device(): pl.pallas_call(functools.partial(main_kernel, 2 * n_row), in_specs=[pl.Bl...  12.6 us
    ppermute x13, waiting for transfers between devices, swap(): return lax.ppermute(x, axis, [(i, i ^ d) for i in range(n)])  11.4 us
    unnamed x10, local copies, waits for them, and re-layouts  0.92 us
  transfers between devices with their start and end apart: 13, of which 7 were waited for; matrix products, arithmetic and copies ran while one was open for 0% of the time, Pallas kernels for 2%

profile of v4, /device:TPU:0, one launch (start us, length us, event | category | flops | bytes accessed | tf_op | source)
XLA Modules:
  0.0 41.2 jit_solution(764001729726427070)
XLA Ops:
  0.6 0.0 copy-start.4
  1.4 12.6 %local_sums.1 = (f32[16,512]{1,0:T(8,128)}, f32[16,512]{1,0:T(8,128)}, f32[16,512]{1,0:T(8,128)}, f32[16,512]{1,0:T(8,128)}, f32[72,512]{1,0:T(8,128)}, /*index=...) custom-call(s32[1,1]{1,0:T(1,128)S(6)} %copy.17.count_ref, bf16[8192,512]{1,0:T(8,128)(2,1)} %features_ref.1, ...), custom_call_target="tpu_custom_call" | custom-call | tf_op jit(solution)/shard_map/local_sums/pallas_call | solution.py:281
  14.0 3.0 %collective-permute-start.1 = (f32[16,512]{1,0:T(8,128)}, f32[16,512]{1,0:T(8,128)S(1)}, u32[]{:S(2)}, u32[]{:S(2)}) collective-permute-start(f32[16,512]{1,0:T(8,128)} %get-tuple-element.27), channel_id=1, source_target_pairs={{0,2},{1,3},{2,0},{3,1},{4,6},{5,7},{6,4},{7,5},{8,10},{9,11},{10,... | collective-permute-start | bytes 98312 | tf_op jit(solution)/shard_map/ppermute | solution.py:222
  17.0 0.0 collective-permute-start.2
  17.0 0.2 collective-permute-start
  17.2 1.9 %collective-permute-done.1 = f32[16,512]{1,0:T(8,128)S(1)} collective-permute-done((f32[16,512]{1,0:T(8,128)}, f32[16,512]{1,0:T(8,128)S(1)}, u32[]{:S(2)}, u32[]{:S(2)}) %collective-permute-start.1) | collective-permute-done | bytes 32800 | tf_op jit(solution)/shard_map/ppermute | solution.py:222
  19.1 1.5 %collective-permute-done.2 = f32[16,512]{1,0:T(8,128)S(1)} collective-permute-done((f32[16,512]{1,0:T(8,128)}, f32[16,512]{1,0:T(8,128)S(1)}, u32[]{:S(2)}, u32[]{:S(2)}) %collective-permute-start.2) | collective-permute-done | bytes 32800 | tf_op jit(solution)/shard_map/ppermute | solution.py:222
  20.6 0.0 collective-permute-done
  20.6 0.8 %add_add_fusion.1 = f32[16,512]{1,0:T(8,128)S(1)} fusion(f32[16,512]{1,0:T(8,128)S(1)} %collective-permute-done.1, f32[16,512]{1,0:T(8,128)S(1)} %collective-permute-done.2, f32[16,512]{1,0:T(8,128)} %get-tuple-element.25, f32[16,512]{1,0:T(8,128)S(1)} %collective-permute-done), kind=kLoop, calls=%fused_computation.1 | loop fusion | flops 24576 | bytes 163840 | tf_op jit(solution)/shard_map/add | solution.py:231
  21.4 1.6 %collective-permute-start.6 = (f32[16,512]{1,0:T(8,128)S(1)}, f32[16,512]{1,0:T(8,128)S(1)}, u32[]{:S(2)}, u32[]{:S(2)}) collective-permute-start(f32[16,512]{1,0:T(8,128)S(1)} %add_add_fusion.1), channel_id=1, source_target_pairs={{0,4},{4,0},{8,12},{12,8},{16,20},{20,16},{24,28},{28,24},{1,5},{5... | collective-permute-start | bytes 98312 | tf_op jit(solution)/shard_map/ppermute | solution.py:222
  23.0 2.4 %collective-permute-done.6 = f32[16,512]{1,0:T(8,128)S(1)} collective-permute-done((f32[16,512]{1,0:T(8,128)S(1)}, f32[16,512]{1,0:T(8,128)S(1)}, u32[]{:S(2)}, u32[]{:S(2)}) %collective-permute-start.6) | collective-permute-done | bytes 32800 | tf_op jit(solution)/shard_map/ppermute | solution.py:222
  25.4 2.6 %collective-permute-start.8 = (f32[16,512]{1,0:T(8,128)S(1)}, f32[16,512]{1,0:T(8,128)S(1)}, u32[]{:S(2)}, u32[]{:S(2)}) collective-permute-start(f32[16,512]{1,0:T(8,128)S(1)} %add.24), channel_id=1, source_target_pairs={{0,16},{4,20},{8,24},{12,28},{16,0},{20,4},{24,8},{28,12},{1,17},{... | collective-permute-start | bytes 98312 | tf_op jit(solution)/shard_map/ppermute | solution.py:222
  28.0 1.4 %collective-permute-start.9 = (f32[16,512]{1,0:T(8,128)S(1)}, f32[16,512]{1,0:T(8,128)S(1)}, u32[]{:S(2)}, u32[]{:S(2)}) collective-permute-start(f32[16,512]{1,0:T(8,128)S(1)} %add.24), channel_id=1, source_target_pairs={{0,24},{4,28},{8,16},{12,20},{16,8},{20,12},{24,0},{28,4},{1,25},{... | collective-permute-start | bytes 98312 | tf_op jit(solution)/shard_map/ppermute | solution.py:222
  29.3 0.2 collective-permute-start.7
  29.6 0.0 collective-permute-start.3
  29.6 0.8 %collective-permute-start.4 = (f32[72,512]{1,0:T(8,128)}, f32[72,512]{1,0:T(8,128)S(1)}, u32[]{:S(2)}, u32[]{:S(2)}) collective-permute-start(f32[72,512]{1,0:T(8,128)} %get-tuple-element.35), channel_id=1, source_target_pairs={{0,2},{1,3},{2,0},{3,1},{4,6},{5,7},{6,4},{7,5},{8,10},{9,11},{10,... | collective-permute-start | bytes 442376 | tf_op jit(solution)/shard_map/ppermute | solution.py:222
  30.3 0.1 collective-permute-done.8
  30.4 1.0 %collective-permute-start.5 = (f32[72,512]{1,0:T(8,128)}, f32[72,512]{1,0:T(8,128)S(1)}, u32[]{:S(2)}, u32[]{:S(2)}) collective-permute-start(f32[72,512]{1,0:T(8,128)} %get-tuple-element.36), channel_id=1, source_target_pairs={{0,3},{1,2},{2,1},{3,0},{4,7},{5,6},{6,5},{7,4},{8,11},{9,10},{10,... | collective-permute-start | bytes 442376 | tf_op jit(solution)/shard_map/ppermute | solution.py:222
  31.4 2.3 %collective-permute-done.9 = f32[16,512]{1,0:T(8,128)S(1)} collective-permute-done((f32[16,512]{1,0:T(8,128)S(1)}, f32[16,512]{1,0:T(8,128)S(1)}, u32[]{:S(2)}, u32[]{:S(2)}) %collective-permute-start.9) | collective-permute-done | bytes 32800 | tf_op jit(solution)/shard_map/ppermute | solution.py:222
  33.7 0.0 collective-permute-done.7
  33.7 0.1 collective-permute-start.10
  33.8 0.9 %collective-permute-start.11 = (f32[16,512]{1,0:T(8,128)S(1)}, f32[16,512]{1,0:T(8,128)S(1)}, u32[]{:S(2)}, u32[]{:S(2)}) collective-permute-start(f32[16,512]{1,0:T(8,128)S(1)} %add_add_fusion.refs_0_), channel_id=1, source_target_pairs={{0,2},{1,3},{2,0},{3,1},{4,6},{5,7},{6,4},{7,5},{8,10},{9,11},{10,... | collective-permute-start | bytes 98312 | tf_op jit(solution)/shard_map/ppermute | solution.py:222
  34.7 0.0 collective-permute-done.3.refs_1_
  34.7 1.0 %collective-permute-start.12 = (f32[16,512]{1,0:T(8,128)S(1)}, f32[16,512]{1,0:T(8,128)S(1)}, u32[]{:S(2)}, u32[]{:S(2)}) collective-permute-start(f32[16,512]{1,0:T(8,128)S(1)} %add_add_fusion.refs_0_), channel_id=1, source_target_pairs={{0,3},{1,2},{2,1},{3,0},{4,7},{5,6},{6,5},{7,4},{8,11},{9,10},{10,... | collective-permute-start | bytes 98312 | tf_op jit(solution)/shard_map/ppermute | solution.py:222
  35.7 0.8 %collective-permute-done.4.refs_2_ = f32[72,512]{1,0:T(8,128)S(1)} collective-permute-done((f32[72,512]{1,0:T(8,128)}, f32[72,512]{1,0:T(8,128)S(1)}, u32[]{:S(2)}, u32[]{:S(2)}) %collective-permute-start.4) | collective-permute-done | bytes 147488 | tf_op jit(solution)/shard_map/ppermute | solution.py:222
  36.4 2.4 %collective-permute-done.5.refs_3_ = f32[72,512]{1,0:T(8,128)S(1)} collective-permute-done((f32[72,512]{1,0:T(8,128)}, f32[72,512]{1,0:T(8,128)S(1)}, u32[]{:S(2)}, u32[]{:S(2)}) %collective-permute-start.5) | collective-permute-done | bytes 147488 | tf_op jit(solution)/shard_map/ppermute | solution.py:222
  38.8 0.9 %copy-done.1 = f32[72,512]{1,0:T(8,128)S(1)} copy-done((f32[72,512]{1,0:T(8,128)S(1)}, f32[72,512]{1,0:T(8,128)}, u32[]{:S(2)}) %copy-start.1) | copy-done | bytes 147480
  39.7 0.7 %county_totals.1 = (f32[64,512]{1,0:T(8,128)}, f32[8,128]{1,0:T(8,128)}, f32[69,512]{1,0:T(8,128)S(1)}, f32[4,64]{1,0:T(4,128)S(1)}) custom-call(s32[1,64]{1,0:T(1,128)S(1)} %bitcast.12, f32[64,512]{1,0:T(8,128)S(1)} %copy-done, f32[4,512]{1,0:T(4,128)S(1)} %copy-done.2, f32[1,512]{1,0:T(1,128)S(1)} %bitcast.10, f32[72,512]{1,0:T(8,128)S(1)} %copy-done.1, ...), custom_call_target="tpu_custom_call" | custom-call | tf_op jit(solution)/shard_map/county_totals/pallas_call | solution.py:325
  40.4 0.0 collective-permute-done.10.refs_1_
  40.4 0.0 collective-permute-done.11.refs_2_
  40.4 0.0 collective-permute-done.12.refs_3_
  40.4 0.8 %upper_totals.1 = (f32[64,512]{1,0:T(8,128)}, f32[4,512]{1,0:T(4,128)}, f32[1,512]{1,0:T(1,128)}) custom-call(f32[69,512]{1,0:T(8,128)S(1)} %get-tuple-element.39.prior_ref, f32[4,64]{1,0:T(4,128)S(1)} %get-tuple-element.40.hot_ref, f32[16,512]{1,0:T(8,128)S(1)} %add_add_fusion.refs_0_, f32[16,512]{1,0:T(8,128)S(1)} %collective-permute-done.10.refs_1_, ...), custom_call_target="tpu_custom_call" | custom-call | tf_op jit(solution)/shard_map/upper_totals/pallas_call | solution.py:337
  (10 shorter events, 0.0 us)
Async XLA Ops:
  0.6 38.2 %copy-start.4 = (s32[64]{0:T(128)S(1)}, s32[64]{0:T(128)}, u32[]{:S(2)}) copy-start(s32[64]{0:T(128)} %param.23) | copy-start | bytes 772
  0.6 38.2 %copy-start = (f32[64,512]{1,0:T(8,128)S(1)}, f32[64,512]{1,0:T(8,128)}, u32[]{:S(2)}) copy-start(f32[64,512]{1,0:T(8,128)} %state_ref.1) | copy-start | bytes 393220
  0.7 38.2 %copy-start.2 = (f32[4,512]{1,0:T(4,128)S(1)}, f32[4,512]{1,0:T(4,128)}, u32[]{:S(2)}) copy-start(f32[4,512]{1,0:T(4,128)} %nation_ref.1) | copy-start | bytes 24580
  0.7 38.2 %copy-start.3 = (f32[512]{0:T(512)S(1)}, f32[512]{0:T(512)}, u32[]{:S(2)}) copy-start(f32[512]{0:T(512)} %param.16) | copy-start | bytes 6148
  14.0 5.1 %collective-permute-start.1 = (f32[16,512]{1,0:T(8,128)}, f32[16,512]{1,0:T(8,128)S(1)}, u32[]{:S(2)}, u32[]{:S(2)}) collective-permute-start(f32[16,512]{1,0:T(8,128)} %get-tuple-element.27), channel_id=1, source_target_pairs={{0,2},{1,3},{2,0},{3,1},{4,6},{5,7},{6,4},{7,5},{8,10},{9,11},{10,... | collective-permute-start | bytes 98312 | tf_op jit(solution)/shard_map/ppermute | solution.py:222
  17.0 3.6 %collective-permute-start.2 = (f32[16,512]{1,0:T(8,128)}, f32[16,512]{1,0:T(8,128)S(1)}, u32[]{:S(2)}, u32[]{:S(2)}) collective-permute-start(f32[16,512]{1,0:T(8,128)} %get-tuple-element.28), channel_id=1, source_target_pairs={{0,3},{1,2},{2,1},{3,0},{4,7},{5,6},{6,5},{7,4},{8,11},{9,10},{10,... | collective-permute-start | bytes 98312 | tf_op jit(solution)/shard_map/ppermute | solution.py:222
  17.0 3.6 %collective-permute-start = (f32[16,512]{1,0:T(8,128)}, f32[16,512]{1,0:T(8,128)S(1)}, u32[]{:S(2)}, u32[]{:S(2)}) collective-permute-start(f32[16,512]{1,0:T(8,128)} %get-tuple-element.26), channel_id=1, source_target_pairs={{0,1},{1,0},{2,3},{3,2},{4,5},{5,4},{6,7},{7,6},{8,9},{9,8},{10,11... | collective-permute-start | bytes 98312 | tf_op jit(solution)/shard_map/ppermute | solution.py:222
  21.4 4.0 %collective-permute-start.6 = (f32[16,512]{1,0:T(8,128)S(1)}, f32[16,512]{1,0:T(8,128)S(1)}, u32[]{:S(2)}, u32[]{:S(2)}) collective-permute-start(f32[16,512]{1,0:T(8,128)S(1)} %add_add_fusion.1), channel_id=1, source_target_pairs={{0,4},{4,0},{8,12},{12,8},{16,20},{20,16},{24,28},{28,24},{1,5},{5... | collective-permute-start | bytes 98312 | tf_op jit(solution)/shard_map/ppermute | solution.py:222
  25.4 5.0 %collective-permute-start.8 = (f32[16,512]{1,0:T(8,128)S(1)}, f32[16,512]{1,0:T(8,128)S(1)}, u32[]{:S(2)}, u32[]{:S(2)}) collective-permute-start(f32[16,512]{1,0:T(8,128)S(1)} %add.24), channel_id=1, source_target_pairs={{0,16},{4,20},{8,24},{12,28},{16,0},{20,4},{24,8},{28,12},{1,17},{... | collective-permute-start | bytes 98312 | tf_op jit(solution)/shard_map/ppermute | solution.py:222
  28.0 5.7 %collective-permute-start.9 = (f32[16,512]{1,0:T(8,128)S(1)}, f32[16,512]{1,0:T(8,128)S(1)}, u32[]{:S(2)}, u32[]{:S(2)}) collective-permute-start(f32[16,512]{1,0:T(8,128)S(1)} %add.24), channel_id=1, source_target_pairs={{0,24},{4,28},{8,16},{12,20},{16,8},{20,12},{24,0},{28,4},{1,25},{... | collective-permute-start | bytes 98312 | tf_op jit(solution)/shard_map/ppermute | solution.py:222
  29.3 4.4 %collective-permute-start.7 = (f32[16,512]{1,0:T(8,128)S(1)}, f32[16,512]{1,0:T(8,128)S(1)}, u32[]{:S(2)}, u32[]{:S(2)}) collective-permute-start(f32[16,512]{1,0:T(8,128)S(1)} %add.24), channel_id=1, source_target_pairs={{0,8},{4,12},{8,0},{12,4},{16,24},{20,28},{24,16},{28,20},{1,9},{5... | collective-permute-start | bytes 98312 | tf_op jit(solution)/shard_map/ppermute | solution.py:222
  29.6 5.1 %collective-permute-start.3 = (f32[72,512]{1,0:T(8,128)}, f32[72,512]{1,0:T(8,128)S(1)}, u32[]{:S(2)}, u32[]{:S(2)}) collective-permute-start(f32[72,512]{1,0:T(8,128)} %get-tuple-element.34), channel_id=1, source_target_pairs={{0,1},{1,0},{2,3},{3,2},{4,5},{5,4},{6,7},{7,6},{8,9},{9,8},{10,11... | collective-permute-start | bytes 442376 | tf_op jit(solution)/shard_map/ppermute | solution.py:222
  29.6 6.9 %collective-permute-start.4 = (f32[72,512]{1,0:T(8,128)}, f32[72,512]{1,0:T(8,128)S(1)}, u32[]{:S(2)}, u32[]{:S(2)}) collective-permute-start(f32[72,512]{1,0:T(8,128)} %get-tuple-element.35), channel_id=1, source_target_pairs={{0,2},{1,3},{2,0},{3,1},{4,6},{5,7},{6,4},{7,5},{8,10},{9,11},{10,... | collective-permute-start | bytes 442376 | tf_op jit(solution)/shard_map/ppermute | solution.py:222
  30.4 8.4 %collective-permute-start.5 = (f32[72,512]{1,0:T(8,128)}, f32[72,512]{1,0:T(8,128)S(1)}, u32[]{:S(2)}, u32[]{:S(2)}) collective-permute-start(f32[72,512]{1,0:T(8,128)} %get-tuple-element.36), channel_id=1, source_target_pairs={{0,3},{1,2},{2,1},{3,0},{4,7},{5,6},{6,5},{7,4},{8,11},{9,10},{10,... | collective-permute-start | bytes 442376 | tf_op jit(solution)/shard_map/ppermute | solution.py:222
  33.7 6.7 %collective-permute-start.10 = (f32[16,512]{1,0:T(8,128)S(1)}, f32[16,512]{1,0:T(8,128)S(1)}, u32[]{:S(2)}, u32[]{:S(2)}) collective-permute-start(f32[16,512]{1,0:T(8,128)S(1)} %add_add_fusion.refs_0_), channel_id=1, source_target_pairs={{0,1},{1,0},{2,3},{3,2},{4,5},{5,4},{6,7},{7,6},{8,9},{9,8},{10,11... | collective-permute-start | bytes 98312 | tf_op jit(solution)/shard_map/ppermute | solution.py:222
  33.8 6.6 %collective-permute-start.11 = (f32[16,512]{1,0:T(8,128)S(1)}, f32[16,512]{1,0:T(8,128)S(1)}, u32[]{:S(2)}, u32[]{:S(2)}) collective-permute-start(f32[16,512]{1,0:T(8,128)S(1)} %add_add_fusion.refs_0_), channel_id=1, source_target_pairs={{0,2},{1,3},{2,0},{3,1},{4,6},{5,7},{6,4},{7,5},{8,10},{9,11},{10,... | collective-permute-start | bytes 98312 | tf_op jit(solution)/shard_map/ppermute | solution.py:222
  34.7 5.8 %collective-permute-start.12 = (f32[16,512]{1,0:T(8,128)S(1)}, f32[16,512]{1,0:T(8,128)S(1)}, u32[]{:S(2)}, u32[]{:S(2)}) collective-permute-start(f32[16,512]{1,0:T(8,128)S(1)} %add_add_fusion.refs_0_), channel_id=1, source_target_pairs={{0,3},{1,2},{2,1},{3,0},{4,7},{5,6},{6,5},{7,4},{8,11},{9,10},{10,... | collective-permute-start | bytes 98312 | tf_op jit(solution)/shard_map/ppermute | solution.py:222
  38.8 0.9 %copy-start.1 = (f32[72,512]{1,0:T(8,128)S(1)}, f32[72,512]{1,0:T(8,128)}, u32[]{:S(2)}) copy-start(f32[72,512]{1,0:T(8,128)} %get-tuple-element.33.refs_0_) | copy-start | bytes 442372

commit v5 on v4

--- a/solution.py
+++ b/solution.py
@@ -87,10 +87,12 @@
     ]
     for copy in small_copies:
         copy.start()
-    for j in range(chunks):
+    for j in range(2):
         fetch(j).start()
     for copy in small_copies:
         copy.wait()
+    for j in range(2, 4):
+        fetch(j).start()
 
     states = county_state_ref[lax.axis_index("grp")]
     state_hot = (iota_rows(n_states) == states).astype(F32).astype(BF16)
@@ -121,7 +123,7 @@
         linear = linear + bases[k][...]
         row = j * size + lax.broadcasted_iota(jnp.int32, (1, size), 1)
         count = outcome_ref[j].astype(F32)
-        residual = jnp.where(row < count_ref[...], count - jnp.exp(linear), 0.0)
+        residual = jnp.where(row < count_ref[0], count - jnp.exp(linear), 0.0)
         residuals[k][...] = residual
         rounded = residual.astype(BF16).astype(F32)
         weights[k][...] = jnp.where(county_hot, rounded, 0.0).astype(BF16)
@@ -147,6 +149,12 @@
         j = 2 * t
         fetch(j).wait()
         fetch(j + 1).wait()
+
+        @pl.when(j + 2 < chunks)
+        def _():
+            fetch(j + 2).start()
+            fetch(j + 3).start()
+
         residue(j - 1, 1)
         score(j, 0)
         collect(j - 2, 0)
@@ -312,16 +320,14 @@
         ],
         compiler_params=pltpu.CompilerParams(vmem_limit_bytes=VMEM_LIMIT),
         name="local_sums",
-    )(row_counts, features, *small)
+    )(row_counts.reshape(1, 1, 1), features, *small)
 
     near = 1 << (n_grp.bit_length() // 2 - 1)
     state_parts = [outs[0]] + [swap(outs[d], "row", d) for d in range(1, n_row)]
     state_piece = total_of(state_parts)
-    state_piece, *county_outs = lax.optimization_barrier((state_piece, *outs[n_row:]))
-    county_parts = [county_outs[0]] + [swap(county_outs[d], "row", d) for d in range(1, n_row)]
+    county_parts = [outs[n_row]] + [swap(outs[n_row + d], "row", d) for d in range(1, n_row)]
     state_piece = total_of(gather_by(state_piece, "grp", range(1, near)))
-    state_piece = total_of(gather_by(state_piece, "grp", range(near, n_grp, near)))
-    gathered = gather_by(state_piece, "row", range(1, n_row))
+    state_piece, *county_parts = lax.optimization_barrier((state_piece, *county_parts))
     county_grad, precinct_grad, prior, nation_hot = pl.pallas_call(
         county_end_kernel,
         out_shape=[
@@ -334,6 +340,8 @@
         name="county_totals",
     )(nation_row, state_coef, nation_coef, beta2, *county_parts)
 
+    state_piece = total_of(gather_by(state_piece, "grp", range(near, n_grp, near)))
+    gathered = gather_by(state_piece, "row", range(1, n_row))
     state_grad, nation_grad, beta_grad = pl.pallas_call(
         end_kernel,
         out_shape=[

time: 41.9 us -> 39 us (0.931)
  Pallas kernels: 14.1 us -> 12.3 us
  waiting for transfers between devices: 11.4 us -> 10.1 us
    pallas_call x1, Pallas kernels: 12.6 us -> 10.9 us  [on_device(): pl.pallas_call(functools.partial(main_kernel, 2 * n_row), in_specs=[pl.Bl...]
    ppermute x13, waiting for transfers between devices: 11.4 us -> 10.1 us  [swap(): return lax.ppermute(x, axis, [(i, i ^ d) for i in range(n)])]
    ppermute x13, starting transfers between devices: 12.7 us -> 13.1 us  [swap(): return lax.ppermute(x, axis, [(i, i ^ d) for i in range(n)])]
  transfers between devices with their start and end apart: 13 -> 13, of which waited for: 7 -> 6; matrix products, arithmetic and copies ran while one was open for 0% -> 2% of each run, Pallas kernels for 2% -> 2%
where the time goes in v5:
time: 39 us; the launch traced here: 38.7 us
  starting transfers between devices  13.1 us (34%)
  Pallas kernels  12.3 us (32%)
  waiting for transfers between devices  10.1 us (26%)
  between operations  1.45 us (4%)
  local copies, waits for them, and re-layouts  0.92 us (2%)
  other arithmetic  0.79 us (2%)
    ppermute x13, starting transfers between devices, swap(): return lax.ppermute(x, axis, [(i, i ^ d) for i in range(n)])  13.1 us
    pallas_call x1, Pallas kernels, on_device(): pl.pallas_call(functools.partial(main_kernel, 2 * n_row), in_specs=[pl.Bl...  10.9 us
    ppermute x13, waiting for transfers between devices, swap(): return lax.ppermute(x, axis, [(i, i ^ d) for i in range(n)])  10.1 us
    unnamed x10, local copies, waits for them, and re-layouts  0.92 us
    add x3, other arithmetic, total_of(): parts = [sum(parts[i:i + 2][1:], parts[i]) for i in range(0, len(parts), 2)]  0.79 us
    pallas_call x1, Pallas kernels, on_device(): pl.pallas_call(end_kernel, out_shape=[jax.ShapeDtypeStruct(state_coef.sha...  0.78 us
  transfers between devices with their start and end apart: 13, of which 6 were waited for; matrix products, arithmetic and copies ran while one was open for 2% of the time, Pallas kernels for 2%

profile of v5, /device:TPU:0, one launch (start us, length us, event | category | flops | bytes accessed | tf_op | source)
XLA Modules:
  0.0 38.7 jit_solution(15121870114601210842)
XLA Ops:
  1.4 10.9 %local_sums.1 = (f32[16,512]{1,0:T(8,128)}, f32[16,512]{1,0:T(8,128)}, f32[16,512]{1,0:T(8,128)}, f32[16,512]{1,0:T(8,128)}, f32[72,512]{1,0:T(8,128)}, /*index=...) custom-call(s32[1,1,1]{2,1,0:T(1,128)} %bitcast.10.count_ref, bf16[8192,512]{1,0:T(8,128)(2,1)} %features_ref.1, ...), custom_call_target="tpu_custom_call" | custom-call | tf_op jit(solution)/shard_map/local_sums/pallas_call | solution.py:289
  12.3 0.5 %collective-permute-start = (f32[16,512]{1,0:T(8,128)}, f32[16,512]{1,0:T(8,128)S(1)}, u32[]{:S(2)}, u32[]{:S(2)}) collective-permute-start(f32[16,512]{1,0:T(8,128)} %get-tuple-element.26), channel_id=1, source_target_pairs={{0,1},{1,0},{2,3},{3,2},{4,5},{5,4},{6,7},{7,6},{8,9},{9,8},{10,11... | collective-permute-start | bytes 98312 | tf_op jit(solution)/shard_map/ppermute | solution.py:230
  12.8 2.6 %collective-permute-start.1 = (f32[16,512]{1,0:T(8,128)}, f32[16,512]{1,0:T(8,128)S(1)}, u32[]{:S(2)}, u32[]{:S(2)}) collective-permute-start(f32[16,512]{1,0:T(8,128)} %get-tuple-element.27), channel_id=1, source_target_pairs={{0,2},{1,3},{2,0},{3,1},{4,6},{5,7},{6,4},{7,5},{8,10},{9,11},{10,... | collective-permute-start | bytes 98312 | tf_op jit(solution)/shard_map/ppermute | solution.py:230
  15.4 0.1 collective-permute-start.2
  15.5 0.1 collective-permute-start.4
  15.6 1.9 %collective-permute-start.5 = (f32[72,512]{1,0:T(8,128)}, f32[72,512]{1,0:T(8,128)S(1)}, u32[]{:S(2)}, u32[]{:S(2)}) collective-permute-start(f32[72,512]{1,0:T(8,128)} %get-tuple-element.31), channel_id=1, source_target_pairs={{0,2},{1,3},{2,0},{3,1},{4,6},{5,7},{6,4},{7,5},{8,10},{9,11},{10,... | collective-permute-start | bytes 442376 | tf_op jit(solution)/shard_map/ppermute | solution.py:230
  17.5 0.0 collective-permute-done
  17.5 0.0 collective-permute-start.6
  17.5 0.0 collective-permute-done.1
  17.6 1.4 %collective-permute-done.2 = f32[16,512]{1,0:T(8,128)S(1)} collective-permute-done((f32[16,512]{1,0:T(8,128)}, f32[16,512]{1,0:T(8,128)S(1)}, u32[]{:S(2)}, u32[]{:S(2)}) %collective-permute-start.2) | collective-permute-done | bytes 32800 | tf_op jit(solution)/shard_map/ppermute | solution.py:230
  18.9 0.8 %add_add_fusion.1 = f32[16,512]{1,0:T(8,128)S(1)} fusion(f32[16,512]{1,0:T(8,128)S(1)} %collective-permute-done.1, f32[16,512]{1,0:T(8,128)S(1)} %collective-permute-done.2, f32[16,512]{1,0:T(8,128)} %get-tuple-element.25, f32[16,512]{1,0:T(8,128)S(1)} %collective-permute-done), kind=kLoop, calls=%fused_computation.1 | loop fusion | flops 24576 | bytes 163840 | tf_op jit(solution)/shard_map/add | solution.py:239
  19.7 1.6 %collective-permute-start.3 = (f32[16,512]{1,0:T(8,128)S(1)}, f32[16,512]{1,0:T(8,128)S(1)}, u32[]{:S(2)}, u32[]{:S(2)}) collective-permute-start(f32[16,512]{1,0:T(8,128)S(1)} %add_add_fusion.1), channel_id=1, source_target_pairs={{0,4},{4,0},{8,12},{12,8},{16,20},{20,16},{24,28},{28,24},{1,5},{5... | collective-permute-start | bytes 98312 | tf_op jit(solution)/shard_map/ppermute | solution.py:230
  21.3 2.4 %collective-permute-done.3 = f32[16,512]{1,0:T(8,128)S(1)} collective-permute-done((f32[16,512]{1,0:T(8,128)S(1)}, f32[16,512]{1,0:T(8,128)S(1)}, u32[]{:S(2)}, u32[]{:S(2)}) %collective-permute-start.3) | collective-permute-done | bytes 32800 | tf_op jit(solution)/shard_map/ppermute | solution.py:230
  23.7 0.0 collective-permute-done.4.refs_1_
  23.7 0.0 collective-permute-done.5.refs_2_
  23.7 1.6 %collective-permute-done.6.refs_3_ = f32[72,512]{1,0:T(8,128)S(1)} collective-permute-done((f32[72,512]{1,0:T(8,128)}, f32[72,512]{1,0:T(8,128)S(1)}, u32[]{:S(2)}, u32[]{:S(2)}) %collective-permute-start.6) | collective-permute-done | bytes 147488 | tf_op jit(solution)/shard_map/ppermute | solution.py:230
  25.3 3.4 %collective-permute-start.9 = (f32[16,512]{1,0:T(8,128)S(1)}, f32[16,512]{1,0:T(8,128)S(1)}, u32[]{:S(2)}, u32[]{:S(2)}) collective-permute-start(f32[16,512]{1,0:T(8,128)S(1)} %add.24), channel_id=1, source_target_pairs={{0,24},{4,28},{8,16},{12,20},{16,8},{20,12},{24,0},{28,4},{1,25},{... | collective-permute-start | bytes 98312 | tf_op jit(solution)/shard_map/ppermute | solution.py:230
  28.7 0.0 collective-permute-start.8
  28.7 1.0 %collective-permute-start.7 = (f32[16,512]{1,0:T(8,128)S(1)}, f32[16,512]{1,0:T(8,128)S(1)}, u32[]{:S(2)}, u32[]{:S(2)}) collective-permute-start(f32[16,512]{1,0:T(8,128)S(1)} %add.24), channel_id=1, source_target_pairs={{0,8},{4,12},{8,0},{12,4},{16,24},{20,28},{24,16},{28,20},{1,9},{5... | collective-permute-start | bytes 98312 | tf_op jit(solution)/shard_map/ppermute | solution.py:230
  29.7 1.3 %collective-permute-done.9 = f32[16,512]{1,0:T(8,128)S(1)} collective-permute-done((f32[16,512]{1,0:T(8,128)S(1)}, f32[16,512]{1,0:T(8,128)S(1)}, u32[]{:S(2)}, u32[]{:S(2)}) %collective-permute-start.9) | collective-permute-done | bytes 32800 | tf_op jit(solution)/shard_map/ppermute | solution.py:230
  31.1 2.5 %collective-permute-done.8 = f32[16,512]{1,0:T(8,128)S(1)} collective-permute-done((f32[16,512]{1,0:T(8,128)S(1)}, f32[16,512]{1,0:T(8,128)S(1)}, u32[]{:S(2)}, u32[]{:S(2)}) %collective-permute-start.8) | collective-permute-done | bytes 32800 | tf_op jit(solution)/shard_map/ppermute | solution.py:230
  33.5 0.0 collective-permute-done.7
  33.6 0.1 collective-permute-start.12
  33.6 1.0 %collective-permute-start.11 = (f32[16,512]{1,0:T(8,128)S(1)}, f32[16,512]{1,0:T(8,128)S(1)}, u32[]{:S(2)}, u32[]{:S(2)}) collective-permute-start(f32[16,512]{1,0:T(8,128)S(1)} %add_add_fusion.refs_0_), channel_id=1, source_target_pairs={{0,2},{1,3},{2,0},{3,1},{4,6},{5,7},{6,4},{7,5},{8,10},{9,11},{10,... | collective-permute-start | bytes 98312 | tf_op jit(solution)/shard_map/ppermute | solution.py:230
  34.6 0.9 %collective-permute-start.10 = (f32[16,512]{1,0:T(8,128)S(1)}, f32[16,512]{1,0:T(8,128)S(1)}, u32[]{:S(2)}, u32[]{:S(2)}) collective-permute-start(f32[16,512]{1,0:T(8,128)S(1)} %add_add_fusion.refs_0_), channel_id=1, source_target_pairs={{0,1},{1,0},{2,3},{3,2},{4,5},{5,4},{6,7},{7,6},{8,9},{9,8},{10,11... | collective-permute-start | bytes 98312 | tf_op jit(solution)/shard_map/ppermute | solution.py:230
  35.5 0.0 copy-done
  35.5 0.9 %copy-done.1 = f32[72,512]{1,0:T(8,128)S(1)} copy-done((f32[72,512]{1,0:T(8,128)S(1)}, f32[72,512]{1,0:T(8,128)}, u32[]{:S(2)}) %copy-start.1) | copy-done | bytes 147480
  36.4 0.7 %county_totals.1 = (f32[64,512]{1,0:T(8,128)}, f32[8,128]{1,0:T(8,128)}, f32[69,512]{1,0:T(8,128)S(1)}, f32[4,64]{1,0:T(4,128)S(1)}) custom-call(s32[1,64]{1,0:T(1,128)S(1)} %bitcast.14, f32[64,512]{1,0:T(8,128)S(1)} %copy-done, f32[4,512]{1,0:T(4,128)S(1)} %copy-done.2, f32[1,512]{1,0:T(1,128)S(1)} %bitcast.12, f32[72,512]{1,0:T(8,128)S(1)} %copy-done.1, ...), custom_call_target="tpu_custom_call" | custom-call | tf_op jit(solution)/shard_map/county_totals/pallas_call | solution.py:331
  37.1 0.0 collective-permute-done.12.refs_3_
  37.1 0.8 %collective-permute-done.11.refs_2_ = f32[16,512]{1,0:T(8,128)S(1)} collective-permute-done((f32[16,512]{1,0:T(8,128)S(1)}, f32[16,512]{1,0:T(8,128)S(1)}, u32[]{:S(2)}, u32[]{:S(2)}) %collective-permute-start.11) | collective-permute-done | bytes 32800 | tf_op jit(solution)/shard_map/ppermute | solution.py:230
  37.9 0.0 collective-permute-done.10.refs_1_
  38.0 0.8 %upper_totals.1 = (f32[64,512]{1,0:T(8,128)}, f32[4,512]{1,0:T(4,128)}, f32[1,512]{1,0:T(1,128)}) custom-call(f32[69,512]{1,0:T(8,128)S(1)} %get-tuple-element.39.prior_ref, f32[4,64]{1,0:T(4,128)S(1)} %get-tuple-element.40.hot_ref, f32[16,512]{1,0:T(8,128)S(1)} %add_add_fusion.refs_0_, f32[16,512]{1,0:T(8,128)S(1)} %collective-permute-done.10.refs_1_, ...), custom_call_target="tpu_custom_call" | custom-call | tf_op jit(solution)/shard_map/upper_totals/pallas_call | solution.py:345
  (10 shorter events, 0.0 us)
Async XLA Ops:
  0.6 34.9 %copy-start = (f32[64,512]{1,0:T(8,128)S(1)}, f32[64,512]{1,0:T(8,128)}, u32[]{:S(2)}) copy-start(f32[64,512]{1,0:T(8,128)} %state_ref.1) | copy-start | bytes 393220
  0.6 34.8 %copy-start.2 = (f32[4,512]{1,0:T(4,128)S(1)}, f32[4,512]{1,0:T(4,128)}, u32[]{:S(2)}) copy-start(f32[4,512]{1,0:T(4,128)} %nation_ref.1) | copy-start | bytes 24580
  0.7 34.8 %copy-start.4 = (s32[64]{0:T(128)S(1)}, s32[64]{0:T(128)}, u32[]{:S(2)}) copy-start(s32[64]{0:T(128)} %param.23) | copy-start | bytes 772
  0.7 34.8 %copy-start.3 = (f32[512]{0:T(512)S(1)}, f32[512]{0:T(512)}, u32[]{:S(2)}) copy-start(f32[512]{0:T(512)} %param.16) | copy-start | bytes 6148
  12.3 5.3 %collective-permute-start = (f32[16,512]{1,0:T(8,128)}, f32[16,512]{1,0:T(8,128)S(1)}, u32[]{:S(2)}, u32[]{:S(2)}) collective-permute-start(f32[16,512]{1,0:T(8,128)} %get-tuple-element.26), channel_id=1, source_target_pairs={{0,1},{1,0},{2,3},{3,2},{4,5},{5,4},{6,7},{7,6},{8,9},{9,8},{10,11... | collective-permute-start | bytes 98312 | tf_op jit(solution)/shard_map/ppermute | solution.py:230
  12.8 4.8 %collective-permute-start.1 = (f32[16,512]{1,0:T(8,128)}, f32[16,512]{1,0:T(8,128)S(1)}, u32[]{:S(2)}, u32[]{:S(2)}) collective-permute-start(f32[16,512]{1,0:T(8,128)} %get-tuple-element.27), channel_id=1, source_target_pairs={{0,2},{1,3},{2,0},{3,1},{4,6},{5,7},{6,4},{7,5},{8,10},{9,11},{10,... | collective-permute-start | bytes 98312 | tf_op jit(solution)/shard_map/ppermute | solution.py:230
  15.4 3.6 %collective-permute-start.2 = (f32[16,512]{1,0:T(8,128)}, f32[16,512]{1,0:T(8,128)S(1)}, u32[]{:S(2)}, u32[]{:S(2)}) collective-permute-start(f32[16,512]{1,0:T(8,128)} %get-tuple-element.28), channel_id=1, source_target_pairs={{0,3},{1,2},{2,1},{3,0},{4,7},{5,6},{6,5},{7,4},{8,11},{9,10},{10,... | collective-permute-start | bytes 98312 | tf_op jit(solution)/shard_map/ppermute | solution.py:230
  15.5 8.2 %collective-permute-start.4 = (f32[72,512]{1,0:T(8,128)}, f32[72,512]{1,0:T(8,128)S(1)}, u32[]{:S(2)}, u32[]{:S(2)}) collective-permute-start(f32[72,512]{1,0:T(8,128)} %get-tuple-element.30), channel_id=1, source_target_pairs={{0,1},{1,0},{2,3},{3,2},{4,5},{5,4},{6,7},{7,6},{8,9},{9,8},{10,11... | collective-permute-start | bytes 442376 | tf_op jit(solution)/shard_map/ppermute | solution.py:230
  15.6 8.1 %collective-permute-start.5 = (f32[72,512]{1,0:T(8,128)}, f32[72,512]{1,0:T(8,128)S(1)}, u32[]{:S(2)}, u32[]{:S(2)}) collective-permute-start(f32[72,512]{1,0:T(8,128)} %get-tuple-element.31), channel_id=1, source_target_pairs={{0,2},{1,3},{2,0},{3,1},{4,6},{5,7},{6,4},{7,5},{8,10},{9,11},{10,... | collective-permute-start | bytes 442376 | tf_op jit(solution)/shard_map/ppermute | solution.py:230
  17.5 7.8 %collective-permute-start.6 = (f32[72,512]{1,0:T(8,128)}, f32[72,512]{1,0:T(8,128)S(1)}, u32[]{:S(2)}, u32[]{:S(2)}) collective-permute-start(f32[72,512]{1,0:T(8,128)} %get-tuple-element.32), channel_id=1, source_target_pairs={{0,3},{1,2},{2,1},{3,0},{4,7},{5,6},{6,5},{7,4},{8,11},{9,10},{10,... | collective-permute-start | bytes 442376 | tf_op jit(solution)/shard_map/ppermute | solution.py:230
  19.7 4.0 %collective-permute-start.3 = (f32[16,512]{1,0:T(8,128)S(1)}, f32[16,512]{1,0:T(8,128)S(1)}, u32[]{:S(2)}, u32[]{:S(2)}) collective-permute-start(f32[16,512]{1,0:T(8,128)S(1)} %add_add_fusion.1), channel_id=1, source_target_pairs={{0,4},{4,0},{8,12},{12,8},{16,20},{20,16},{24,28},{28,24},{1,5},{5... | collective-permute-start | bytes 98312 | tf_op jit(solution)/shard_map/ppermute | solution.py:230
  25.3 5.7 %collective-permute-start.9 = (f32[16,512]{1,0:T(8,128)S(1)}, f32[16,512]{1,0:T(8,128)S(1)}, u32[]{:S(2)}, u32[]{:S(2)}) collective-permute-start(f32[16,512]{1,0:T(8,128)S(1)} %add.24), channel_id=1, source_target_pairs={{0,24},{4,28},{8,16},{12,20},{16,8},{20,12},{24,0},{28,4},{1,25},{... | collective-permute-start | bytes 98312 | tf_op jit(solution)/shard_map/ppermute | solution.py:230
  28.7 4.8 %collective-permute-start.8 = (f32[16,512]{1,0:T(8,128)S(1)}, f32[16,512]{1,0:T(8,128)S(1)}, u32[]{:S(2)}, u32[]{:S(2)}) collective-permute-start(f32[16,512]{1,0:T(8,128)S(1)} %add.24), channel_id=1, source_target_pairs={{0,16},{4,20},{8,24},{12,28},{16,0},{20,4},{24,8},{28,12},{1,17},{... | collective-permute-start | bytes 98312 | tf_op jit(solution)/shard_map/ppermute | solution.py:230
  28.7 4.8 %collective-permute-start.7 = (f32[16,512]{1,0:T(8,128)S(1)}, f32[16,512]{1,0:T(8,128)S(1)}, u32[]{:S(2)}, u32[]{:S(2)}) collective-permute-start(f32[16,512]{1,0:T(8,128)S(1)} %add.24), channel_id=1, source_target_pairs={{0,8},{4,12},{8,0},{12,4},{16,24},{20,28},{24,16},{28,20},{1,9},{5... | collective-permute-start | bytes 98312 | tf_op jit(solution)/shard_map/ppermute | solution.py:230
  33.6 3.6 %collective-permute-start.12 = (f32[16,512]{1,0:T(8,128)S(1)}, f32[16,512]{1,0:T(8,128)S(1)}, u32[]{:S(2)}, u32[]{:S(2)}) collective-permute-start(f32[16,512]{1,0:T(8,128)S(1)} %add_add_fusion.refs_0_), channel_id=1, source_target_pairs={{0,3},{1,2},{2,1},{3,0},{4,7},{5,6},{6,5},{7,4},{8,11},{9,10},{10,... | collective-permute-start | bytes 98312 | tf_op jit(solution)/shard_map/ppermute | solution.py:230
  33.6 4.3 %collective-permute-start.11 = (f32[16,512]{1,0:T(8,128)S(1)}, f32[16,512]{1,0:T(8,128)S(1)}, u32[]{:S(2)}, u32[]{:S(2)}) collective-permute-start(f32[16,512]{1,0:T(8,128)S(1)} %add_add_fusion.refs_0_), channel_id=1, source_target_pairs={{0,2},{1,3},{2,0},{3,1},{4,6},{5,7},{6,4},{7,5},{8,10},{9,11},{10,... | collective-permute-start | bytes 98312 | tf_op jit(solution)/shard_map/ppermute | solution.py:230
  34.6 3.3 %collective-permute-start.10 = (f32[16,512]{1,0:T(8,128)S(1)}, f32[16,512]{1,0:T(8,128)S(1)}, u32[]{:S(2)}, u32[]{:S(2)}) collective-permute-start(f32[16,512]{1,0:T(8,128)S(1)} %add_add_fusion.refs_0_), channel_id=1, source_target_pairs={{0,1},{1,0},{2,3},{3,2},{4,5},{5,4},{6,7},{7,6},{8,9},{9,8},{10,11... | collective-permute-start | bytes 98312 | tf_op jit(solution)/shard_map/ppermute | solution.py:230
  35.5 0.9 %copy-start.1 = (f32[72,512]{1,0:T(8,128)S(1)}, f32[72,512]{1,0:T(8,128)}, u32[]{:S(2)}) copy-start(f32[72,512]{1,0:T(8,128)} %get-tuple-element.33.refs_0_) | copy-start | bytes 442372

commit v6 on v5

--- a/solution.py
+++ b/solution.py
@@ -8,7 +8,7 @@
 from jax.sharding import PartitionSpec as P
 
 LANES = 128
-ROW_STEP = 1024
+ROW_STEP = 512
 SMALL = 10
 VMEM_LIMIT = 60 * 1024 * 1024
 END_LIMIT = 16 * 1024 * 1024
@@ -34,6 +34,11 @@
 
 def iota_rows(n):
     return lax.broadcasted_iota(jnp.int32, (n, 1), 0)
+
+
+def small_hot(n, ids, value):
+    rows = lax.broadcasted_iota(jnp.int32, (n, ids.shape[1]), 0).astype(F32).astype(BF16)
+    return jnp.where(rows == ids.astype(F32).astype(BF16), value.astype(BF16), jnp.zeros((), BF16))
 
 
 def pick(values, low, high_hot):
@@ -125,13 +130,12 @@
         count = outcome_ref[j].astype(F32)
         residual = jnp.where(row < count_ref[0], count - jnp.exp(linear), 0.0)
         residuals[k][...] = residual
-        rounded = residual.astype(BF16).astype(F32)
-        weights[k][...] = jnp.where(county_hot, rounded, 0.0).astype(BF16)
+        weights[k][...] = small_hot(n_cnt, hot_rows[k][...], residual)
 
     def collect(j, k):
         county_acc[...] += jnp.dot(weights[k][...], block(j), preferred_element_type=F32)
         low, high_hot = parts_of(j)
-        low_hot = (iota_rows(LANES) == low).astype(F32).astype(BF16)
+        low_hot = small_hot(LANES, low, jnp.ones((), F32))
         by_high = jnp.concatenate(
             [jnp.where(high_hot, x.astype(F32), 0.0) for x in split3(residuals[k][...])[:2]], axis=0
         ).astype(BF16)
@@ -325,9 +329,14 @@
     near = 1 << (n_grp.bit_length() // 2 - 1)
     state_parts = [outs[0]] + [swap(outs[d], "row", d) for d in range(1, n_row)]
     state_piece = total_of(state_parts)
-    county_parts = [outs[n_row]] + [swap(outs[n_row + d], "row", d) for d in range(1, n_row)]
+    county_outs = outs[n_row:]
+    from_core = [swap(county_outs[d ^ 1], "row", 1) for d in range(0, n_row, 2)]
+    state_piece, *from_core = lax.optimization_barrier((state_piece, *from_core))
+    chip_sums = [county_outs[d] + from_core[d // 2] for d in range(2, n_row, 2)]
+    county_parts = [county_outs[0], from_core[0]] + [
+        swap(x, "row", d) for x, d in zip(chip_sums, range(2, n_row, 2))
+    ]
     state_piece = total_of(gather_by(state_piece, "grp", range(1, near)))
-    state_piece, *county_parts = lax.optimization_barrier((state_piece, *county_parts))
     county_grad, precinct_grad, prior, nation_hot = pl.pallas_call(
         county_end_kernel,
         out_shape=[

time: 39 us -> 39.4 us (1.010)
  Pallas kernels: 12.3 us -> 14 us
  waiting for transfers between devices: 10.1 us -> 8.74 us
  other arithmetic: 0.79 us -> 1.72 us
  starting transfers between devices: 13.1 us -> 12.2 us
    pallas_call x1, Pallas kernels: 10.9 us -> 12.5 us  [on_device(): pl.pallas_call(functools.partial(main_kernel, 2 * n_row), in_specs=[pl.Bl...]
    ppermute x13, waiting for transfers between devices: 10.1 us -> 8.74 us  [swap(): return lax.ppermute(x, axis, [(i, i ^ d) for i in range(n)])]
    add x0 -> x1, other arithmetic: none -> 0.93 us  [on_device(): chip_sums = [county_outs[d] + from_core[d // 2] for d in range(2, n_row, 2)]]
    ppermute x13, starting transfers between devices: 13.1 us -> 12.2 us  [swap(): return lax.ppermute(x, axis, [(i, i ^ d) for i in range(n)])]
  transfers between devices with their start and end apart: 13 -> 13, of which waited for: 6 -> 7; matrix products, arithmetic and copies ran while one was open for 2% -> 4% of each run, Pallas kernels for 2% -> 2%
where the time goes in v6:
time: 39.4 us; the launch traced here: 39 us
  Pallas kernels  14 us (36%)
  starting transfers between devices  12.2 us (31%)
  waiting for transfers between devices  8.74 us (22%)
  other arithmetic  1.72 us (4%)
  between operations  1.42 us (4%)
  local copies, waits for them, and re-layouts  0.92 us (2%)
    pallas_call x1, Pallas kernels, on_device(): pl.pallas_call(functools.partial(main_kernel, 2 * n_row), in_specs=[pl.Bl...  12.5 us
    ppermute x13, starting transfers between devices, swap(): return lax.ppermute(x, axis, [(i, i ^ d) for i in range(n)])  12.2 us
    ppermute x13, waiting for transfers between devices, swap(): return lax.ppermute(x, axis, [(i, i ^ d) for i in range(n)])  8.74 us
    add x1, other arithmetic, on_device(): chip_sums = [county_outs[d] + from_core[d // 2] for d in range(2, n_row, 2)]  0.93 us
    unnamed x10, local copies, waits for them, and re-layouts  0.92 us
    add x3, other arithmetic, total_of(): parts = [sum(parts[i:i + 2][1:], parts[i]) for i in range(0, len(parts), 2)]  0.79 us
  transfers between devices with their start and end apart: 13, of which 7 were waited for; matrix products, arithmetic and copies ran while one was open for 4% of the time, Pallas kernels for 2%

profile of v6, /device:TPU:0, one launch (start us, length us, event | category | flops | bytes accessed | tf_op | source)
XLA Modules:
  0.0 39.0 jit_solution(3841950435333868554)
XLA Ops:
  1.4 12.5 %local_sums.1 = (f32[16,512]{1,0:T(8,128)}, f32[16,512]{1,0:T(8,128)}, f32[16,512]{1,0:T(8,128)}, f32[16,512]{1,0:T(8,128)}, f32[72,512]{1,0:T(8,128)}, /*index=...) custom-call(s32[1,1,1]{2,1,0:T(1,128)} %bitcast.10.count_ref, bf16[8192,512]{1,0:T(8,128)(2,1)} %features_ref.1, ...), custom_call_target="tpu_custom_call" | custom-call | tf_op jit(solution)/shard_map/local_sums/pallas_call | solution.py:293
  13.9 3.0 %collective-permute-start.1 = (f32[16,512]{1,0:T(8,128)}, f32[16,512]{1,0:T(8,128)S(1)}, u32[]{:S(2)}, u32[]{:S(2)}) collective-permute-start(f32[16,512]{1,0:T(8,128)} %get-tuple-element.26), channel_id=1, source_target_pairs={{0,2},{1,3},{2,0},{3,1},{4,6},{5,7},{6,4},{7,5},{8,10},{9,11},{10,... | collective-permute-start | bytes 98312 | tf_op jit(solution)/shard_map/ppermute | solution.py:234
  16.9 0.0 collective-permute-start.2
  16.9 0.2 collective-permute-start
  17.1 0.3 collective-permute-start.3
  17.4 0.2 collective-permute-start.4
  17.6 1.4 %collective-permute-done.1 = f32[16,512]{1,0:T(8,128)S(1)} collective-permute-done((f32[16,512]{1,0:T(8,128)}, f32[16,512]{1,0:T(8,128)S(1)}, u32[]{:S(2)}, u32[]{:S(2)}) %collective-permute-start.1) | collective-permute-done | bytes 32800 | tf_op jit(solution)/shard_map/ppermute | solution.py:234
  19.0 1.5 %collective-permute-done.2 = f32[16,512]{1,0:T(8,128)S(1)} collective-permute-done((f32[16,512]{1,0:T(8,128)}, f32[16,512]{1,0:T(8,128)S(1)}, u32[]{:S(2)}, u32[]{:S(2)}) %collective-permute-start.2) | collective-permute-done | bytes 32800 | tf_op jit(solution)/shard_map/ppermute | solution.py:234
  20.6 0.0 collective-permute-done
  20.6 0.8 %add_add_fusion.1 = f32[16,512]{1,0:T(8,128)S(1)} fusion(f32[16,512]{1,0:T(8,128)S(1)} %collective-permute-done.1, f32[16,512]{1,0:T(8,128)S(1)} %collective-permute-done.2, f32[16,512]{1,0:T(8,128)} %get-tuple-element.24, f32[16,512]{1,0:T(8,128)S(1)} %collective-permute-done), kind=kLoop, calls=%fused_computation.1 | loop fusion | flops 24576 | bytes 163840 | tf_op jit(solution)/shard_map/add | solution.py:243
  21.3 0.0 collective-permute-done.3.refs_1_
  21.4 0.0 collective-permute-done.4
  21.4 1.6 %collective-permute-start.6 = (f32[16,512]{1,0:T(8,128)S(1)}, f32[16,512]{1,0:T(8,128)S(1)}, u32[]{:S(2)}, u32[]{:S(2)}) collective-permute-start(f32[16,512]{1,0:T(8,128)S(1)} %add_add_fusion.1), channel_id=1, source_target_pairs={{0,4},{4,0},{8,12},{12,8},{16,20},{20,16},{24,28},{28,24},{1,5},{5... | collective-permute-start | bytes 98312 | tf_op jit(solution)/shard_map/ppermute | solution.py:234
  22.9 2.4 %collective-permute-done.6 = f32[16,512]{1,0:T(8,128)S(1)} collective-permute-done((f32[16,512]{1,0:T(8,128)S(1)}, f32[16,512]{1,0:T(8,128)S(1)}, u32[]{:S(2)}, u32[]{:S(2)}) %collective-permute-start.6) | collective-permute-done | bytes 32800 | tf_op jit(solution)/shard_map/ppermute | solution.py:234
  25.4 2.6 %collective-permute-start.8 = (f32[16,512]{1,0:T(8,128)S(1)}, f32[16,512]{1,0:T(8,128)S(1)}, u32[]{:S(2)}, u32[]{:S(2)}) collective-permute-start(f32[16,512]{1,0:T(8,128)S(1)} %add.28), channel_id=1, source_target_pairs={{0,16},{4,20},{8,24},{12,28},{16,0},{20,4},{24,8},{28,12},{1,17},{... | collective-permute-start | bytes 98312 | tf_op jit(solution)/shard_map/ppermute | solution.py:234
  27.9 1.3 %collective-permute-start.9 = (f32[16,512]{1,0:T(8,128)S(1)}, f32[16,512]{1,0:T(8,128)S(1)}, u32[]{:S(2)}, u32[]{:S(2)}) collective-permute-start(f32[16,512]{1,0:T(8,128)S(1)} %add.28), channel_id=1, source_target_pairs={{0,24},{4,28},{8,16},{12,20},{16,8},{20,12},{24,0},{28,4},{1,25},{... | collective-permute-start | bytes 98312 | tf_op jit(solution)/shard_map/ppermute | solution.py:234
  29.3 0.2 collective-permute-start.7
  29.5 0.9 %add.27 = f32[72,512]{1,0:T(8,128)S(1)} add(f32[72,512]{1,0:T(8,128)} %get-tuple-element.31, f32[72,512]{1,0:T(8,128)S(1)} %collective-permute-done.4) | non-fusion elementwise | flops 36864 | bytes 442368 | tf_op jit(solution)/shard_map/add | solution.py:335
  30.5 0.8 %collective-permute-start.5 = (f32[72,512]{1,0:T(8,128)S(1)}, f32[72,512]{1,0:T(8,128)S(1)}, u32[]{:S(2)}, u32[]{:S(2)}) collective-permute-start(f32[72,512]{1,0:T(8,128)S(1)} %add.27), channel_id=1, source_target_pairs={{0,2},{1,3},{2,0},{3,1},{4,6},{5,7},{6,4},{7,5},{8,10},{9,11},{10,... | collective-permute-start | bytes 442376 | tf_op jit(solution)/shard_map/ppermute | solution.py:234
  31.3 0.0 collective-permute-done.8
  31.3 2.4 %collective-permute-done.9 = f32[16,512]{1,0:T(8,128)S(1)} collective-permute-done((f32[16,512]{1,0:T(8,128)S(1)}, f32[16,512]{1,0:T(8,128)S(1)}, u32[]{:S(2)}, u32[]{:S(2)}) %collective-permute-start.9) | collective-permute-done | bytes 32800 | tf_op jit(solution)/shard_map/ppermute | solution.py:234
  33.7 0.0 collective-permute-done.7
  33.7 0.1 collective-permute-start.10
  33.7 0.8 %collective-permute-start.11 = (f32[16,512]{1,0:T(8,128)S(1)}, f32[16,512]{1,0:T(8,128)S(1)}, u32[]{:S(2)}, u32[]{:S(2)}) collective-permute-start(f32[16,512]{1,0:T(8,128)S(1)} %add_add_fusion.refs_0_), channel_id=1, source_target_pairs={{0,2},{1,3},{2,0},{3,1},{4,6},{5,7},{6,4},{7,5},{8,10},{9,11},{10,... | collective-permute-start | bytes 98312 | tf_op jit(solution)/shard_map/ppermute | solution.py:234
  34.6 1.0 %collective-permute-start.12 = (f32[16,512]{1,0:T(8,128)S(1)}, f32[16,512]{1,0:T(8,128)S(1)}, u32[]{:S(2)}, u32[]{:S(2)}) collective-permute-start(f32[16,512]{1,0:T(8,128)S(1)} %add_add_fusion.refs_0_), channel_id=1, source_target_pairs={{0,3},{1,2},{2,1},{3,0},{4,7},{5,6},{6,5},{7,4},{8,11},{9,10},{10,... | collective-permute-start | bytes 98312 | tf_op jit(solution)/shard_map/ppermute | solution.py:234
  35.6 0.1 collective-permute-done.5.refs_2_
  35.7 0.9 %copy-done.1 = f32[72,512]{1,0:T(8,128)S(1)} copy-done((f32[72,512]{1,0:T(8,128)S(1)}, f32[72,512]{1,0:T(8,128)}, u32[]{:S(2)}) %copy-start.1) | copy-done | bytes 147480
  36.6 0.7 %county_totals.1 = (f32[64,512]{1,0:T(8,128)}, f32[8,128]{1,0:T(8,128)}, f32[69,512]{1,0:T(8,128)S(1)}, f32[4,64]{1,0:T(4,128)S(1)}) custom-call(s32[1,64]{1,0:T(1,128)S(1)} %bitcast.14, f32[64,512]{1,0:T(8,128)S(1)} %copy-done, f32[4,512]{1,0:T(4,128)S(1)} %copy-done.2, f32[1,512]{1,0:T(1,128)S(1)} %bitcast.12, f32[72,512]{1,0:T(8,128)S(1)} %copy-done.1, ...), custom_call_target="tpu_custom_call" | custom-call | tf_op jit(solution)/shard_map/county_totals/pallas_call | solution.py:340
  37.3 0.0 collective-permute-done.10.refs_1_
  37.3 0.6 %collective-permute-done.11.refs_2_ = f32[16,512]{1,0:T(8,128)S(1)} collective-permute-done((f32[16,512]{1,0:T(8,128)S(1)}, f32[16,512]{1,0:T(8,128)S(1)}, u32[]{:S(2)}, u32[]{:S(2)}) %collective-permute-start.11) | collective-permute-done | bytes 32800 | tf_op jit(solution)/shard_map/ppermute | solution.py:234
  37.9 0.4 collective-permute-done.12.refs_3_
  38.2 0.8 %upper_totals.1 = (f32[64,512]{1,0:T(8,128)}, f32[4,512]{1,0:T(4,128)}, f32[1,512]{1,0:T(1,128)}) custom-call(f32[69,512]{1,0:T(8,128)S(1)} %get-tuple-element.35.prior_ref, f32[4,64]{1,0:T(4,128)S(1)} %get-tuple-element.36.hot_ref, f32[16,512]{1,0:T(8,128)S(1)} %add_add_fusion.refs_0_, f32[16,512]{1,0:T(8,128)S(1)} %collective-permute-done.10.refs_1_, ...), custom_call_target="tpu_custom_call" | custom-call | tf_op jit(solution)/shard_map/upper_totals/pallas_call | solution.py:354
  (11 shorter events, 0.0 us)
Async XLA Ops:
  0.6 35.0 %copy-start.4 = (s32[64]{0:T(128)S(1)}, s32[64]{0:T(128)}, u32[]{:S(2)}) copy-start(s32[64]{0:T(128)} %param.23) | copy-start | bytes 772
  0.6 35.0 %copy-start = (f32[64,512]{1,0:T(8,128)S(1)}, f32[64,512]{1,0:T(8,128)}, u32[]{:S(2)}) copy-start(f32[64,512]{1,0:T(8,128)} %state_ref.1) | copy-start | bytes 393220
  0.7 35.0 %copy-start.2 = (f32[4,512]{1,0:T(4,128)S(1)}, f32[4,512]{1,0:T(4,128)}, u32[]{:S(2)}) copy-start(f32[4,512]{1,0:T(4,128)} %nation_ref.1) | copy-start | bytes 24580
  0.7 35.0 %copy-start.3 = (f32[512]{0:T(512)S(1)}, f32[512]{0:T(512)}, u32[]{:S(2)}) copy-start(f32[512]{0:T(512)} %param.16) | copy-start | bytes 6148
  13.9 5.1 %collective-permute-start.1 = (f32[16,512]{1,0:T(8,128)}, f32[16,512]{1,0:T(8,128)S(1)}, u32[]{:S(2)}, u32[]{:S(2)}) collective-permute-start(f32[16,512]{1,0:T(8,128)} %get-tuple-element.26), channel_id=1, source_target_pairs={{0,2},{1,3},{2,0},{3,1},{4,6},{5,7},{6,4},{7,5},{8,10},{9,11},{10,... | collective-permute-start | bytes 98312 | tf_op jit(solution)/shard_map/ppermute | solution.py:234
  16.9 3.6 %collective-permute-start.2 = (f32[16,512]{1,0:T(8,128)}, f32[16,512]{1,0:T(8,128)S(1)}, u32[]{:S(2)}, u32[]{:S(2)}) collective-permute-start(f32[16,512]{1,0:T(8,128)} %get-tuple-element.27), channel_id=1, source_target_pairs={{0,3},{1,2},{2,1},{3,0},{4,7},{5,6},{6,5},{7,4},{8,11},{9,10},{10,... | collective-permute-start | bytes 98312 | tf_op jit(solution)/shard_map/ppermute | solution.py:234
  16.9 3.6 %collective-permute-start = (f32[16,512]{1,0:T(8,128)}, f32[16,512]{1,0:T(8,128)S(1)}, u32[]{:S(2)}, u32[]{:S(2)}) collective-permute-start(f32[16,512]{1,0:T(8,128)} %get-tuple-element.25), channel_id=1, source_target_pairs={{0,1},{1,0},{2,3},{3,2},{4,5},{5,4},{6,7},{7,6},{8,9},{9,8},{10,11... | collective-permute-start | bytes 98312 | tf_op jit(solution)/shard_map/ppermute | solution.py:234
  17.1 4.2 %collective-permute-start.3 = (f32[72,512]{1,0:T(8,128)}, f32[72,512]{1,0:T(8,128)S(1)}, u32[]{:S(2)}, u32[]{:S(2)}) collective-permute-start(f32[72,512]{1,0:T(8,128)} %get-tuple-element.28), channel_id=1, source_target_pairs={{0,1},{1,0},{2,3},{3,2},{4,5},{5,4},{6,7},{7,6},{8,9},{9,8},{10,11... | collective-permute-start | bytes 442376 | tf_op jit(solution)/shard_map/ppermute | solution.py:234
  17.4 3.9 %collective-permute-start.4 = (f32[72,512]{1,0:T(8,128)}, f32[72,512]{1,0:T(8,128)S(1)}, u32[]{:S(2)}, u32[]{:S(2)}) collective-permute-start(f32[72,512]{1,0:T(8,128)} %get-tuple-element.29), channel_id=1, source_target_pairs={{0,1},{1,0},{2,3},{3,2},{4,5},{5,4},{6,7},{7,6},{8,9},{9,8},{10,11... | collective-permute-start | bytes 442376 | tf_op jit(solution)/shard_map/ppermute | solution.py:234
  21.4 4.0 %collective-permute-start.6 = (f32[16,512]{1,0:T(8,128)S(1)}, f32[16,512]{1,0:T(8,128)S(1)}, u32[]{:S(2)}, u32[]{:S(2)}) collective-permute-start(f32[16,512]{1,0:T(8,128)S(1)} %add_add_fusion.1), channel_id=1, source_target_pairs={{0,4},{4,0},{8,12},{12,8},{16,20},{20,16},{24,28},{28,24},{1,5},{5... | collective-permute-start | bytes 98312 | tf_op jit(solution)/shard_map/ppermute | solution.py:234
  25.4 5.9 %collective-permute-start.8 = (f32[16,512]{1,0:T(8,128)S(1)}, f32[16,512]{1,0:T(8,128)S(1)}, u32[]{:S(2)}, u32[]{:S(2)}) collective-permute-start(f32[16,512]{1,0:T(8,128)S(1)} %add.28), channel_id=1, source_target_pairs={{0,16},{4,20},{8,24},{12,28},{16,0},{20,4},{24,8},{28,12},{1,17},{... | collective-permute-start | bytes 98312 | tf_op jit(solution)/shard_map/ppermute | solution.py:234
  27.9 5.7 %collective-permute-start.9 = (f32[16,512]{1,0:T(8,128)S(1)}, f32[16,512]{1,0:T(8,128)S(1)}, u32[]{:S(2)}, u32[]{:S(2)}) collective-permute-start(f32[16,512]{1,0:T(8,128)S(1)} %add.28), channel_id=1, source_target_pairs={{0,24},{4,28},{8,16},{12,20},{16,8},{20,12},{24,0},{28,4},{1,25},{... | collective-permute-start | bytes 98312 | tf_op jit(solution)/shard_map/ppermute | solution.py:234
  29.3 4.4 %collective-permute-start.7 = (f32[16,512]{1,0:T(8,128)S(1)}, f32[16,512]{1,0:T(8,128)S(1)}, u32[]{:S(2)}, u32[]{:S(2)}) collective-permute-start(f32[16,512]{1,0:T(8,128)S(1)} %add.28), channel_id=1, source_target_pairs={{0,8},{4,12},{8,0},{12,4},{16,24},{20,28},{24,16},{28,20},{1,9},{5... | collective-permute-start | bytes 98312 | tf_op jit(solution)/shard_map/ppermute | solution.py:234
  30.5 5.2 %collective-permute-start.5 = (f32[72,512]{1,0:T(8,128)S(1)}, f32[72,512]{1,0:T(8,128)S(1)}, u32[]{:S(2)}, u32[]{:S(2)}) collective-permute-start(f32[72,512]{1,0:T(8,128)S(1)} %add.27), channel_id=1, source_target_pairs={{0,2},{1,3},{2,0},{3,1},{4,6},{5,7},{6,4},{7,5},{8,10},{9,11},{10,... | collective-permute-start | bytes 442376 | tf_op jit(solution)/shard_map/ppermute | solution.py:234
  33.7 3.6 %collective-permute-start.10 = (f32[16,512]{1,0:T(8,128)S(1)}, f32[16,512]{1,0:T(8,128)S(1)}, u32[]{:S(2)}, u32[]{:S(2)}) collective-permute-start(f32[16,512]{1,0:T(8,128)S(1)} %add_add_fusion.refs_0_), channel_id=1, source_target_pairs={{0,1},{1,0},{2,3},{3,2},{4,5},{5,4},{6,7},{7,6},{8,9},{9,8},{10,11... | collective-permute-start | bytes 98312 | tf_op jit(solution)/shard_map/ppermute | solution.py:234
  33.7 4.1 %collective-permute-start.11 = (f32[16,512]{1,0:T(8,128)S(1)}, f32[16,512]{1,0:T(8,128)S(1)}, u32[]{:S(2)}, u32[]{:S(2)}) collective-permute-start(f32[16,512]{1,0:T(8,128)S(1)} %add_add_fusion.refs_0_), channel_id=1, source_target_pairs={{0,2},{1,3},{2,0},{3,1},{4,6},{5,7},{6,4},{7,5},{8,10},{9,11},{10,... | collective-permute-start | bytes 98312 | tf_op jit(solution)/shard_map/ppermute | solution.py:234
  34.6 3.7 %collective-permute-start.12 = (f32[16,512]{1,0:T(8,128)S(1)}, f32[16,512]{1,0:T(8,128)S(1)}, u32[]{:S(2)}, u32[]{:S(2)}) collective-permute-start(f32[16,512]{1,0:T(8,128)S(1)} %add_add_fusion.refs_0_), channel_id=1, source_target_pairs={{0,3},{1,2},{2,1},{3,0},{4,7},{5,6},{6,5},{7,4},{8,11},{9,10},{10,... | collective-permute-start | bytes 98312 | tf_op jit(solution)/shard_map/ppermute | solution.py:234
  35.7 0.9 %copy-start.1 = (f32[72,512]{1,0:T(8,128)S(1)}, f32[72,512]{1,0:T(8,128)}, u32[]{:S(2)}) copy-start(f32[72,512]{1,0:T(8,128)} %get-tuple-element.23.refs_0_) | copy-start | bytes 442372

commit v7 on v5

--- a/solution.py
+++ b/solution.py
@@ -114,8 +114,8 @@
         bases[k][...] = pick(prec_ref[...], low, high_hot)
         hot_rows[k][...] = pick(map_ref[...], low, high_hot)
         scores[k][...] = lax.dot_general(
-            table[...], block(j), (((1,), (1,)), ((), ())), preferred_element_type=F32
-        )
+            block(j), table[...], (((1,), (1,)), ((), ())), preferred_element_type=F32
+        ).T
 
     def residue(j, k):
         county_hot = iota_rows(n_cnt) == hot_rows[k][...]
@@ -325,9 +325,14 @@
     near = 1 << (n_grp.bit_length() // 2 - 1)
     state_parts = [outs[0]] + [swap(outs[d], "row", d) for d in range(1, n_row)]
     state_piece = total_of(state_parts)
-    county_parts = [outs[n_row]] + [swap(outs[n_row + d], "row", d) for d in range(1, n_row)]
+    county_outs = outs[n_row:]
+    from_core = [swap(county_outs[d ^ 1], "row", 1) for d in range(0, n_row, 2)]
+    state_piece, *from_core = lax.optimization_barrier((state_piece, *from_core))
+    chip_sums = [county_outs[d] + from_core[d // 2] for d in range(2, n_row, 2)]
+    county_parts = [county_outs[0], from_core[0]] + [
+        swap(x, "row", d) for x, d in zip(chip_sums, range(2, n_row, 2))
+    ]
     state_piece = total_of(gather_by(state_piece, "grp", range(1, near)))
-    state_piece, *county_parts = lax.optimization_barrier((state_piece, *county_parts))
     county_grad, precinct_grad, prior, nation_hot = pl.pallas_call(
         county_end_kernel,
         out_shape=[

time: 39 us -> 38.3 us (0.982)
  waiting for transfers between devices: 10.1 us -> 8.72 us
  other arithmetic: 0.79 us -> 1.72 us
  starting transfers between devices: 13.1 us -> 12.2 us
  Pallas kernels: 12.3 us -> 13 us
    ppermute x13, waiting for transfers between devices: 10.1 us -> 8.72 us  [swap(): return lax.ppermute(x, axis, [(i, i ^ d) for i in range(n)])]
    add x0 -> x1, other arithmetic: none -> 0.93 us  [on_device(): chip_sums = [county_outs[d] + from_core[d // 2] for d in range(2, n_row, 2)]]
    ppermute x13, starting transfers between devices: 13.1 us -> 12.2 us  [swap(): return lax.ppermute(x, axis, [(i, i ^ d) for i in range(n)])]
    pallas_call x1, Pallas kernels: 10.9 us -> 11.5 us  [on_device(): pl.pallas_call(functools.partial(main_kernel, 2 * n_row), in_specs=[pl.Bl...]
  transfers between devices with their start and end apart: 13 -> 13, of which waited for: 6 -> 7; matrix products, arithmetic and copies ran while one was open for 2% -> 5% of each run, Pallas kernels for 2% -> 2%
where the time goes in v7:
time: 38.3 us; the launch traced here: 38 us
  Pallas kernels  13 us (34%)
  starting transfers between devices  12.2 us (32%)
  waiting for transfers between devices  8.72 us (23%)
  other arithmetic  1.72 us (4%)
  between operations  1.42 us (4%)
  local copies, waits for them, and re-layouts  0.92 us (2%)
    ppermute x13, starting transfers between devices, swap(): return lax.ppermute(x, axis, [(i, i ^ d) for i in range(n)])  12.2 us
    pallas_call x1, Pallas kernels, on_device(): pl.pallas_call(functools.partial(main_kernel, 2 * n_row), in_specs=[pl.Bl...  11.5 us
    ppermute x13, waiting for transfers between devices, swap(): return lax.ppermute(x, axis, [(i, i ^ d) for i in range(n)])  8.72 us
    add x1, other arithmetic, on_device(): chip_sums = [county_outs[d] + from_core[d // 2] for d in range(2, n_row, 2)]  0.93 us
    unnamed x10, local copies, waits for them, and re-layouts  0.92 us
    add x3, other arithmetic, total_of(): parts = [sum(parts[i:i + 2][1:], parts[i]) for i in range(0, len(parts), 2)]  0.79 us
    pallas_call x1, Pallas kernels, on_device(): pl.pallas_call(end_kernel, out_shape=[jax.ShapeDtypeStruct(state_coef.sha...  0.78 us
  transfers between devices with their start and end apart: 13, of which 7 were waited for; matrix products, arithmetic and copies ran while one was open for 5% of the time, Pallas kernels for 2%

profile of v7, /device:TPU:0, one launch (start us, length us, event | category | flops | bytes accessed | tf_op | source)
XLA Modules:
  0.0 38.0 jit_solution(1845450827846425614)
XLA Ops:
  1.4 11.5 %local_sums.1 = (f32[16,512]{1,0:T(8,128)}, f32[16,512]{1,0:T(8,128)}, f32[16,512]{1,0:T(8,128)}, f32[16,512]{1,0:T(8,128)}, f32[72,512]{1,0:T(8,128)}, /*index=...) custom-call(s32[1,1,1]{2,1,0:T(1,128)} %bitcast.10.count_ref, bf16[8192,512]{1,0:T(8,128)(2,1)} %features_ref.1, ...), custom_call_target="tpu_custom_call" | custom-call | tf_op jit(solution)/shard_map/local_sums/pallas_call | solution.py:289
  12.9 3.0 %collective-permute-start.1 = (f32[16,512]{1,0:T(8,128)}, f32[16,512]{1,0:T(8,128)S(1)}, u32[]{:S(2)}, u32[]{:S(2)}) collective-permute-start(f32[16,512]{1,0:T(8,128)} %get-tuple-element.26), channel_id=1, source_target_pairs={{0,2},{1,3},{2,0},{3,1},{4,6},{5,7},{6,4},{7,5},{8,10},{9,11},{10,... | collective-permute-start | bytes 98312 | tf_op jit(solution)/shard_map/ppermute | solution.py:230
  15.9 0.0 collective-permute-start.2
  15.9 0.2 collective-permute-start
  16.1 0.3 collective-permute-start.3
  16.4 0.2 collective-permute-start.4
  16.6 1.4 %collective-permute-done.1 = f32[16,512]{1,0:T(8,128)S(1)} collective-permute-done((f32[16,512]{1,0:T(8,128)}, f32[16,512]{1,0:T(8,128)S(1)}, u32[]{:S(2)}, u32[]{:S(2)}) %collective-permute-start.1) | collective-permute-done | bytes 32800 | tf_op jit(solution)/shard_map/ppermute | solution.py:230
  18.0 1.5 %collective-permute-done.2 = f32[16,512]{1,0:T(8,128)S(1)} collective-permute-done((f32[16,512]{1,0:T(8,128)}, f32[16,512]{1,0:T(8,128)S(1)}, u32[]{:S(2)}, u32[]{:S(2)}) %collective-permute-start.2) | collective-permute-done | bytes 32800 | tf_op jit(solution)/shard_map/ppermute | solution.py:230
  19.5 0.0 collective-permute-done
  19.6 0.8 %add_add_fusion.1 = f32[16,512]{1,0:T(8,128)S(1)} fusion(f32[16,512]{1,0:T(8,128)S(1)} %collective-permute-done.1, f32[16,512]{1,0:T(8,128)S(1)} %collective-permute-done.2, f32[16,512]{1,0:T(8,128)} %get-tuple-element.24, f32[16,512]{1,0:T(8,128)S(1)} %collective-permute-done), kind=kLoop, calls=%fused_computation.1 | loop fusion | flops 24576 | bytes 163840 | tf_op jit(solution)/shard_map/add | solution.py:239
  20.3 0.0 collective-permute-done.3.refs_1_
  20.3 0.0 collective-permute-done.4
  20.3 1.6 %collective-permute-start.6 = (f32[16,512]{1,0:T(8,128)S(1)}, f32[16,512]{1,0:T(8,128)S(1)}, u32[]{:S(2)}, u32[]{:S(2)}) collective-permute-start(f32[16,512]{1,0:T(8,128)S(1)} %add_add_fusion.1), channel_id=1, source_target_pairs={{0,4},{4,0},{8,12},{12,8},{16,20},{20,16},{24,28},{28,24},{1,5},{5... | collective-permute-start | bytes 98312 | tf_op jit(solution)/shard_map/ppermute | solution.py:230
  21.9 2.4 %collective-permute-done.6 = f32[16,512]{1,0:T(8,128)S(1)} collective-permute-done((f32[16,512]{1,0:T(8,128)S(1)}, f32[16,512]{1,0:T(8,128)S(1)}, u32[]{:S(2)}, u32[]{:S(2)}) %collective-permute-start.6) | collective-permute-done | bytes 32800 | tf_op jit(solution)/shard_map/ppermute | solution.py:230
  24.3 2.6 %collective-permute-start.8 = (f32[16,512]{1,0:T(8,128)S(1)}, f32[16,512]{1,0:T(8,128)S(1)}, u32[]{:S(2)}, u32[]{:S(2)}) collective-permute-start(f32[16,512]{1,0:T(8,128)S(1)} %add.28), channel_id=1, source_target_pairs={{0,16},{4,20},{8,24},{12,28},{16,0},{20,4},{24,8},{28,12},{1,17},{... | collective-permute-start | bytes 98312 | tf_op jit(solution)/shard_map/ppermute | solution.py:230
  26.9 1.3 %collective-permute-start.9 = (f32[16,512]{1,0:T(8,128)S(1)}, f32[16,512]{1,0:T(8,128)S(1)}, u32[]{:S(2)}, u32[]{:S(2)}) collective-permute-start(f32[16,512]{1,0:T(8,128)S(1)} %add.28), channel_id=1, source_target_pairs={{0,24},{4,28},{8,16},{12,20},{16,8},{20,12},{24,0},{28,4},{1,25},{... | collective-permute-start | bytes 98312 | tf_op jit(solution)/shard_map/ppermute | solution.py:230
  28.3 0.2 collective-permute-start.7
  28.5 0.9 %add.27 = f32[72,512]{1,0:T(8,128)S(1)} add(f32[72,512]{1,0:T(8,128)} %get-tuple-element.31, f32[72,512]{1,0:T(8,128)S(1)} %collective-permute-done.4) | non-fusion elementwise | flops 36864 | bytes 442368 | tf_op jit(solution)/shard_map/add | solution.py:331
  29.4 0.8 %collective-permute-start.5 = (f32[72,512]{1,0:T(8,128)S(1)}, f32[72,512]{1,0:T(8,128)S(1)}, u32[]{:S(2)}, u32[]{:S(2)}) collective-permute-start(f32[72,512]{1,0:T(8,128)S(1)} %add.27), channel_id=1, source_target_pairs={{0,2},{1,3},{2,0},{3,1},{4,6},{5,7},{6,4},{7,5},{8,10},{9,11},{10,... | collective-permute-start | bytes 442376 | tf_op jit(solution)/shard_map/ppermute | solution.py:230
  30.3 0.0 collective-permute-done.8
  30.3 2.4 %collective-permute-done.9 = f32[16,512]{1,0:T(8,128)S(1)} collective-permute-done((f32[16,512]{1,0:T(8,128)S(1)}, f32[16,512]{1,0:T(8,128)S(1)}, u32[]{:S(2)}, u32[]{:S(2)}) %collective-permute-start.9) | collective-permute-done | bytes 32800 | tf_op jit(solution)/shard_map/ppermute | solution.py:230
  32.6 0.0 collective-permute-done.7
  32.7 0.1 collective-permute-start.10
  32.7 0.8 %collective-permute-start.11 = (f32[16,512]{1,0:T(8,128)S(1)}, f32[16,512]{1,0:T(8,128)S(1)}, u32[]{:S(2)}, u32[]{:S(2)}) collective-permute-start(f32[16,512]{1,0:T(8,128)S(1)} %add_add_fusion.refs_0_), channel_id=1, source_target_pairs={{0,2},{1,3},{2,0},{3,1},{4,6},{5,7},{6,4},{7,5},{8,10},{9,11},{10,... | collective-permute-start | bytes 98312 | tf_op jit(solution)/shard_map/ppermute | solution.py:230
  33.6 1.0 %collective-permute-start.12 = (f32[16,512]{1,0:T(8,128)S(1)}, f32[16,512]{1,0:T(8,128)S(1)}, u32[]{:S(2)}, u32[]{:S(2)}) collective-permute-start(f32[16,512]{1,0:T(8,128)S(1)} %add_add_fusion.refs_0_), channel_id=1, source_target_pairs={{0,3},{1,2},{2,1},{3,0},{4,7},{5,6},{6,5},{7,4},{8,11},{9,10},{10,... | collective-permute-start | bytes 98312 | tf_op jit(solution)/shard_map/ppermute | solution.py:230
  34.6 0.1 collective-permute-done.5.refs_2_
  34.7 0.9 %copy-done.1 = f32[72,512]{1,0:T(8,128)S(1)} copy-done((f32[72,512]{1,0:T(8,128)S(1)}, f32[72,512]{1,0:T(8,128)}, u32[]{:S(2)}) %copy-start.1) | copy-done | bytes 147480
  35.6 0.7 %county_totals.1 = (f32[64,512]{1,0:T(8,128)}, f32[8,128]{1,0:T(8,128)}, f32[69,512]{1,0:T(8,128)S(1)}, f32[4,64]{1,0:T(4,128)S(1)}) custom-call(s32[1,64]{1,0:T(1,128)S(1)} %bitcast.14, f32[64,512]{1,0:T(8,128)S(1)} %copy-done, f32[4,512]{1,0:T(4,128)S(1)} %copy-done.2, f32[1,512]{1,0:T(1,128)S(1)} %bitcast.12, f32[72,512]{1,0:T(8,128)S(1)} %copy-done.1, ...), custom_call_target="tpu_custom_call" | custom-call | tf_op jit(solution)/shard_map/county_totals/pallas_call | solution.py:336
  36.3 0.0 collective-permute-done.10.refs_1_
  36.3 0.6 %collective-permute-done.11.refs_2_ = f32[16,512]{1,0:T(8,128)S(1)} collective-permute-done((f32[16,512]{1,0:T(8,128)S(1)}, f32[16,512]{1,0:T(8,128)S(1)}, u32[]{:S(2)}, u32[]{:S(2)}) %collective-permute-start.11) | collective-permute-done | bytes 32800 | tf_op jit(solution)/shard_map/ppermute | solution.py:230
  36.9 0.4 collective-permute-done.12.refs_3_
  37.2 0.8 %upper_totals.1 = (f32[64,512]{1,0:T(8,128)}, f32[4,512]{1,0:T(4,128)}, f32[1,512]{1,0:T(1,128)}) custom-call(f32[69,512]{1,0:T(8,128)S(1)} %get-tuple-element.35.prior_ref, f32[4,64]{1,0:T(4,128)S(1)} %get-tuple-element.36.hot_ref, f32[16,512]{1,0:T(8,128)S(1)} %add_add_fusion.refs_0_, f32[16,512]{1,0:T(8,128)S(1)} %collective-permute-done.10.refs_1_, ...), custom_call_target="tpu_custom_call" | custom-call | tf_op jit(solution)/shard_map/upper_totals/pallas_call | solution.py:350
  (11 shorter events, 0.0 us)
Async XLA Ops:
  0.6 34.0 %copy-start.4 = (s32[64]{0:T(128)S(1)}, s32[64]{0:T(128)}, u32[]{:S(2)}) copy-start(s32[64]{0:T(128)} %param.23) | copy-start | bytes 772
  0.6 34.0 %copy-start = (f32[64,512]{1,0:T(8,128)S(1)}, f32[64,512]{1,0:T(8,128)}, u32[]{:S(2)}) copy-start(f32[64,512]{1,0:T(8,128)} %state_ref.1) | copy-start | bytes 393220
  0.7 34.0 %copy-start.2 = (f32[4,512]{1,0:T(4,128)S(1)}, f32[4,512]{1,0:T(4,128)}, u32[]{:S(2)}) copy-start(f32[4,512]{1,0:T(4,128)} %nation_ref.1) | copy-start | bytes 24580
  0.7 34.0 %copy-start.3 = (f32[512]{0:T(512)S(1)}, f32[512]{0:T(512)}, u32[]{:S(2)}) copy-start(f32[512]{0:T(512)} %param.16) | copy-start | bytes 6148
  12.9 5.1 %collective-permute-start.1 = (f32[16,512]{1,0:T(8,128)}, f32[16,512]{1,0:T(8,128)S(1)}, u32[]{:S(2)}, u32[]{:S(2)}) collective-permute-start(f32[16,512]{1,0:T(8,128)} %get-tuple-element.26), channel_id=1, source_target_pairs={{0,2},{1,3},{2,0},{3,1},{4,6},{5,7},{6,4},{7,5},{8,10},{9,11},{10,... | collective-permute-start | bytes 98312 | tf_op jit(solution)/shard_map/ppermute | solution.py:230
  15.9 3.6 %collective-permute-start.2 = (f32[16,512]{1,0:T(8,128)}, f32[16,512]{1,0:T(8,128)S(1)}, u32[]{:S(2)}, u32[]{:S(2)}) collective-permute-start(f32[16,512]{1,0:T(8,128)} %get-tuple-element.27), channel_id=1, source_target_pairs={{0,3},{1,2},{2,1},{3,0},{4,7},{5,6},{6,5},{7,4},{8,11},{9,10},{10,... | collective-permute-start | bytes 98312 | tf_op jit(solution)/shard_map/ppermute | solution.py:230
  15.9 3.6 %collective-permute-start = (f32[16,512]{1,0:T(8,128)}, f32[16,512]{1,0:T(8,128)S(1)}, u32[]{:S(2)}, u32[]{:S(2)}) collective-permute-start(f32[16,512]{1,0:T(8,128)} %get-tuple-element.25), channel_id=1, source_target_pairs={{0,1},{1,0},{2,3},{3,2},{4,5},{5,4},{6,7},{7,6},{8,9},{9,8},{10,11... | collective-permute-start | bytes 98312 | tf_op jit(solution)/shard_map/ppermute | solution.py:230
  16.1 4.2 %collective-permute-start.3 = (f32[72,512]{1,0:T(8,128)}, f32[72,512]{1,0:T(8,128)S(1)}, u32[]{:S(2)}, u32[]{:S(2)}) collective-permute-start(f32[72,512]{1,0:T(8,128)} %get-tuple-element.28), channel_id=1, source_target_pairs={{0,1},{1,0},{2,3},{3,2},{4,5},{5,4},{6,7},{7,6},{8,9},{9,8},{10,11... | collective-permute-start | bytes 442376 | tf_op jit(solution)/shard_map/ppermute | solution.py:230
  16.4 3.9 %collective-permute-start.4 = (f32[72,512]{1,0:T(8,128)}, f32[72,512]{1,0:T(8,128)S(1)}, u32[]{:S(2)}, u32[]{:S(2)}) collective-permute-start(f32[72,512]{1,0:T(8,128)} %get-tuple-element.29), channel_id=1, source_target_pairs={{0,1},{1,0},{2,3},{3,2},{4,5},{5,4},{6,7},{7,6},{8,9},{9,8},{10,11... | collective-permute-start | bytes 442376 | tf_op jit(solution)/shard_map/ppermute | solution.py:230
  20.3 4.0 %collective-permute-start.6 = (f32[16,512]{1,0:T(8,128)S(1)}, f32[16,512]{1,0:T(8,128)S(1)}, u32[]{:S(2)}, u32[]{:S(2)}) collective-permute-start(f32[16,512]{1,0:T(8,128)S(1)} %add_add_fusion.1), channel_id=1, source_target_pairs={{0,4},{4,0},{8,12},{12,8},{16,20},{20,16},{24,28},{28,24},{1,5},{5... | collective-permute-start | bytes 98312 | tf_op jit(solution)/shard_map/ppermute | solution.py:230
  24.3 6.0 %collective-permute-start.8 = (f32[16,512]{1,0:T(8,128)S(1)}, f32[16,512]{1,0:T(8,128)S(1)}, u32[]{:S(2)}, u32[]{:S(2)}) collective-permute-start(f32[16,512]{1,0:T(8,128)S(1)} %add.28), channel_id=1, source_target_pairs={{0,16},{4,20},{8,24},{12,28},{16,0},{20,4},{24,8},{28,12},{1,17},{... | collective-permute-start | bytes 98312 | tf_op jit(solution)/shard_map/ppermute | solution.py:230
  26.9 5.7 %collective-permute-start.9 = (f32[16,512]{1,0:T(8,128)S(1)}, f32[16,512]{1,0:T(8,128)S(1)}, u32[]{:S(2)}, u32[]{:S(2)}) collective-permute-start(f32[16,512]{1,0:T(8,128)S(1)} %add.28), channel_id=1, source_target_pairs={{0,24},{4,28},{8,16},{12,20},{16,8},{20,12},{24,0},{28,4},{1,25},{... | collective-permute-start | bytes 98312 | tf_op jit(solution)/shard_map/ppermute | solution.py:230
  28.3 4.4 %collective-permute-start.7 = (f32[16,512]{1,0:T(8,128)S(1)}, f32[16,512]{1,0:T(8,128)S(1)}, u32[]{:S(2)}, u32[]{:S(2)}) collective-permute-start(f32[16,512]{1,0:T(8,128)S(1)} %add.28), channel_id=1, source_target_pairs={{0,8},{4,12},{8,0},{12,4},{16,24},{20,28},{24,16},{28,20},{1,9},{5... | collective-permute-start | bytes 98312 | tf_op jit(solution)/shard_map/ppermute | solution.py:230
  29.4 5.2 %collective-permute-start.5 = (f32[72,512]{1,0:T(8,128)S(1)}, f32[72,512]{1,0:T(8,128)S(1)}, u32[]{:S(2)}, u32[]{:S(2)}) collective-permute-start(f32[72,512]{1,0:T(8,128)S(1)} %add.27), channel_id=1, source_target_pairs={{0,2},{1,3},{2,0},{3,1},{4,6},{5,7},{6,4},{7,5},{8,10},{9,11},{10,... | collective-permute-start | bytes 442376 | tf_op jit(solution)/shard_map/ppermute | solution.py:230
  32.7 3.6 %collective-permute-start.10 = (f32[16,512]{1,0:T(8,128)S(1)}, f32[16,512]{1,0:T(8,128)S(1)}, u32[]{:S(2)}, u32[]{:S(2)}) collective-permute-start(f32[16,512]{1,0:T(8,128)S(1)} %add_add_fusion.refs_0_), channel_id=1, source_target_pairs={{0,1},{1,0},{2,3},{3,2},{4,5},{5,4},{6,7},{7,6},{8,9},{9,8},{10,11... | collective-permute-start | bytes 98312 | tf_op jit(solution)/shard_map/ppermute | solution.py:230
  32.7 4.1 %collective-permute-start.11 = (f32[16,512]{1,0:T(8,128)S(1)}, f32[16,512]{1,0:T(8,128)S(1)}, u32[]{:S(2)}, u32[]{:S(2)}) collective-permute-start(f32[16,512]{1,0:T(8,128)S(1)} %add_add_fusion.refs_0_), channel_id=1, source_target_pairs={{0,2},{1,3},{2,0},{3,1},{4,6},{5,7},{6,4},{7,5},{8,10},{9,11},{10,... | collective-permute-start | bytes 98312 | tf_op jit(solution)/shard_map/ppermute | solution.py:230
  33.6 3.7 %collective-permute-start.12 = (f32[16,512]{1,0:T(8,128)S(1)}, f32[16,512]{1,0:T(8,128)S(1)}, u32[]{:S(2)}, u32[]{:S(2)}) collective-permute-start(f32[16,512]{1,0:T(8,128)S(1)} %add_add_fusion.refs_0_), channel_id=1, source_target_pairs={{0,3},{1,2},{2,1},{3,0},{4,7},{5,6},{6,5},{7,4},{8,11},{9,10},{10,... | collective-permute-start | bytes 98312 | tf_op jit(solution)/shard_map/ppermute | solution.py:230
  34.7 0.9 %copy-start.1 = (f32[72,512]{1,0:T(8,128)S(1)}, f32[72,512]{1,0:T(8,128)}, u32[]{:S(2)}) copy-start(f32[72,512]{1,0:T(8,128)} %get-tuple-element.23.refs_0_) | copy-start | bytes 442372

commit v8 on v7

--- a/solution.py
+++ b/solution.py
@@ -25,11 +25,13 @@
 
 
 def hot_dot(hot, x, dims):
-    out = None
-    for part in reversed(split3(x)):
-        term = lax.dot_general(hot, part, (dims, ((), ())), preferred_element_type=F32)
-        out = term if out is None else out + term
-    return out
+    (left,), (right,) = dims
+    return lax.dot_general(
+        jnp.concatenate([hot] * 3, axis=left),
+        jnp.concatenate(split3(x), axis=right),
+        (dims, ((), ())),
+        preferred_element_type=F32,
+    )
 
 
 def iota_rows(n):
@@ -68,8 +70,8 @@
         outcome_ref,
     ) = held
     scores, hot_rows, bases, residuals, weights = (s0, s1), (h0, h1), (b0, b1), (r0, r1), (w0, w1)
-    n_row = len(outs) // 2
-    state_outs, county_outs = outs[:n_row], outs[n_row:]
+    state_outs, county_outs = outs[:2], outs[2:]
+    n_row = len(county_outs)
     n_states = state_ref.shape[0]
     n_nations = nation_ref.shape[0]
     n_cnt, p_size = county_ref.shape
@@ -114,8 +116,8 @@
         bases[k][...] = pick(prec_ref[...], low, high_hot)
         hot_rows[k][...] = pick(map_ref[...], low, high_hot)
         scores[k][...] = lax.dot_general(
-            block(j), table[...], (((1,), (1,)), ((), ())), preferred_element_type=F32
-        ).T
+            table[...], block(j), (((1,), (1,)), ((), ())), preferred_element_type=F32
+        )
 
     def residue(j, k):
         county_hot = iota_rows(n_cnt) == hot_rows[k][...]
@@ -170,7 +172,7 @@
 
     me = lax.axis_index("row")
     share = n_cnt // n_row
-    per = n_states // n_row
+    half = n_states // 2
     prec_sum = prec_acc[:n_hi] + prec_acc[n_hi:]
     own_rows = pl.ds(pl.multiple_of(me * share, share), share)
 
@@ -186,14 +188,33 @@
         county_outs[d][:share, :] = sums if d else sums - county_ref[own_rows, :]
         county_outs[d][share:, :LANES] = prec_sum if d else prec_sum - prec_ref[...]
         county_outs[d][share:, LANES:] = jnp.zeros((n_hi, p_size - LANES), F32)
-        copies.append(send(n_row + d))
+        copies.append(send(2 + d))
     state_acc[...] = hot_dot(state_hot, county_acc[...], ((1,), (0,)))
-    for d in range(n_row):
-        peer = jnp.bitwise_xor(me, d)
-        state_outs[d][...] = state_acc[pl.ds(pl.multiple_of(peer * per, per), per), :]
+    for d in range(2):
+        core = jnp.bitwise_xor(jnp.bitwise_and(me, 1), d)
+        sums = state_acc[pl.ds(pl.multiple_of(core * half, half), half), :]
+        pieces, per, _ = state_outs[d].shape
+        for q in range(pieces):
+            state_outs[d][q] = sums[q * per : (q + 1) * per, :]
         copies.append(send(d))
     for copy in copies:
         copy.wait()
+
+
+def plane_index(near, n_row):
+    x = jnp.bitwise_and(lax.axis_index("grp"), near - 1)
+    return x * (n_row // 2) + jnp.right_shift(lax.axis_index("row"), 1)
+
+
+def chip_sum_kernel(near, n_row, own_ref, core_ref, *refs):
+    *outs, own, sem = refs
+    copy = pltpu.make_async_copy(own_ref, own, sem)
+    copy.start()
+    copy.wait()
+    me = plane_index(near, n_row)
+    for d, out in enumerate(outs):
+        piece = jnp.bitwise_xor(me, d)
+        out[...] = own[piece] + core_ref[piece]
 
 
 def county_end_kernel(state_nation_ref, state_ref, nation_ref, beta_ref, *refs):
@@ -209,15 +230,19 @@
     prec_out[...] = total_of([part[share:, :LANES] for part in parts])
 
 
-def end_kernel(prior_ref, hot_ref, *refs):
-    *gathered, state_out, nation_out, beta_out, total = refs
-    me = lax.axis_index("row")
+def end_kernel(near, n_row, prior_ref, hot_ref, *refs):
+    *gathered, state_out, nation_out, beta_out, parts, total = refs
+    me = plane_index(near, n_row)
+    core = jnp.bitwise_and(lax.axis_index("row"), 1)
     per = gathered[0].shape[0]
     n_states = state_out.shape[0]
     n_nations = nation_out.shape[0]
-    for d, part in enumerate(gathered):
-        peer = jnp.bitwise_xor(me, d)
-        total[pl.ds(pl.multiple_of(peer * per, per), per), :] = part[...]
+    chips = len(gathered) // 2
+    for k, part in enumerate(gathered):
+        place = jnp.bitwise_xor(core, k // chips) * chips + jnp.bitwise_xor(me, k % chips)
+        parts[place] = part[...]
+    for k in range(len(gathered)):
+        total[k * per : (k + 1) * per, :] = parts[k]
     sums = total[...]
     nation_total = hot_dot(hot_ref[...].astype(BF16), sums, ((1,), (0,)))
     state_out[...] = sums - prior_ref[:n_states, :]
@@ -232,6 +257,15 @@
 
 def gather_by(x, axis, distances):
     return [x] + [swap(x, axis, d) for d in distances]
+
+
+def swap_plane(x, near, d):
+    n_grp, n_row = lax.axis_size("grp"), lax.axis_size("row")
+    up, across = d // (n_row // 2), d % (n_row // 2) * 2
+    pairs = [
+        (g * n_row + r, (g ^ up) * n_row + (r ^ across)) for g in range(n_grp) for r in range(n_row)
+    ]
+    return lax.ppermute(x, ("grp", "row"), pairs)
 
 
 def total_of(parts):
@@ -263,7 +297,10 @@
     share = cnt_here // n_row
     n_hi = prec_here // LANES
     steps = rows_here // ROW_STEP
-    per = n_states // n_row
+    near = 1 << (n_grp.bit_length() // 2 - 1)
+    chips = near * n_row // 2
+    half = n_states // 2
+    per = half // chips
 
     precinct3 = precinct.reshape(steps, 1, ROW_STEP)
     outcome3 = outcome.reshape(steps, 1, ROW_STEP)
@@ -287,11 +324,11 @@
         outcome3,
     )
     outs = pl.pallas_call(
-        functools.partial(main_kernel, 2 * n_row),
+        functools.partial(main_kernel, 2 + n_row),
         in_specs=[pl.BlockSpec(memory_space=pltpu.VMEM)]
         + [pl.BlockSpec(memory_space=pltpu.HBM)] * (SMALL + 1),
-        out_specs=[pl.BlockSpec(memory_space=pltpu.HBM)] * (2 * n_row),
-        out_shape=[jax.ShapeDtypeStruct((per, p_size), F32)] * n_row
+        out_specs=[pl.BlockSpec(memory_space=pltpu.HBM)] * (2 + n_row),
+        out_shape=[jax.ShapeDtypeStruct((chips, per, p_size), F32)] * 2
         + [jax.ShapeDtypeStruct((share + n_hi, p_size), F32)] * n_row,
         scratch_shapes=[pltpu.VMEM(x.shape, x.dtype) for x in small]
         + [
@@ -311,28 +348,34 @@
             pltpu.VMEM((2 * n_hi, LANES), F32),
             pltpu.VMEM(state_coef.shape, F32),
         ]
-        + [pltpu.VMEM((per, p_size), F32)] * n_row
+        + [pltpu.VMEM((chips, per, p_size), F32)] * 2
         + [pltpu.VMEM((share + n_hi, p_size), F32)] * n_row
         + [
             pltpu.SemaphoreType.DMA((SMALL,)),
             pltpu.SemaphoreType.DMA((steps,)),
-            pltpu.SemaphoreType.DMA((2 * n_row,)),
+            pltpu.SemaphoreType.DMA((2 + n_row,)),
         ],
         compiler_params=pltpu.CompilerParams(vmem_limit_bytes=VMEM_LIMIT),
         name="local_sums",
     )(row_counts.reshape(1, 1, 1), features, *small)
 
-    near = 1 << (n_grp.bit_length() // 2 - 1)
-    state_parts = [outs[0]] + [swap(outs[d], "row", d) for d in range(1, n_row)]
-    state_piece = total_of(state_parts)
-    county_outs = outs[n_row:]
+    state_core = swap(outs[1], "row", 1)
+    pieces = pl.pallas_call(
+        functools.partial(chip_sum_kernel, near, n_row),
+        in_specs=[pl.BlockSpec(memory_space=pl.ANY), pl.BlockSpec(memory_space=pltpu.VMEM)],
+        out_shape=[jax.ShapeDtypeStruct((per, p_size), F32)] * chips,
+        scratch_shapes=[pltpu.VMEM((chips, per, p_size), F32), pltpu.SemaphoreType.DMA(())],
+        compiler_params=pltpu.CompilerParams(vmem_limit_bytes=END_LIMIT),
+        name="chip_sums",
+    )(outs[0], state_core)
+    state_piece = total_of([pieces[0]] + [swap_plane(pieces[d], near, d) for d in range(1, chips)])
+    county_outs = outs[2:]
     from_core = [swap(county_outs[d ^ 1], "row", 1) for d in range(0, n_row, 2)]
     state_piece, *from_core = lax.optimization_barrier((state_piece, *from_core))
     chip_sums = [county_outs[d] + from_core[d // 2] for d in range(2, n_row, 2)]
     county_parts = [county_outs[0], from_core[0]] + [
         swap(x, "row", d) for x, d in zip(chip_sums, range(2, n_row, 2))
     ]
-    state_piece = total_of(gather_by(state_piece, "grp", range(1, near)))
     county_grad, precinct_grad, prior, nation_hot = pl.pallas_call(
         county_end_kernel,
         out_shape=[
@@ -346,15 +389,19 @@
     )(nation_row, state_coef, nation_coef, beta2, *county_parts)
 
     state_piece = total_of(gather_by(state_piece, "grp", range(near, n_grp, near)))
-    gathered = gather_by(state_piece, "row", range(1, n_row))
+    gathered = [state_piece] + [swap_plane(state_piece, near, d) for d in range(1, chips)]
+    gathered += [swap(x, "row", 1) for x in gathered]
     state_grad, nation_grad, beta_grad = pl.pallas_call(
-        end_kernel,
+        functools.partial(end_kernel, near, n_row),
         out_shape=[
             jax.ShapeDtypeStruct(state_coef.shape, F32),
             jax.ShapeDtypeStruct(nation_coef.shape, F32),
             jax.ShapeDtypeStruct((1, p_size), F32),
         ],
-        scratch_shapes=[pltpu.VMEM(state_coef.shape, F32)],
+        scratch_shapes=[
+            pltpu.VMEM((2 * chips, per, p_size), F32),
+            pltpu.VMEM(state_coef.shape, F32),
+        ],
         compiler_params=pltpu.CompilerParams(vmem_limit_bytes=END_LIMIT),
         name="upper_totals",
     )(prior, nation_hot, *gathered)

time: 38.3 us -> 40.5 us (1.057)
  starting transfers between devices: 12.2 us -> 14.5 us
  local copies, waits for them, and re-layouts: 0.92 us -> 1.76 us
  other arithmetic: 1.72 us -> 0.95 us
  Pallas kernels: 13 us -> 12.3 us
  waiting for transfers between devices: 8.72 us -> 9.2 us
    ppermute x0 -> x6, starting transfers between devices: none -> 7.98 us  [swap_plane(): return lax.ppermute(x, ('grp', 'row'), pairs)]
    ppermute x0 -> x6, waiting for transfers between devices: none -> 6.04 us  [swap_plane(): return lax.ppermute(x, ('grp', 'row'), pairs)]
    ppermute x13 -> x11, starting transfers between devices: 12.2 us -> 6.56 us  [swap(): return lax.ppermute(x, axis, [(i, i ^ d) for i in range(n)])]
    ppermute x13 -> x11, waiting for transfers between devices: 8.72 us -> 3.15 us  [swap(): return lax.ppermute(x, axis, [(i, i ^ d) for i in range(n)])]
    unnamed x10 -> x12, local copies, waits for them, and re-layouts: 0.92 us -> 1.76 us
    add x3 -> x2, other arithmetic: 0.79 us -> 0.01 us  [total_of(): parts = [sum(parts[i:i + 2][1:], parts[i]) for i in range(0, len(parts), 2)]]
    pallas_call x2 -> x3, Pallas kernels: 12.3 us -> 11.6 us  [the longest x1 10.8 us: on_device(): pl.pallas_call(functools.partial(main_kernel, 2 + n_row), in_specs=[pl.Bl...]
  transfers between devices with their start and end apart: 13 -> 17, of which waited for: 7 -> 7; matrix products, arithmetic and copies ran while one was open for 5% -> 2% of each run, Pallas kernels for 2% -> 2%
where the time goes in v8:
time: 40.5 us; the launch traced here: 40.2 us
  starting transfers between devices  14.5 us (36%)
  Pallas kernels  12.3 us (30%)
  waiting for transfers between devices  9.2 us (23%)
  local copies, waits for them, and re-layouts  1.76 us (4%)
  between operations  1.45 us (4%)
  other arithmetic  0.95 us (2%)
    pallas_call x1, Pallas kernels, on_device(): pl.pallas_call(functools.partial(main_kernel, 2 + n_row), in_specs=[pl.Bl...  10.8 us
    ppermute x6, starting transfers between devices, swap_plane(): return lax.ppermute(x, ('grp', 'row'), pairs)  7.98 us
    ppermute x11, starting transfers between devices, swap(): return lax.ppermute(x, axis, [(i, i ^ d) for i in range(n)])  6.56 us
    ppermute x6, waiting for transfers between devices, swap_plane(): return lax.ppermute(x, ('grp', 'row'), pairs)  6.04 us
    ppermute x11, waiting for transfers between devices, swap(): return lax.ppermute(x, axis, [(i, i ^ d) for i in range(n)])  3.15 us
    unnamed x12, local copies, waits for them, and re-layouts  1.76 us
    add x1, other arithmetic, on_device(): chip_sums = [county_outs[d] + from_core[d // 2] for d in range(2, n_row, 2)]  0.93 us
  transfers between devices with their start and end apart: 17, of which 7 were waited for; matrix products, arithmetic and copies ran while one was open for 2% of the time, Pallas kernels for 2%

profile of v8, /device:TPU:0, one launch (start us, length us, event | category | flops | bytes accessed | tf_op | source)
XLA Modules:
  0.0 40.2 jit_solution(3869940810512642350)
XLA Ops:
  1.4 10.8 %local_sums.1 = (f32[4,8,512]{2,1,0:T(8,128)}, f32[4,8,512]{2,1,0:T(8,128)}, f32[72,512]{1,0:T(8,128)}, f32[72,512]{1,0:T(8,128)}, f32[72,512]{1,0:T(8,128)}, /*index=5*/f32[72,512]{1,0:T(8,128)}) custom-call(s32[1,1,1]{2,1,0:T(1,128)} %bitcast.10.count_ref, bf16[8192,512]{1,0:T(8,128)(2,1)} %features_ref.1, s32[1,64]{1,0:T(1,128)} %bitcast.13, ...), custom_call_target="tpu_custom_call" | custom-call | tf_op jit(solution)/shard_map/local_sums/pallas_call | solution.py:326
  12.1 0.5 %collective-permute-start = (f32[4,8,512]{2,1,0:T(8,128)}, f32[4,8,512]{2,1,0:T(8,128)S(1)}, u32[]{:S(2)}, u32[]{:S(2)}) collective-permute-start(f32[4,8,512]{2,1,0:T(8,128)} %get-tuple-element.27), channel_id=1, source_target_pairs={{0,1},{1,0},{2,3},{3,2},{4,5},{5,4},{6,7},{7,6},{8,9},{9,8},{10,11... | collective-permute-start | bytes 196616 | tf_op jit(solution)/shard_map/ppermute | solution.py:255
  12.7 1.1 %collective-permute-done.core_ref = f32[4,8,512]{2,1,0:T(8,128)S(1)} collective-permute-done((f32[4,8,512]{2,1,0:T(8,128)}, f32[4,8,512]{2,1,0:T(8,128)S(1)}, u32[]{:S(2)}, u32[]{:S(2)}) %collective-permute-start) | collective-permute-done | bytes 65568 | tf_op jit(solution)/shard_map/ppermute | solution.py:255
  13.8 0.8 %copy-done.2 = f32[4,8,512]{2,1,0:T(8,128)S(1)} copy-done((f32[4,8,512]{2,1,0:T(8,128)S(1)}, f32[4,8,512]{2,1,0:T(8,128)}, u32[]{:S(2)}) %copy-start.2) | copy-done | bytes 65560
  14.6 0.1 chip_sums.1
  14.7 2.9 %collective-permute-start.2 = (f32[8,512]{1,0:T(8,128)S(1)}, f32[8,512]{1,0:T(8,128)S(1)}, u32[]{:S(2)}, u32[]{:S(2)}) collective-permute-start(f32[8,512]{1,0:T(8,128)S(1)} %get-tuple-element.30), channel_id=1, source_target_pairs={{0,4},{1,5},{2,6},{3,7},{4,0},{5,1},{6,2},{7,3},{8,12},{9,13},{10,... | collective-permute-start | bytes 49160 | tf_op jit(solution)/shard_map/ppermute | solution.py:268
  17.6 1.5 %collective-permute-start.3 = (f32[8,512]{1,0:T(8,128)S(1)}, f32[8,512]{1,0:T(8,128)S(1)}, u32[]{:S(2)}, u32[]{:S(2)}) collective-permute-start(f32[8,512]{1,0:T(8,128)S(1)} %get-tuple-element.31), channel_id=1, source_target_pairs={{0,6},{1,7},{2,4},{3,5},{4,2},{5,3},{6,0},{7,1},{8,14},{9,15},{10,... | collective-permute-start | bytes 49160 | tf_op jit(solution)/shard_map/ppermute | solution.py:268
  19.1 0.1 collective-permute-start.1
  19.1 0.5 %collective-permute-start.5 = (f32[72,512]{1,0:T(8,128)}, f32[72,512]{1,0:T(8,128)S(1)}, u32[]{:S(2)}, u32[]{:S(2)}) collective-permute-start(f32[72,512]{1,0:T(8,128)} %get-tuple-element.33), channel_id=1, source_target_pairs={{0,1},{1,0},{2,3},{3,2},{4,5},{5,4},{6,7},{7,6},{8,9},{9,8},{10,11... | collective-permute-start | bytes 442376 | tf_op jit(solution)/shard_map/ppermute | solution.py:255
  19.6 0.0 collective-permute-done.2
  19.6 2.6 %collective-permute-done.3 = f32[8,512]{1,0:T(8,128)S(1)} collective-permute-done((f32[8,512]{1,0:T(8,128)S(1)}, f32[8,512]{1,0:T(8,128)S(1)}, u32[]{:S(2)}, u32[]{:S(2)}) %collective-permute-start.3) | collective-permute-done | bytes 16416 | tf_op jit(solution)/shard_map/ppermute | solution.py:268
  22.2 0.6 %collective-permute-done.1 = f32[8,512]{1,0:T(8,128)S(1)} collective-permute-done((f32[8,512]{1,0:T(8,128)S(1)}, f32[8,512]{1,0:T(8,128)S(1)}, u32[]{:S(2)}, u32[]{:S(2)}) %collective-permute-start.1) | collective-permute-done | bytes 16416 | tf_op jit(solution)/shard_map/ppermute | solution.py:268
  22.8 0.0 collective-permute-done.4.refs_1_
  22.8 2.7 %collective-permute-start.8 = (f32[8,512]{1,0:T(8,128)S(1)}, f32[8,512]{1,0:T(8,128)S(1)}, u32[]{:S(2)}, u32[]{:S(2)}) collective-permute-start(f32[8,512]{1,0:T(8,128)S(1)} %add_add_fusion.1), channel_id=1, source_target_pairs={{0,16},{4,20},{8,24},{12,28},{16,0},{20,4},{24,8},{28,12},{1,17},{... | collective-permute-start | bytes 49160 | tf_op jit(solution)/shard_map/ppermute | solution.py:255
  25.5 1.3 %collective-permute-start.9 = (f32[8,512]{1,0:T(8,128)S(1)}, f32[8,512]{1,0:T(8,128)S(1)}, u32[]{:S(2)}, u32[]{:S(2)}) collective-permute-start(f32[8,512]{1,0:T(8,128)S(1)} %add_add_fusion.1), channel_id=1, source_target_pairs={{0,24},{4,28},{8,16},{12,20},{16,8},{20,12},{24,0},{28,4},{1,25},{... | collective-permute-start | bytes 49160 | tf_op jit(solution)/shard_map/ppermute | solution.py:255
  26.8 0.2 collective-permute-start.7
  27.1 0.9 %add.24 = f32[72,512]{1,0:T(8,128)S(1)} add(f32[72,512]{1,0:T(8,128)} %get-tuple-element.35, f32[72,512]{1,0:T(8,128)S(1)} %collective-permute-done.5) | non-fusion elementwise | flops 36864 | bytes 442368 | tf_op jit(solution)/shard_map/add | solution.py:375
  28.0 1.0 %collective-permute-start.6 = (f32[72,512]{1,0:T(8,128)S(1)}, f32[72,512]{1,0:T(8,128)S(1)}, u32[]{:S(2)}, u32[]{:S(2)}) collective-permute-start(f32[72,512]{1,0:T(8,128)S(1)} %add.24), channel_id=1, source_target_pairs={{0,2},{1,3},{2,0},{3,1},{4,6},{5,7},{6,4},{7,5},{8,10},{9,11},{10,... | collective-permute-start | bytes 442376 | tf_op jit(solution)/shard_map/ppermute | solution.py:255
  29.0 2.0 %collective-permute-done.9 = f32[8,512]{1,0:T(8,128)S(1)} collective-permute-done((f32[8,512]{1,0:T(8,128)S(1)}, f32[8,512]{1,0:T(8,128)S(1)}, u32[]{:S(2)}, u32[]{:S(2)}) %collective-permute-start.9) | collective-permute-done | bytes 16416 | tf_op jit(solution)/shard_map/ppermute | solution.py:255
  31.0 0.0 collective-permute-done.7
  31.0 1.0 %collective-permute-start.10 = (f32[8,512]{1,0:T(8,128)S(1)}, f32[8,512]{1,0:T(8,128)S(1)}, u32[]{:S(2)}, u32[]{:S(2)}) collective-permute-start(f32[8,512]{1,0:T(8,128)S(1)} %add_add_fusion.refs_0_), channel_id=1, source_target_pairs={{0,2},{1,3},{2,0},{3,1},{4,6},{5,7},{6,4},{7,5},{8,10},{9,11},{10,... | collective-permute-start | bytes 49160 | tf_op jit(solution)/shard_map/ppermute | solution.py:268
  32.0 1.1 %collective-permute-start.11 = (f32[8,512]{1,0:T(8,128)S(1)}, f32[8,512]{1,0:T(8,128)S(1)}, u32[]{:S(2)}, u32[]{:S(2)}) collective-permute-start(f32[8,512]{1,0:T(8,128)S(1)} %add_add_fusion.refs_0_), channel_id=1, source_target_pairs={{0,4},{1,5},{2,6},{3,7},{4,0},{5,1},{6,2},{7,3},{8,12},{9,13},{10,... | collective-permute-start | bytes 49160 | tf_op jit(solution)/shard_map/ppermute | solution.py:268
  33.1 1.5 %collective-permute-start.12 = (f32[8,512]{1,0:T(8,128)S(1)}, f32[8,512]{1,0:T(8,128)S(1)}, u32[]{:S(2)}, u32[]{:S(2)}) collective-permute-start(f32[8,512]{1,0:T(8,128)S(1)} %add_add_fusion.refs_0_), channel_id=1, source_target_pairs={{0,6},{1,7},{2,4},{3,5},{4,2},{5,3},{6,0},{7,1},{8,14},{9,15},{10,... | collective-permute-start | bytes 49160 | tf_op jit(solution)/shard_map/ppermute | solution.py:268
  34.6 0.2 collective-permute-done.10.refs_1_
  34.8 0.3 collective-permute-start.14
  35.1 0.7 %collective-permute-done.11.refs_2_ = f32[8,512]{1,0:T(8,128)S(1)} collective-permute-done((f32[8,512]{1,0:T(8,128)S(1)}, f32[8,512]{1,0:T(8,128)S(1)}, u32[]{:S(2)}, u32[]{:S(2)}) %collective-permute-start.11) | collective-permute-done | bytes 16416 | tf_op jit(solution)/shard_map/ppermute | solution.py:268
  35.8 0.0 collective-permute-start.15
  35.8 2.0 %collective-permute-done.12.refs_3_ = f32[8,512]{1,0:T(8,128)S(1)} collective-permute-done((f32[8,512]{1,0:T(8,128)S(1)}, f32[8,512]{1,0:T(8,128)S(1)}, u32[]{:S(2)}, u32[]{:S(2)}) %collective-permute-start.12) | collective-permute-done | bytes 16416 | tf_op jit(solution)/shard_map/ppermute | solution.py:268
  37.8 0.9 %copy-done.1 = f32[72,512]{1,0:T(8,128)S(1)} copy-done((f32[72,512]{1,0:T(8,128)S(1)}, f32[72,512]{1,0:T(8,128)}, u32[]{:S(2)}) %copy-start.1) | copy-done | bytes 147480
  38.7 0.7 %county_totals.1 = (f32[64,512]{1,0:T(8,128)}, f32[8,128]{1,0:T(8,128)}, f32[69,512]{1,0:T(8,128)S(1)}, f32[4,64]{1,0:T(4,128)S(1)}) custom-call(s32[1,64]{1,0:T(1,128)S(1)} %bitcast.14, f32[64,512]{1,0:T(8,128)S(1)} %copy-done, f32[4,512]{1,0:T(4,128)S(1)} %copy-done.3, f32[1,512]{1,0:T(1,128)S(1)} %bitcast.12, f32[72,512]{1,0:T(8,128)S(1)} %copy-done.1, ...), custom_call_target="tpu_custom_call" | custom-call | tf_op jit(solution)/shard_map/county_totals/pallas_call | solution.py:379
  39.4 0.0 collective-permute-done.13.refs_4_
  39.4 0.8 %upper_totals.1 = (f32[64,512]{1,0:T(8,128)}, f32[4,512]{1,0:T(4,128)}, f32[1,512]{1,0:T(1,128)}) custom-call(f32[69,512]{1,0:T(8,128)S(1)} %get-tuple-element.39.prior_ref, f32[4,64]{1,0:T(4,128)S(1)} %get-tuple-element.40.hot_ref, f32[8,512]{1,0:T(8,128)S(1)} %add_add_fusion.refs_0_, f32[8,512]{1,0:T(8,128)S(1)} %collective-permute-done.10.refs_1_, ...), custom_call_target="tpu_custom_call" | custom-call | tf_op jit(solution)/shard_map/upper_totals/pallas_call | solution.py:394
  (21 shorter events, 0.1 us)
Async XLA Ops:
  0.6 37.1 %copy-start.5 = (s32[64]{0:T(128)S(1)}, s32[64]{0:T(128)}, u32[]{:S(2)}) copy-start(s32[64]{0:T(128)} %param.23) | copy-start | bytes 772
  0.6 37.1 %copy-start = (f32[64,512]{1,0:T(8,128)S(1)}, f32[64,512]{1,0:T(8,128)}, u32[]{:S(2)}) copy-start(f32[64,512]{1,0:T(8,128)} %state_ref.1) | copy-start | bytes 393220
  0.7 37.1 %copy-start.3 = (f32[4,512]{1,0:T(4,128)S(1)}, f32[4,512]{1,0:T(4,128)}, u32[]{:S(2)}) copy-start(f32[4,512]{1,0:T(4,128)} %nation_ref.1) | copy-start | bytes 24580
  0.7 37.1 %copy-start.4 = (f32[512]{0:T(512)S(1)}, f32[512]{0:T(512)}, u32[]{:S(2)}) copy-start(f32[512]{0:T(512)} %param.16) | copy-start | bytes 6148
  12.1 1.7 %collective-permute-start = (f32[4,8,512]{2,1,0:T(8,128)}, f32[4,8,512]{2,1,0:T(8,128)S(1)}, u32[]{:S(2)}, u32[]{:S(2)}) collective-permute-start(f32[4,8,512]{2,1,0:T(8,128)} %get-tuple-element.27), channel_id=1, source_target_pairs={{0,1},{1,0},{2,3},{3,2},{4,5},{5,4},{6,7},{7,6},{8,9},{9,8},{10,11... | collective-permute-start | bytes 196616 | tf_op jit(solution)/shard_map/ppermute | solution.py:255
  13.8 0.8 %copy-start.2 = (f32[4,8,512]{2,1,0:T(8,128)S(1)}, f32[4,8,512]{2,1,0:T(8,128)}, u32[]{:S(2)}) copy-start(f32[4,8,512]{2,1,0:T(8,128)} %get-tuple-element.26.own_ref) | copy-start | bytes 196612
  14.7 4.9 %collective-permute-start.2 = (f32[8,512]{1,0:T(8,128)S(1)}, f32[8,512]{1,0:T(8,128)S(1)}, u32[]{:S(2)}, u32[]{:S(2)}) collective-permute-start(f32[8,512]{1,0:T(8,128)S(1)} %get-tuple-element.30), channel_id=1, source_target_pairs={{0,4},{1,5},{2,6},{3,7},{4,0},{5,1},{6,2},{7,3},{8,12},{9,13},{10,... | collective-permute-start | bytes 49160 | tf_op jit(solution)/shard_map/ppermute | solution.py:268
  17.6 4.6 %collective-permute-start.3 = (f32[8,512]{1,0:T(8,128)S(1)}, f32[8,512]{1,0:T(8,128)S(1)}, u32[]{:S(2)}, u32[]{:S(2)}) collective-permute-start(f32[8,512]{1,0:T(8,128)S(1)} %get-tuple-element.31), channel_id=1, source_target_pairs={{0,6},{1,7},{2,4},{3,5},{4,2},{5,3},{6,0},{7,1},{8,14},{9,15},{10,... | collective-permute-start | bytes 49160 | tf_op jit(solution)/shard_map/ppermute | solution.py:268
  19.1 3.7 %collective-permute-start.1 = (f32[8,512]{1,0:T(8,128)S(1)}, f32[8,512]{1,0:T(8,128)S(1)}, u32[]{:S(2)}, u32[]{:S(2)}) collective-permute-start(f32[8,512]{1,0:T(8,128)S(1)} %get-tuple-element.29), channel_id=1, source_target_pairs={{0,2},{1,3},{2,0},{3,1},{4,6},{5,7},{6,4},{7,5},{8,10},{9,11},{10,... | collective-permute-start | bytes 49160 | tf_op jit(solution)/shard_map/ppermute | solution.py:268
  19.1 3.7 %collective-permute-start.4 = (f32[72,512]{1,0:T(8,128)}, f32[72,512]{1,0:T(8,128)S(1)}, u32[]{:S(2)}, u32[]{:S(2)}) collective-permute-start(f32[72,512]{1,0:T(8,128)} %get-tuple-element.32), channel_id=1, source_target_pairs={{0,1},{1,0},{2,3},{3,2},{4,5},{5,4},{6,7},{7,6},{8,9},{9,8},{10,11... | collective-permute-start | bytes 442376 | tf_op jit(solution)/shard_map/ppermute | solution.py:255
  19.1 3.7 %collective-permute-start.5 = (f32[72,512]{1,0:T(8,128)}, f32[72,512]{1,0:T(8,128)S(1)}, u32[]{:S(2)}, u32[]{:S(2)}) collective-permute-start(f32[72,512]{1,0:T(8,128)} %get-tuple-element.33), channel_id=1, source_target_pairs={{0,1},{1,0},{2,3},{3,2},{4,5},{5,4},{6,7},{7,6},{8,9},{9,8},{10,11... | collective-permute-start | bytes 442376 | tf_op jit(solution)/shard_map/ppermute | solution.py:255
  22.8 6.2 %collective-permute-start.8 = (f32[8,512]{1,0:T(8,128)S(1)}, f32[8,512]{1,0:T(8,128)S(1)}, u32[]{:S(2)}, u32[]{:S(2)}) collective-permute-start(f32[8,512]{1,0:T(8,128)S(1)} %add_add_fusion.1), channel_id=1, source_target_pairs={{0,16},{4,20},{8,24},{12,28},{16,0},{20,4},{24,8},{28,12},{1,17},{... | collective-permute-start | bytes 49160 | tf_op jit(solution)/shard_map/ppermute | solution.py:255
  25.5 5.5 %collective-permute-start.9 = (f32[8,512]{1,0:T(8,128)S(1)}, f32[8,512]{1,0:T(8,128)S(1)}, u32[]{:S(2)}, u32[]{:S(2)}) collective-permute-start(f32[8,512]{1,0:T(8,128)S(1)} %add_add_fusion.1), channel_id=1, source_target_pairs={{0,24},{4,28},{8,16},{12,20},{16,8},{20,12},{24,0},{28,4},{1,25},{... | collective-permute-start | bytes 49160 | tf_op jit(solution)/shard_map/ppermute | solution.py:255
  26.8 4.2 %collective-permute-start.7 = (f32[8,512]{1,0:T(8,128)S(1)}, f32[8,512]{1,0:T(8,128)S(1)}, u32[]{:S(2)}, u32[]{:S(2)}) collective-permute-start(f32[8,512]{1,0:T(8,128)S(1)} %add_add_fusion.1), channel_id=1, source_target_pairs={{0,8},{4,12},{8,0},{12,4},{16,24},{20,28},{24,16},{28,20},{1,9},{5... | collective-permute-start | bytes 49160 | tf_op jit(solution)/shard_map/ppermute | solution.py:255
  28.0 9.7 %collective-permute-start.6 = (f32[72,512]{1,0:T(8,128)S(1)}, f32[72,512]{1,0:T(8,128)S(1)}, u32[]{:S(2)}, u32[]{:S(2)}) collective-permute-start(f32[72,512]{1,0:T(8,128)S(1)} %add.24), channel_id=1, source_target_pairs={{0,2},{1,3},{2,0},{3,1},{4,6},{5,7},{6,4},{7,5},{8,10},{9,11},{10,... | collective-permute-start | bytes 442376 | tf_op jit(solution)/shard_map/ppermute | solution.py:255
  31.0 3.8 %collective-permute-start.10 = (f32[8,512]{1,0:T(8,128)S(1)}, f32[8,512]{1,0:T(8,128)S(1)}, u32[]{:S(2)}, u32[]{:S(2)}) collective-permute-start(f32[8,512]{1,0:T(8,128)S(1)} %add_add_fusion.refs_0_), channel_id=1, source_target_pairs={{0,2},{1,3},{2,0},{3,1},{4,6},{5,7},{6,4},{7,5},{8,10},{9,11},{10,... | collective-permute-start | bytes 49160 | tf_op jit(solution)/shard_map/ppermute | solution.py:268
  32.0 3.7 %collective-permute-start.11 = (f32[8,512]{1,0:T(8,128)S(1)}, f32[8,512]{1,0:T(8,128)S(1)}, u32[]{:S(2)}, u32[]{:S(2)}) collective-permute-start(f32[8,512]{1,0:T(8,128)S(1)} %add_add_fusion.refs_0_), channel_id=1, source_target_pairs={{0,4},{1,5},{2,6},{3,7},{4,0},{5,1},{6,2},{7,3},{8,12},{9,13},{10,... | collective-permute-start | bytes 49160 | tf_op jit(solution)/shard_map/ppermute | solution.py:268
  33.1 4.6 %collective-permute-start.12 = (f32[8,512]{1,0:T(8,128)S(1)}, f32[8,512]{1,0:T(8,128)S(1)}, u32[]{:S(2)}, u32[]{:S(2)}) collective-permute-start(f32[8,512]{1,0:T(8,128)S(1)} %add_add_fusion.refs_0_), channel_id=1, source_target_pairs={{0,6},{1,7},{2,4},{3,5},{4,2},{5,3},{6,0},{7,1},{8,14},{9,15},{10,... | collective-permute-start | bytes 49160 | tf_op jit(solution)/shard_map/ppermute | solution.py:268
  34.6 4.8 %collective-permute-start.13 = (f32[8,512]{1,0:T(8,128)S(1)}, f32[8,512]{1,0:T(8,128)S(1)}, u32[]{:S(2)}, u32[]{:S(2)}) collective-permute-start(f32[8,512]{1,0:T(8,128)S(1)} %add_add_fusion.refs_0_), channel_id=1, source_target_pairs={{0,1},{1,0},{2,3},{3,2},{4,5},{5,4},{6,7},{7,6},{8,9},{9,8},{10,11... | collective-permute-start | bytes 49160 | tf_op jit(solution)/shard_map/ppermute | solution.py:255
  34.8 4.5 %collective-permute-start.14 = (f32[8,512]{1,0:T(8,128)S(1)}, f32[8,512]{1,0:T(8,128)S(1)}, u32[]{:S(2)}, u32[]{:S(2)}) collective-permute-start(f32[8,512]{1,0:T(8,128)S(1)} %collective-permute-done.10.refs_1_), channel_id=1, source_target_pairs={{0,1},{1,0},{2,3},{3,2},{4,5},{5,4},{6,7},{7,6},{8,9},{9,8},{10,11... | collective-permute-start | bytes 49160 | tf_op jit(solution)/shard_map/ppermute | solution.py:255
  35.8 3.6 %collective-permute-start.15 = (f32[8,512]{1,0:T(8,128)S(1)}, f32[8,512]{1,0:T(8,128)S(1)}, u32[]{:S(2)}, u32[]{:S(2)}) collective-permute-start(f32[8,512]{1,0:T(8,128)S(1)} %collective-permute-done.11.refs_2_), channel_id=1, source_target_pairs={{0,1},{1,0},{2,3},{3,2},{4,5},{5,4},{6,7},{7,6},{8,9},{9,8},{10,11... | collective-permute-start | bytes 49160 | tf_op jit(solution)/shard_map/ppermute | solution.py:255
  37.7 1.7 %collective-permute-start.16 = (f32[8,512]{1,0:T(8,128)S(1)}, f32[8,512]{1,0:T(8,128)S(1)}, u32[]{:S(2)}, u32[]{:S(2)}) collective-permute-start(f32[8,512]{1,0:T(8,128)S(1)} %collective-permute-done.12.refs_3_), channel_id=1, source_target_pairs={{0,1},{1,0},{2,3},{3,2},{4,5},{5,4},{6,7},{7,6},{8,9},{9,8},{10,11... | collective-permute-start | bytes 49160 | tf_op jit(solution)/shard_map/ppermute | solution.py:255
  37.8 0.9 %copy-start.1 = (f32[72,512]{1,0:T(8,128)S(1)}, f32[72,512]{1,0:T(8,128)}, u32[]{:S(2)}) copy-start(f32[72,512]{1,0:T(8,128)} %get-tuple-element.25.refs_0_) | copy-start | bytes 442372

commit v9 on v7

--- a/solution.py
+++ b/solution.py
@@ -25,11 +25,13 @@
 
 
 def hot_dot(hot, x, dims):
-    out = None
-    for part in reversed(split3(x)):
-        term = lax.dot_general(hot, part, (dims, ((), ())), preferred_element_type=F32)
-        out = term if out is None else out + term
-    return out
+    (left,), (right,) = dims
+    return lax.dot_general(
+        jnp.concatenate([hot] * 3, axis=left),
+        jnp.concatenate(split3(x), axis=right),
+        (dims, ((), ())),
+        preferred_element_type=F32,
+    )
 
 
 def iota_rows(n):
@@ -114,8 +116,8 @@
         bases[k][...] = pick(prec_ref[...], low, high_hot)
         hot_rows[k][...] = pick(map_ref[...], low, high_hot)
         scores[k][...] = lax.dot_general(
-            block(j), table[...], (((1,), (1,)), ((), ())), preferred_element_type=F32
-        ).T
+            table[...], block(j), (((1,), (1,)), ((), ())), preferred_element_type=F32
+        )
 
     def residue(j, k):
         county_hot = iota_rows(n_cnt) == hot_rows[k][...]
@@ -332,7 +334,8 @@
     county_parts = [county_outs[0], from_core[0]] + [
         swap(x, "row", d) for x, d in zip(chip_sums, range(2, n_row, 2))
     ]
-    state_piece = total_of(gather_by(state_piece, "grp", range(1, near)))
+    pairs = [[g + d for d in range(near)] for g in range(0, n_grp, near)]
+    state_piece = lax.psum(state_piece, "grp", axis_index_groups=pairs)
     county_grad, precinct_grad, prior, nation_hot = pl.pallas_call(
         county_end_kernel,
         out_shape=[
@@ -345,7 +348,8 @@
         name="county_totals",
     )(nation_row, state_coef, nation_coef, beta2, *county_parts)
 
-    state_piece = total_of(gather_by(state_piece, "grp", range(near, n_grp, near)))
+    lines = [list(range(d, n_grp, near)) for d in range(near)]
+    state_piece = lax.psum(state_piece, "grp", axis_index_groups=lines)
     gathered = gather_by(state_piece, "row", range(1, n_row))
     state_grad, nation_grad, beta_grad = pl.pallas_call(
         end_kernel,

time: 38.3 us -> 54.8 us (1.43)
  blocking collectives: 0 us -> 27.7 us
  starting transfers between devices: 12.2 us -> 6.45 us
  waiting for transfers between devices: 8.72 us -> 4.06 us
  Pallas kernels: 13 us -> 12.2 us
    psum x0 -> x2, blocking collectives: none -> 27.7 us  [the longest x1 19.3 us: on_device(): state_piece = lax.psum(state_piece, 'grp', axis_index_groups=lines)]
    ppermute x13 -> x9, starting transfers between devices: 12.2 us -> 6.45 us  [swap(): return lax.ppermute(x, axis, [(i, i ^ d) for i in range(n)])]
    ppermute x13 -> x9, waiting for transfers between devices: 8.72 us -> 4.06 us  [swap(): return lax.ppermute(x, axis, [(i, i ^ d) for i in range(n)])]
    pallas_call x1, Pallas kernels: 11.5 us -> 10.8 us  [on_device(): pl.pallas_call(functools.partial(main_kernel, 2 * n_row), in_specs=[pl.Bl...]
  transfers between devices with their start and end apart: 13 -> 9, of which waited for: 7 -> 4; matrix products, arithmetic and copies ran while one was open for 5% -> 1% of each run, Pallas kernels for 2% -> 1%
where the time goes in v9:
time: 54.8 us; the launch traced here: 54.5 us
  blocking collectives  27.7 us (51%)
  Pallas kernels  12.2 us (22%)
  starting transfers between devices  6.45 us (12%)
  waiting for transfers between devices  4.06 us (7%)
  other arithmetic  1.7 us (3%)
  between operations  1.44 us (3%)
  local copies, waits for them, and re-layouts  0.92 us (2%)
    psum x1, blocking collectives, on_device(): state_piece = lax.psum(state_piece, 'grp', axis_index_groups=lines)  19.3 us
    pallas_call x1, Pallas kernels, on_device(): pl.pallas_call(functools.partial(main_kernel, 2 * n_row), in_specs=[pl.Bl...  10.8 us
    psum x1, blocking collectives, on_device(): state_piece = lax.psum(state_piece, 'grp', axis_index_groups=pairs)  8.43 us
    ppermute x9, starting transfers between devices, swap(): return lax.ppermute(x, axis, [(i, i ^ d) for i in range(n)])  6.45 us
    ppermute x9, waiting for transfers between devices, swap(): return lax.ppermute(x, axis, [(i, i ^ d) for i in range(n)])  4.06 us
  transfers between devices with their start and end apart: 9, of which 4 were waited for; matrix products, arithmetic and copies ran while one was open for 1% of the time, Pallas kernels for 1%

profile of v9, /device:TPU:0, one launch (start us, length us, event | category | flops | bytes accessed | tf_op | source)
XLA Modules:
  0.0 54.5 jit_solution(6768284433641734589)
XLA Ops:
  0.6 0.0 copy-start.4
  0.6 0.0 copy-start.3
  0.7 0.0 copy-start.2
  0.7 0.0 copy-start
  1.4 10.8 %local_sums.1 = (f32[16,512]{1,0:T(8,128)}, f32[16,512]{1,0:T(8,128)}, f32[16,512]{1,0:T(8,128)}, f32[16,512]{1,0:T(8,128)}, f32[72,512]{1,0:T(8,128)}, /*index=...) custom-call(s32[1,1,1]{2,1,0:T(1,128)} %bitcast.10.count_ref, bf16[8192,512]{1,0:T(8,128)(2,1)} %features_ref.1, ...), custom_call_target="tpu_custom_call" | custom-call | tf_op jit(solution)/shard_map/local_sums/pallas_call | solution.py:291
  12.1 0.5 collective-permute-start
  12.6 2.6 %collective-permute-start.1 = (f32[16,512]{1,0:T(8,128)}, f32[16,512]{1,0:T(8,128)S(1)}, u32[]{:S(2)}, u32[]{:S(2)}) collective-permute-start(f32[16,512]{1,0:T(8,128)} %get-tuple-element.26), channel_id=1, source_target_pairs={{0,2},{1,3},{2,0},{3,1},{4,6},{5,7},{6,4},{7,5},{8,10},{9,11},{10,... | collective-permute-start | bytes 98312 | tf_op jit(solution)/shard_map/ppermute | solution.py:232
  15.2 0.1 collective-permute-start.2
  15.3 0.1 collective-permute-start.3
  15.4 0.4 collective-permute-start.4
  15.8 0.0 collective-permute-done
  15.8 1.6 %collective-permute-done.1 = f32[16,512]{1,0:T(8,128)S(1)} collective-permute-done((f32[16,512]{1,0:T(8,128)}, f32[16,512]{1,0:T(8,128)S(1)}, u32[]{:S(2)}, u32[]{:S(2)}) %collective-permute-start.1) | collective-permute-done | bytes 32800 | tf_op jit(solution)/shard_map/ppermute | solution.py:232
  17.4 1.4 %collective-permute-done.2 = f32[16,512]{1,0:T(8,128)S(1)} collective-permute-done((f32[16,512]{1,0:T(8,128)}, f32[16,512]{1,0:T(8,128)S(1)}, u32[]{:S(2)}, u32[]{:S(2)}) %collective-permute-start.2) | collective-permute-done | bytes 32800 | tf_op jit(solution)/shard_map/ppermute | solution.py:232
  18.8 0.8 %add_add_fusion = f32[16,512]{1,0:T(8,128)S(1)} fusion(f32[16,512]{1,0:T(8,128)S(1)} %collective-permute-done.1, f32[16,512]{1,0:T(8,128)S(1)} %collective-permute-done.2, f32[16,512]{1,0:T(8,128)} %get-tuple-element.24, f32[16,512]{1,0:T(8,128)S(1)} %collective-permute-done), kind=kLoop, calls=%fused_computation | loop fusion | flops 24576 | bytes 163840 | tf_op jit(solution)/shard_map/add | solution.py:241
  19.6 0.0 collective-permute-done.3.refs_1_
  19.6 0.0 collective-permute-done.4
  19.6 0.9 %add.19 = f32[72,512]{1,0:T(8,128)S(1)} add(f32[72,512]{1,0:T(8,128)} %get-tuple-element.31, f32[72,512]{1,0:T(8,128)S(1)} %collective-permute-done.4) | non-fusion elementwise | flops 36864 | bytes 442368 | tf_op jit(solution)/shard_map/add | solution.py:333
  20.5 0.8 %collective-permute-start.5 = (f32[72,512]{1,0:T(8,128)S(1)}, f32[72,512]{1,0:T(8,128)S(1)}, u32[]{:S(2)}, u32[]{:S(2)}) collective-permute-start(f32[72,512]{1,0:T(8,128)S(1)} %add.19), channel_id=1, source_target_pairs={{0,2},{1,3},{2,0},{3,1},{4,6},{5,7},{6,4},{7,5},{8,10},{9,11},{10,... | collective-permute-start | bytes 442376 | tf_op jit(solution)/shard_map/ppermute | solution.py:232
  21.3 8.4 %psum.14 = f32[16,512]{1,0:T(8,128)S(1)} all-reduce(f32[16,512]{1,0:T(8,128)S(1)} %add_add_fusion), channel_id=1, replica_groups={{0,4},{8,12},{16,20},{24,28},{1,5},{9,13},{17,21},{25,29},{2,6},{10,14}..., use_global_device_ids=true, to_apply=%region_0.0 | all-reduce | flops 8192 | bytes 65536 | tf_op jit(solution)/shard_map/psum | solution.py:338
  29.8 19.3 %psum.15.refs_0_ = f32[16,512]{1,0:T(8,128)S(1)} all-reduce(f32[16,512]{1,0:T(8,128)S(1)} %psum.14), channel_id=1, replica_groups={{0,8,16,24},{4,12,20,28},{1,9,17,25},{5,13,21,29},{2,10,18,26},{6,14,22..., use_global_device_ids=true, to_apply=%region_1.0 | all-reduce | flops 8192 | bytes 65536 | tf_op jit(solution)/shard_map/psum | solution.py:352
  49.0 0.1 collective-permute-start.6
  49.1 1.2 %collective-permute-start.7 = (f32[16,512]{1,0:T(8,128)S(1)}, f32[16,512]{1,0:T(8,128)S(1)}, u32[]{:S(2)}, u32[]{:S(2)}) collective-permute-start(f32[16,512]{1,0:T(8,128)S(1)} %psum.15.refs_0_), channel_id=1, source_target_pairs={{0,2},{1,3},{2,0},{3,1},{4,6},{5,7},{6,4},{7,5},{8,10},{9,11},{10,... | collective-permute-start | bytes 98312 | tf_op jit(solution)/shard_map/ppermute | solution.py:232
  50.3 0.6 %collective-permute-start.8 = (f32[16,512]{1,0:T(8,128)S(1)}, f32[16,512]{1,0:T(8,128)S(1)}, u32[]{:S(2)}, u32[]{:S(2)}) collective-permute-start(f32[16,512]{1,0:T(8,128)S(1)} %psum.15.refs_0_), channel_id=1, source_target_pairs={{0,3},{1,2},{2,1},{3,0},{4,7},{5,6},{6,5},{7,4},{8,11},{9,10},{10,... | collective-permute-start | bytes 98312 | tf_op jit(solution)/shard_map/ppermute | solution.py:232
  51.0 0.0 collective-permute-done.5.refs_2_
  51.0 0.0 copy-done.4
  51.0 0.0 copy-done.3
  51.0 0.9 %copy-done.1 = f32[72,512]{1,0:T(8,128)S(1)} copy-done((f32[72,512]{1,0:T(8,128)S(1)}, f32[72,512]{1,0:T(8,128)}, u32[]{:S(2)}) %copy-start.1) | copy-done | bytes 147480
  51.9 0.7 %county_totals.1 = (f32[64,512]{1,0:T(8,128)}, f32[8,128]{1,0:T(8,128)}, f32[69,512]{1,0:T(8,128)S(1)}, f32[4,64]{1,0:T(4,128)S(1)}) custom-call(s32[1,64]{1,0:T(1,128)S(1)} %bitcast.14, f32[64,512]{1,0:T(8,128)S(1)} %copy-done, f32[4,512]{1,0:T(4,128)S(1)} %copy-done.2, f32[1,512]{1,0:T(1,128)S(1)} %bitcast.12, f32[72,512]{1,0:T(8,128)S(1)} %copy-done.1, ...), custom_call_target="tpu_custom_call" | custom-call | tf_op jit(solution)/shard_map/county_totals/pallas_call | solution.py:339
  52.6 0.0 collective-permute-done.6.refs_1_
  52.6 0.5 collective-permute-done.7.refs_2_
  53.1 0.6 %collective-permute-done.8.refs_3_ = f32[16,512]{1,0:T(8,128)S(1)} collective-permute-done((f32[16,512]{1,0:T(8,128)S(1)}, f32[16,512]{1,0:T(8,128)S(1)}, u32[]{:S(2)}, u32[]{:S(2)}) %collective-permute-start.8) | collective-permute-done | bytes 32800 | tf_op jit(solution)/shard_map/ppermute | solution.py:232
  53.7 0.8 %upper_totals.1 = (f32[64,512]{1,0:T(8,128)}, f32[4,512]{1,0:T(4,128)}, f32[1,512]{1,0:T(1,128)}) custom-call(f32[69,512]{1,0:T(8,128)S(1)} %get-tuple-element.35.prior_ref, f32[4,64]{1,0:T(4,128)S(1)} %get-tuple-element.36.hot_ref, f32[16,512]{1,0:T(8,128)S(1)} %psum.15.refs_0_, f32[16,512]{1,0:T(8,128)S(1)} %collective-permute-done.6.refs_1_, ...), custom_call_target="tpu_custom_call" | custom-call | tf_op jit(solution)/shard_map/upper_totals/pallas_call | solution.py:354
  (3 shorter events, 0.0 us)
Async XLA Ops:
  0.6 50.3 %copy-start.4 = (s32[64]{0:T(128)S(1)}, s32[64]{0:T(128)}, u32[]{:S(2)}) copy-start(s32[64]{0:T(128)} %param.23) | copy-start | bytes 772
  0.6 50.3 %copy-start.3 = (f32[512]{0:T(512)S(1)}, f32[512]{0:T(512)}, u32[]{:S(2)}) copy-start(f32[512]{0:T(512)} %param.16) | copy-start | bytes 6148
  0.7 50.3 %copy-start.2 = (f32[4,512]{1,0:T(4,128)S(1)}, f32[4,512]{1,0:T(4,128)}, u32[]{:S(2)}) copy-start(f32[4,512]{1,0:T(4,128)} %nation_ref.1) | copy-start | bytes 24580
  0.7 50.3 %copy-start = (f32[64,512]{1,0:T(8,128)S(1)}, f32[64,512]{1,0:T(8,128)}, u32[]{:S(2)}) copy-start(f32[64,512]{1,0:T(8,128)} %state_ref.1) | copy-start | bytes 393220
  12.1 3.7 %collective-permute-start = (f32[16,512]{1,0:T(8,128)}, f32[16,512]{1,0:T(8,128)S(1)}, u32[]{:S(2)}, u32[]{:S(2)}) collective-permute-start(f32[16,512]{1,0:T(8,128)} %get-tuple-element.25), channel_id=1, source_target_pairs={{0,1},{1,0},{2,3},{3,2},{4,5},{5,4},{6,7},{7,6},{8,9},{9,8},{10,11... | collective-permute-start | bytes 98312 | tf_op jit(solution)/shard_map/ppermute | solution.py:232
  12.6 4.8 %collective-permute-start.1 = (f32[16,512]{1,0:T(8,128)}, f32[16,512]{1,0:T(8,128)S(1)}, u32[]{:S(2)}, u32[]{:S(2)}) collective-permute-start(f32[16,512]{1,0:T(8,128)} %get-tuple-element.26), channel_id=1, source_target_pairs={{0,2},{1,3},{2,0},{3,1},{4,6},{5,7},{6,4},{7,5},{8,10},{9,11},{10,... | collective-permute-start | bytes 98312 | tf_op jit(solution)/shard_map/ppermute | solution.py:232
  15.2 3.6 %collective-permute-start.2 = (f32[16,512]{1,0:T(8,128)}, f32[16,512]{1,0:T(8,128)S(1)}, u32[]{:S(2)}, u32[]{:S(2)}) collective-permute-start(f32[16,512]{1,0:T(8,128)} %get-tuple-element.27), channel_id=1, source_target_pairs={{0,3},{1,2},{2,1},{3,0},{4,7},{5,6},{6,5},{7,4},{8,11},{9,10},{10,... | collective-permute-start | bytes 98312 | tf_op jit(solution)/shard_map/ppermute | solution.py:232
  15.3 4.3 %collective-permute-start.3 = (f32[72,512]{1,0:T(8,128)}, f32[72,512]{1,0:T(8,128)S(1)}, u32[]{:S(2)}, u32[]{:S(2)}) collective-permute-start(f32[72,512]{1,0:T(8,128)} %get-tuple-element.28), channel_id=1, source_target_pairs={{0,1},{1,0},{2,3},{3,2},{4,5},{5,4},{6,7},{7,6},{8,9},{9,8},{10,11... | collective-permute-start | bytes 442376 | tf_op jit(solution)/shard_map/ppermute | solution.py:232
  15.4 4.1 %collective-permute-start.4 = (f32[72,512]{1,0:T(8,128)}, f32[72,512]{1,0:T(8,128)S(1)}, u32[]{:S(2)}, u32[]{:S(2)}) collective-permute-start(f32[72,512]{1,0:T(8,128)} %get-tuple-element.29), channel_id=1, source_target_pairs={{0,1},{1,0},{2,3},{3,2},{4,5},{5,4},{6,7},{7,6},{8,9},{9,8},{10,11... | collective-permute-start | bytes 442376 | tf_op jit(solution)/shard_map/ppermute | solution.py:232
  20.5 30.5 %collective-permute-start.5 = (f32[72,512]{1,0:T(8,128)S(1)}, f32[72,512]{1,0:T(8,128)S(1)}, u32[]{:S(2)}, u32[]{:S(2)}) collective-permute-start(f32[72,512]{1,0:T(8,128)S(1)} %add.19), channel_id=1, source_target_pairs={{0,2},{1,3},{2,0},{3,1},{4,6},{5,7},{6,4},{7,5},{8,10},{9,11},{10,... | collective-permute-start | bytes 442376 | tf_op jit(solution)/shard_map/ppermute | solution.py:232
  49.0 3.6 %collective-permute-start.6 = (f32[16,512]{1,0:T(8,128)S(1)}, f32[16,512]{1,0:T(8,128)S(1)}, u32[]{:S(2)}, u32[]{:S(2)}) collective-permute-start(f32[16,512]{1,0:T(8,128)S(1)} %psum.15.refs_0_), channel_id=1, source_target_pairs={{0,1},{1,0},{2,3},{3,2},{4,5},{5,4},{6,7},{7,6},{8,9},{9,8},{10,11... | collective-permute-start | bytes 98312 | tf_op jit(solution)/shard_map/ppermute | solution.py:232
  49.1 4.0 %collective-permute-start.7 = (f32[16,512]{1,0:T(8,128)S(1)}, f32[16,512]{1,0:T(8,128)S(1)}, u32[]{:S(2)}, u32[]{:S(2)}) collective-permute-start(f32[16,512]{1,0:T(8,128)S(1)} %psum.15.refs_0_), channel_id=1, source_target_pairs={{0,2},{1,3},{2,0},{3,1},{4,6},{5,7},{6,4},{7,5},{8,10},{9,11},{10,... | collective-permute-start | bytes 98312 | tf_op jit(solution)/shard_map/ppermute | solution.py:232
  50.3 3.3 %collective-permute-start.8 = (f32[16,512]{1,0:T(8,128)S(1)}, f32[16,512]{1,0:T(8,128)S(1)}, u32[]{:S(2)}, u32[]{:S(2)}) collective-permute-start(f32[16,512]{1,0:T(8,128)S(1)} %psum.15.refs_0_), channel_id=1, source_target_pairs={{0,3},{1,2},{2,1},{3,0},{4,7},{5,6},{6,5},{7,4},{8,11},{9,10},{10,... | collective-permute-start | bytes 98312 | tf_op jit(solution)/shard_map/ppermute | solution.py:232
  51.0 0.9 %copy-start.1 = (f32[72,512]{1,0:T(8,128)S(1)}, f32[72,512]{1,0:T(8,128)}, u32[]{:S(2)}) copy-start(f32[72,512]{1,0:T(8,128)} %get-tuple-element.23.refs_0_) | copy-start | bytes 442372

commit v10 on v9

--- a/solution.py
+++ b/solution.py
@@ -8,7 +8,7 @@
 from jax.sharding import PartitionSpec as P
 
 LANES = 128
-ROW_STEP = 1024
+ROW_STEP = 2048
 SMALL = 10
 VMEM_LIMIT = 60 * 1024 * 1024
 END_LIMIT = 16 * 1024 * 1024
@@ -325,17 +325,16 @@
     )(row_counts.reshape(1, 1, 1), features, *small)
 
     near = 1 << (n_grp.bit_length() // 2 - 1)
-    state_parts = [outs[0]] + [swap(outs[d], "row", d) for d in range(1, n_row)]
+    state_parts = [swap(outs[d], "row", d) for d in range(n_row)]
     state_piece = total_of(state_parts)
     county_outs = outs[n_row:]
     from_core = [swap(county_outs[d ^ 1], "row", 1) for d in range(0, n_row, 2)]
     state_piece, *from_core = lax.optimization_barrier((state_piece, *from_core))
     chip_sums = [county_outs[d] + from_core[d // 2] for d in range(2, n_row, 2)]
-    county_parts = [county_outs[0], from_core[0]] + [
+    county_parts = [swap(county_outs[0], "row", 0), from_core[0]] + [
         swap(x, "row", d) for x, d in zip(chip_sums, range(2, n_row, 2))
     ]
-    pairs = [[g + d for d in range(near)] for g in range(0, n_grp, near)]
-    state_piece = lax.psum(state_piece, "grp", axis_index_groups=pairs)
+    state_piece = total_of(gather_by(state_piece, "grp", range(1, near)))
     county_grad, precinct_grad, prior, nation_hot = pl.pallas_call(
         county_end_kernel,
         out_shape=[
@@ -348,8 +347,7 @@
         name="county_totals",
     )(nation_row, state_coef, nation_coef, beta2, *county_parts)
 
-    lines = [list(range(d, n_grp, near)) for d in range(near)]
-    state_piece = lax.psum(state_piece, "grp", axis_index_groups=lines)
+    state_piece = total_of(gather_by(state_piece, "grp", range(near, n_grp, near)))
     gathered = gather_by(state_piece, "row", range(1, n_row))
     state_grad, nation_grad, beta_grad = pl.pallas_call(
         end_kernel,

time: 54.8 us -> 37.2 us (0.68)
  blocking collectives: 27.7 us -> 0 us
  starting transfers between devices: 6.45 us -> 14 us
  waiting for transfers between devices: 4.06 us -> 8.38 us
  local copies, waits for them, and re-layouts: 0.92 us -> 0.02 us
  other arithmetic: 1.7 us -> 0.96 us
    psum x2 -> x0, blocking collectives: 27.7 us -> none  [the longest x1 19.3 us: on_device(): state_piece = lax.psum(state_piece, 'grp', axis_index_groups=lines)]
    ppermute x9 -> x15, starting transfers between devices: 6.45 us -> 14 us  [swap(): return lax.ppermute(x, axis, [(i, i ^ d) for i in range(n)])]
    ppermute x9 -> x15, waiting for transfers between devices: 4.06 us -> 8.38 us  [swap(): return lax.ppermute(x, axis, [(i, i ^ d) for i in range(n)])]
    unnamed x10 -> x8, local copies, waits for them, and re-layouts: 0.92 us -> 0.02 us
    add x1 -> x3, other arithmetic: 0.77 us -> 0.03 us  [total_of(): parts = [sum(parts[i:i + 2][1:], parts[i]) for i in range(0, len(parts), 2)]]
  transfers between devices with their start and end apart: 9 -> 15, of which waited for: 4 -> 6; matrix products, arithmetic and copies ran while one was open for 1% -> 3% of each run, Pallas kernels for 1% -> 2%
where the time goes in v10:
time: 37.2 us; the launch traced here: 36.9 us
  starting transfers between devices  14 us (38%)
  Pallas kernels  12.1 us (33%)
  waiting for transfers between devices  8.38 us (23%)
  between operations  1.46 us (4%)
  other arithmetic  0.96 us (3%)
    ppermute x15, starting transfers between devices, swap(): return lax.ppermute(x, axis, [(i, i ^ d) for i in range(n)])  14 us
    pallas_call x1, Pallas kernels, on_device(): pl.pallas_call(functools.partial(main_kernel, 2 * n_row), in_specs=[pl.Bl...  10.6 us
    ppermute x15, waiting for transfers between devices, swap(): return lax.ppermute(x, axis, [(i, i ^ d) for i in range(n)])  8.38 us
    add x1, other arithmetic, on_device(): chip_sums = [county_outs[d] + from_core[d // 2] for d in range(2, n_row, 2)]  0.93 us
    pallas_call x1, Pallas kernels, on_device(): pl.pallas_call(end_kernel, out_shape=[jax.ShapeDtypeStruct(state_coef.sha...  0.79 us
  transfers between devices with their start and end apart: 15, of which 6 were waited for; matrix products, arithmetic and copies ran while one was open for 3% of the time, Pallas kernels for 2%

profile of v10, /device:TPU:0, one launch (start us, length us, event | category | flops | bytes accessed | tf_op | source)
XLA Modules:
  0.0 36.9 jit_solution(7742297039749544125)
XLA Ops:
  1.4 10.6 %local_sums.1 = (f32[16,512]{1,0:T(8,128)}, f32[16,512]{1,0:T(8,128)}, f32[16,512]{1,0:T(8,128)}, f32[16,512]{1,0:T(8,128)}, f32[72,512]{1,0:T(8,128)}, /*index=...) custom-call(s32[1,1,1]{2,1,0:T(1,128)} %bitcast.10.count_ref, bf16[8192,512]{1,0:T(8,128)(2,1)} %features_ref.1, ...), custom_call_target="tpu_custom_call" | custom-call | tf_op jit(solution)/shard_map/local_sums/pallas_call | solution.py:291
  12.0 0.8 %collective-permute-start.1 = (f32[16,512]{1,0:T(8,128)}, f32[16,512]{1,0:T(8,128)S(1)}, u32[]{:S(2)}, u32[]{:S(2)}) collective-permute-start(f32[16,512]{1,0:T(8,128)} %get-tuple-element.24), channel_id=1, source_target_pairs={{0,0},{1,1},{2,2},{3,3},{4,4},{5,5},{6,6},{7,7},{8,8},{9,9},{10,10... | collective-permute-start | bytes 98312 | tf_op jit(solution)/shard_map/ppermute | solution.py:232
  12.8 0.5 %collective-permute-start.2 = (f32[16,512]{1,0:T(8,128)}, f32[16,512]{1,0:T(8,128)S(1)}, u32[]{:S(2)}, u32[]{:S(2)}) collective-permute-start(f32[16,512]{1,0:T(8,128)} %get-tuple-element.25), channel_id=1, source_target_pairs={{0,1},{1,0},{2,3},{3,2},{4,5},{5,4},{6,7},{7,6},{8,9},{9,8},{10,11... | collective-permute-start | bytes 98312 | tf_op jit(solution)/shard_map/ppermute | solution.py:232
  13.2 2.5 %collective-permute-start.3 = (f32[16,512]{1,0:T(8,128)}, f32[16,512]{1,0:T(8,128)S(1)}, u32[]{:S(2)}, u32[]{:S(2)}) collective-permute-start(f32[16,512]{1,0:T(8,128)} %get-tuple-element.26), channel_id=1, source_target_pairs={{0,2},{1,3},{2,0},{3,1},{4,6},{5,7},{6,4},{7,5},{8,10},{9,11},{10,... | collective-permute-start | bytes 98312 | tf_op jit(solution)/shard_map/ppermute | solution.py:232
  15.7 0.1 collective-permute-start.4
  15.9 0.1 collective-permute-start.5
  16.0 0.0 collective-permute-done.1
  16.0 0.4 %collective-permute-start.6 = (f32[72,512]{1,0:T(8,128)}, f32[72,512]{1,0:T(8,128)S(1)}, u32[]{:S(2)}, u32[]{:S(2)}) collective-permute-start(f32[72,512]{1,0:T(8,128)} %get-tuple-element.29), channel_id=1, source_target_pairs={{0,1},{1,0},{2,3},{3,2},{4,5},{5,4},{6,7},{7,6},{8,9},{9,8},{10,11... | collective-permute-start | bytes 442376 | tf_op jit(solution)/shard_map/ppermute | solution.py:232
  16.4 0.0 collective-permute-done.2
  16.4 1.6 %collective-permute-done.3 = f32[16,512]{1,0:T(8,128)S(1)} collective-permute-done((f32[16,512]{1,0:T(8,128)}, f32[16,512]{1,0:T(8,128)S(1)}, u32[]{:S(2)}, u32[]{:S(2)}) %collective-permute-start.3) | collective-permute-done | bytes 32800 | tf_op jit(solution)/shard_map/ppermute | solution.py:232
  18.0 1.3 %collective-permute-done.4 = f32[16,512]{1,0:T(8,128)S(1)} collective-permute-done((f32[16,512]{1,0:T(8,128)}, f32[16,512]{1,0:T(8,128)S(1)}, u32[]{:S(2)}, u32[]{:S(2)}) %collective-permute-start.4) | collective-permute-done | bytes 32800 | tf_op jit(solution)/shard_map/ppermute | solution.py:232
  19.3 0.0 collective-permute-done.5.refs_1_
  19.3 0.0 collective-permute-done.6
  19.3 1.6 %collective-permute-start.8 = (f32[16,512]{1,0:T(8,128)S(1)}, f32[16,512]{1,0:T(8,128)S(1)}, u32[]{:S(2)}, u32[]{:S(2)}) collective-permute-start(f32[16,512]{1,0:T(8,128)S(1)} %add_add_fusion.1), channel_id=1, source_target_pairs={{0,4},{4,0},{8,12},{12,8},{16,20},{20,16},{24,28},{28,24},{1,5},{5... | collective-permute-start | bytes 98312 | tf_op jit(solution)/shard_map/ppermute | solution.py:232
  20.9 2.4 %collective-permute-done.8 = f32[16,512]{1,0:T(8,128)S(1)} collective-permute-done((f32[16,512]{1,0:T(8,128)S(1)}, f32[16,512]{1,0:T(8,128)S(1)}, u32[]{:S(2)}, u32[]{:S(2)}) %collective-permute-start.8) | collective-permute-done | bytes 32800 | tf_op jit(solution)/shard_map/ppermute | solution.py:232
  23.3 3.6 %collective-permute-start.11 = (f32[16,512]{1,0:T(8,128)S(1)}, f32[16,512]{1,0:T(8,128)S(1)}, u32[]{:S(2)}, u32[]{:S(2)}) collective-permute-start(f32[16,512]{1,0:T(8,128)S(1)} %add.28), channel_id=1, source_target_pairs={{0,24},{4,28},{8,16},{12,20},{16,8},{20,12},{24,0},{28,4},{1,25},{... | collective-permute-start | bytes 98312 | tf_op jit(solution)/shard_map/ppermute | solution.py:232
  26.9 0.0 collective-permute-start.10
  26.9 0.8 %collective-permute-start.9 = (f32[16,512]{1,0:T(8,128)S(1)}, f32[16,512]{1,0:T(8,128)S(1)}, u32[]{:S(2)}, u32[]{:S(2)}) collective-permute-start(f32[16,512]{1,0:T(8,128)S(1)} %add.28), channel_id=1, source_target_pairs={{0,8},{4,12},{8,0},{12,4},{16,24},{20,28},{24,16},{28,20},{1,9},{5... | collective-permute-start | bytes 98312 | tf_op jit(solution)/shard_map/ppermute | solution.py:232
  27.7 0.9 %collective-permute-start = (f32[72,512]{1,0:T(8,128)}, f32[72,512]{1,0:T(8,128)S(1)}, u32[]{:S(2)}, u32[]{:S(2)}) collective-permute-start(f32[72,512]{1,0:T(8,128)} %get-tuple-element.23), channel_id=1, source_target_pairs={{0,0},{1,1},{2,2},{3,3},{4,4},{5,5},{6,6},{7,7},{8,8},{9,9},{10,10... | collective-permute-start | bytes 442376 | tf_op jit(solution)/shard_map/ppermute | solution.py:232
  28.6 0.9 %add.27 = f32[72,512]{1,0:T(8,128)S(1)} add(f32[72,512]{1,0:T(8,128)} %get-tuple-element.31, f32[72,512]{1,0:T(8,128)S(1)} %collective-permute-done.6) | non-fusion elementwise | flops 36864 | bytes 442368 | tf_op jit(solution)/shard_map/add | solution.py:333
  29.5 0.9 %collective-permute-start.7 = (f32[72,512]{1,0:T(8,128)S(1)}, f32[72,512]{1,0:T(8,128)S(1)}, u32[]{:S(2)}, u32[]{:S(2)}) collective-permute-start(f32[72,512]{1,0:T(8,128)S(1)} %add.27), channel_id=1, source_target_pairs={{0,2},{1,3},{2,0},{3,1},{4,6},{5,7},{6,4},{7,5},{8,10},{9,11},{10,... | collective-permute-start | bytes 442376 | tf_op jit(solution)/shard_map/ppermute | solution.py:232
  30.4 0.0 collective-permute-done.11
  30.4 1.3 %collective-permute-done.10 = f32[16,512]{1,0:T(8,128)S(1)} collective-permute-done((f32[16,512]{1,0:T(8,128)S(1)}, f32[16,512]{1,0:T(8,128)S(1)}, u32[]{:S(2)}, u32[]{:S(2)}) %collective-permute-start.10) | collective-permute-done | bytes 32800 | tf_op jit(solution)/shard_map/ppermute | solution.py:232
  31.7 0.0 collective-permute-done.9
  31.7 0.1 collective-permute-start.14
  31.8 0.9 %collective-permute-start.13 = (f32[16,512]{1,0:T(8,128)S(1)}, f32[16,512]{1,0:T(8,128)S(1)}, u32[]{:S(2)}, u32[]{:S(2)}) collective-permute-start(f32[16,512]{1,0:T(8,128)S(1)} %add_add_fusion.refs_0_), channel_id=1, source_target_pairs={{0,2},{1,3},{2,0},{3,1},{4,6},{5,7},{6,4},{7,5},{8,10},{9,11},{10,... | collective-permute-start | bytes 98312 | tf_op jit(solution)/shard_map/ppermute | solution.py:232
  32.7 0.9 %collective-permute-start.12 = (f32[16,512]{1,0:T(8,128)S(1)}, f32[16,512]{1,0:T(8,128)S(1)}, u32[]{:S(2)}, u32[]{:S(2)}) collective-permute-start(f32[16,512]{1,0:T(8,128)S(1)} %add_add_fusion.refs_0_), channel_id=1, source_target_pairs={{0,1},{1,0},{2,3},{3,2},{4,5},{5,4},{6,7},{7,6},{8,9},{9,8},{10,11... | collective-permute-start | bytes 98312 | tf_op jit(solution)/shard_map/ppermute | solution.py:232
  33.6 0.0 collective-permute-done.refs_0_
  33.6 1.1 %collective-permute-done.7.refs_2_ = f32[72,512]{1,0:T(8,128)S(1)} collective-permute-done((f32[72,512]{1,0:T(8,128)S(1)}, f32[72,512]{1,0:T(8,128)S(1)}, u32[]{:S(2)}, u32[]{:S(2)}) %collective-permute-start.7) | collective-permute-done | bytes 147488 | tf_op jit(solution)/shard_map/ppermute | solution.py:232
  34.8 0.7 %county_totals.1 = (f32[64,512]{1,0:T(8,128)}, f32[8,128]{1,0:T(8,128)}, f32[69,512]{1,0:T(8,128)S(1)}, f32[4,64]{1,0:T(4,128)S(1)}) custom-call(s32[1,64]{1,0:T(1,128)S(1)} %bitcast.14, f32[64,512]{1,0:T(8,128)S(1)} %copy-done, f32[4,512]{1,0:T(4,128)S(1)} %copy-done.1, f32[1,512]{1,0:T(1,128)S(1)} %bitcast.12, f32[72,512]{1,0:T(8,128)S(1)} %collective-permute-done.refs_0_, ...), custom_call_target="tpu_custom_call" | custom-call | tf_op jit(solution)/shard_map/county_totals/pallas_call | solution.py:338
  35.5 0.7 %collective-permute-done.13.refs_2_ = f32[16,512]{1,0:T(8,128)S(1)} collective-permute-done((f32[16,512]{1,0:T(8,128)S(1)}, f32[16,512]{1,0:T(8,128)S(1)}, u32[]{:S(2)}, u32[]{:S(2)}) %collective-permute-start.13) | collective-permute-done | bytes 32800 | tf_op jit(solution)/shard_map/ppermute | solution.py:232
  36.1 0.8 %upper_totals.1 = (f32[64,512]{1,0:T(8,128)}, f32[4,512]{1,0:T(4,128)}, f32[1,512]{1,0:T(1,128)}) custom-call(f32[69,512]{1,0:T(8,128)S(1)} %get-tuple-element.35.prior_ref, f32[4,64]{1,0:T(4,128)S(1)} %get-tuple-element.36.hot_ref, f32[16,512]{1,0:T(8,128)S(1)} %add_add_fusion.refs_0_, f32[16,512]{1,0:T(8,128)S(1)} %collective-permute-done.12.refs_1_, ...), custom_call_target="tpu_custom_call" | custom-call | tf_op jit(solution)/shard_map/upper_totals/pallas_call | solution.py:352
  (13 shorter events, 0.1 us)
Async XLA Ops:
  0.6 34.1 %copy-start = (f32[64,512]{1,0:T(8,128)S(1)}, f32[64,512]{1,0:T(8,128)}, u32[]{:S(2)}) copy-start(f32[64,512]{1,0:T(8,128)} %state_ref.1) | copy-start | bytes 393220
  0.6 34.1 %copy-start.1 = (f32[4,512]{1,0:T(4,128)S(1)}, f32[4,512]{1,0:T(4,128)}, u32[]{:S(2)}) copy-start(f32[4,512]{1,0:T(4,128)} %nation_ref.1) | copy-start | bytes 24580
  0.7 34.1 %copy-start.3 = (s32[64]{0:T(128)S(1)}, s32[64]{0:T(128)}, u32[]{:S(2)}) copy-start(s32[64]{0:T(128)} %param.23) | copy-start | bytes 772
  0.7 34.1 %copy-start.2 = (f32[512]{0:T(512)S(1)}, f32[512]{0:T(512)}, u32[]{:S(2)}) copy-start(f32[512]{0:T(512)} %param.16) | copy-start | bytes 6148
  12.0 4.0 %collective-permute-start.1 = (f32[16,512]{1,0:T(8,128)}, f32[16,512]{1,0:T(8,128)S(1)}, u32[]{:S(2)}, u32[]{:S(2)}) collective-permute-start(f32[16,512]{1,0:T(8,128)} %get-tuple-element.24), channel_id=1, source_target_pairs={{0,0},{1,1},{2,2},{3,3},{4,4},{5,5},{6,6},{7,7},{8,8},{9,9},{10,10... | collective-permute-start | bytes 98312 | tf_op jit(solution)/shard_map/ppermute | solution.py:232
  12.8 3.6 %collective-permute-start.2 = (f32[16,512]{1,0:T(8,128)}, f32[16,512]{1,0:T(8,128)S(1)}, u32[]{:S(2)}, u32[]{:S(2)}) collective-permute-start(f32[16,512]{1,0:T(8,128)} %get-tuple-element.25), channel_id=1, source_target_pairs={{0,1},{1,0},{2,3},{3,2},{4,5},{5,4},{6,7},{7,6},{8,9},{9,8},{10,11... | collective-permute-start | bytes 98312 | tf_op jit(solution)/shard_map/ppermute | solution.py:232
  13.2 4.8 %collective-permute-start.3 = (f32[16,512]{1,0:T(8,128)}, f32[16,512]{1,0:T(8,128)S(1)}, u32[]{:S(2)}, u32[]{:S(2)}) collective-permute-start(f32[16,512]{1,0:T(8,128)} %get-tuple-element.26), channel_id=1, source_target_pairs={{0,2},{1,3},{2,0},{3,1},{4,6},{5,7},{6,4},{7,5},{8,10},{9,11},{10,... | collective-permute-start | bytes 98312 | tf_op jit(solution)/shard_map/ppermute | solution.py:232
  15.7 3.6 %collective-permute-start.4 = (f32[16,512]{1,0:T(8,128)}, f32[16,512]{1,0:T(8,128)S(1)}, u32[]{:S(2)}, u32[]{:S(2)}) collective-permute-start(f32[16,512]{1,0:T(8,128)} %get-tuple-element.27), channel_id=1, source_target_pairs={{0,3},{1,2},{2,1},{3,0},{4,7},{5,6},{6,5},{7,4},{8,11},{9,10},{10,... | collective-permute-start | bytes 98312 | tf_op jit(solution)/shard_map/ppermute | solution.py:232
  15.9 3.4 %collective-permute-start.5 = (f32[72,512]{1,0:T(8,128)}, f32[72,512]{1,0:T(8,128)S(1)}, u32[]{:S(2)}, u32[]{:S(2)}) collective-permute-start(f32[72,512]{1,0:T(8,128)} %get-tuple-element.28), channel_id=1, source_target_pairs={{0,1},{1,0},{2,3},{3,2},{4,5},{5,4},{6,7},{7,6},{8,9},{9,8},{10,11... | collective-permute-start | bytes 442376 | tf_op jit(solution)/shard_map/ppermute | solution.py:232
  16.0 3.3 %collective-permute-start.6 = (f32[72,512]{1,0:T(8,128)}, f32[72,512]{1,0:T(8,128)S(1)}, u32[]{:S(2)}, u32[]{:S(2)}) collective-permute-start(f32[72,512]{1,0:T(8,128)} %get-tuple-element.29), channel_id=1, source_target_pairs={{0,1},{1,0},{2,3},{3,2},{4,5},{5,4},{6,7},{7,6},{8,9},{9,8},{10,11... | collective-permute-start | bytes 442376 | tf_op jit(solution)/shard_map/ppermute | solution.py:232
  19.3 4.0 %collective-permute-start.8 = (f32[16,512]{1,0:T(8,128)S(1)}, f32[16,512]{1,0:T(8,128)S(1)}, u32[]{:S(2)}, u32[]{:S(2)}) collective-permute-start(f32[16,512]{1,0:T(8,128)S(1)} %add_add_fusion.1), channel_id=1, source_target_pairs={{0,4},{4,0},{8,12},{12,8},{16,20},{20,16},{24,28},{28,24},{1,5},{5... | collective-permute-start | bytes 98312 | tf_op jit(solution)/shard_map/ppermute | solution.py:232
  23.3 7.1 %collective-permute-start.11 = (f32[16,512]{1,0:T(8,128)S(1)}, f32[16,512]{1,0:T(8,128)S(1)}, u32[]{:S(2)}, u32[]{:S(2)}) collective-permute-start(f32[16,512]{1,0:T(8,128)S(1)} %add.28), channel_id=1, source_target_pairs={{0,24},{4,28},{8,16},{12,20},{16,8},{20,12},{24,0},{28,4},{1,25},{... | collective-permute-start | bytes 98312 | tf_op jit(solution)/shard_map/ppermute | solution.py:232
  26.9 4.8 %collective-permute-start.10 = (f32[16,512]{1,0:T(8,128)S(1)}, f32[16,512]{1,0:T(8,128)S(1)}, u32[]{:S(2)}, u32[]{:S(2)}) collective-permute-start(f32[16,512]{1,0:T(8,128)S(1)} %add.28), channel_id=1, source_target_pairs={{0,16},{4,20},{8,24},{12,28},{16,0},{20,4},{24,8},{28,12},{1,17},{... | collective-permute-start | bytes 98312 | tf_op jit(solution)/shard_map/ppermute | solution.py:232
  26.9 4.8 %collective-permute-start.9 = (f32[16,512]{1,0:T(8,128)S(1)}, f32[16,512]{1,0:T(8,128)S(1)}, u32[]{:S(2)}, u32[]{:S(2)}) collective-permute-start(f32[16,512]{1,0:T(8,128)S(1)} %add.28), channel_id=1, source_target_pairs={{0,8},{4,12},{8,0},{12,4},{16,24},{20,28},{24,16},{28,20},{1,9},{5... | collective-permute-start | bytes 98312 | tf_op jit(solution)/shard_map/ppermute | solution.py:232
  27.7 6.0 %collective-permute-start = (f32[72,512]{1,0:T(8,128)}, f32[72,512]{1,0:T(8,128)S(1)}, u32[]{:S(2)}, u32[]{:S(2)}) collective-permute-start(f32[72,512]{1,0:T(8,128)} %get-tuple-element.23), channel_id=1, source_target_pairs={{0,0},{1,1},{2,2},{3,3},{4,4},{5,5},{6,6},{7,7},{8,8},{9,9},{10,10... | collective-permute-start | bytes 442376 | tf_op jit(solution)/shard_map/ppermute | solution.py:232
  29.5 5.2 %collective-permute-start.7 = (f32[72,512]{1,0:T(8,128)S(1)}, f32[72,512]{1,0:T(8,128)S(1)}, u32[]{:S(2)}, u32[]{:S(2)}) collective-permute-start(f32[72,512]{1,0:T(8,128)S(1)} %add.27), channel_id=1, source_target_pairs={{0,2},{1,3},{2,0},{3,1},{4,6},{5,7},{6,4},{7,5},{8,10},{9,11},{10,... | collective-permute-start | bytes 442376 | tf_op jit(solution)/shard_map/ppermute | solution.py:232
  31.7 3.7 %collective-permute-start.14 = (f32[16,512]{1,0:T(8,128)S(1)}, f32[16,512]{1,0:T(8,128)S(1)}, u32[]{:S(2)}, u32[]{:S(2)}) collective-permute-start(f32[16,512]{1,0:T(8,128)S(1)} %add_add_fusion.refs_0_), channel_id=1, source_target_pairs={{0,3},{1,2},{2,1},{3,0},{4,7},{5,6},{6,5},{7,4},{8,11},{9,10},{10,... | collective-permute-start | bytes 98312 | tf_op jit(solution)/shard_map/ppermute | solution.py:232
  31.8 4.3 %collective-permute-start.13 = (f32[16,512]{1,0:T(8,128)S(1)}, f32[16,512]{1,0:T(8,128)S(1)}, u32[]{:S(2)}, u32[]{:S(2)}) collective-permute-start(f32[16,512]{1,0:T(8,128)S(1)} %add_add_fusion.refs_0_), channel_id=1, source_target_pairs={{0,2},{1,3},{2,0},{3,1},{4,6},{5,7},{6,4},{7,5},{8,10},{9,11},{10,... | collective-permute-start | bytes 98312 | tf_op jit(solution)/shard_map/ppermute | solution.py:232
  32.7 3.4 %collective-permute-start.12 = (f32[16,512]{1,0:T(8,128)S(1)}, f32[16,512]{1,0:T(8,128)S(1)}, u32[]{:S(2)}, u32[]{:S(2)}) collective-permute-start(f32[16,512]{1,0:T(8,128)S(1)} %add_add_fusion.refs_0_), channel_id=1, source_target_pairs={{0,1},{1,0},{2,3},{3,2},{4,5},{5,4},{6,7},{7,6},{8,9},{9,8},{10,11... | collective-permute-start | bytes 98312 | tf_op jit(solution)/shard_map/ppermute | solution.py:232

commit v11 on v10

--- a/solution.py
+++ b/solution.py
@@ -9,6 +9,7 @@
 
 LANES = 128
 ROW_STEP = 2048
+PIECE = 1024
 SMALL = 10
 VMEM_LIMIT = 60 * 1024 * 1024
 END_LIMIT = 16 * 1024 * 1024
@@ -80,8 +81,22 @@
     size = precinct_ref.shape[2]
 
     def fetch(j):
-        rows = pl.ds(pl.multiple_of(j * size, size), size)
-        return pltpu.make_async_copy(features_ref.at[rows], feats.at[rows], sems.at[j])
+        copies = []
+        for k in range(size // PIECE):
+            piece = j * (size // PIECE) + k
+            rows = pl.ds(pl.multiple_of(piece * PIECE, PIECE), PIECE)
+            copies.append(
+                pltpu.make_async_copy(features_ref.at[rows], feats.at[rows], sems.at[piece])
+            )
+        return copies
+
+    def start(j):
+        for copy in fetch(j):
+            copy.start()
+
+    def wait(j):
+        for copy in fetch(j):
+            copy.wait()
 
     small_copies = [
         pltpu.make_async_copy(source, target, small_sems.at[k])
@@ -89,12 +104,10 @@
     ]
     for copy in small_copies:
         copy.start()
-    for j in range(2):
-        fetch(j).start()
+    start(0)
     for copy in small_copies:
         copy.wait()
-    for j in range(2, 4):
-        fetch(j).start()
+    start(1)
 
     states = county_state_ref[lax.axis_index("grp")]
     state_hot = (iota_rows(n_states) == states).astype(F32).astype(BF16)
@@ -141,21 +154,23 @@
             by_high, low_hot, (((1,), (1,)), ((), ())), preferred_element_type=F32
         )
 
-    fetch(0).wait()
+    wait(0)
     score(0, 0)
-    fetch(1).wait()
+    wait(1)
+    start(2)
+    start(3)
     score(1, 1)
     residue(0, 0)
 
     def body(t, carry):
         j = 2 * t
-        fetch(j).wait()
-        fetch(j + 1).wait()
+        wait(j)
+        wait(j + 1)
 
         @pl.when(j + 2 < chunks)
         def _():
-            fetch(j + 2).start()
-            fetch(j + 3).start()
+            start(j + 2)
+            start(j + 3)
 
         residue(j - 1, 1)
         score(j, 0)
@@ -317,7 +332,7 @@
         + [pltpu.VMEM((share + n_hi, p_size), F32)] * n_row
         + [
             pltpu.SemaphoreType.DMA((SMALL,)),
-            pltpu.SemaphoreType.DMA((steps,)),
+            pltpu.SemaphoreType.DMA((rows_here // PIECE,)),
             pltpu.SemaphoreType.DMA((2 * n_row,)),
         ],
         compiler_params=pltpu.CompilerParams(vmem_limit_bytes=VMEM_LIMIT),
@@ -325,16 +340,17 @@
     )(row_counts.reshape(1, 1, 1), features, *small)
 
     near = 1 << (n_grp.bit_length() // 2 - 1)
-    state_parts = [swap(outs[d], "row", d) for d in range(n_row)]
-    state_piece = total_of(state_parts)
+    own_sum = lax.optimization_barrier(outs[0] + swap(outs[1], "row", 1))
+    state_piece = total_of([swap(outs[d], "row", d) for d in range(2, n_row)]) + own_sum
     county_outs = outs[n_row:]
     from_core = [swap(county_outs[d ^ 1], "row", 1) for d in range(0, n_row, 2)]
     state_piece, *from_core = lax.optimization_barrier((state_piece, *from_core))
     chip_sums = [county_outs[d] + from_core[d // 2] for d in range(2, n_row, 2)]
-    county_parts = [swap(county_outs[0], "row", 0), from_core[0]] + [
+    state_piece = total_of(gather_by(state_piece, "grp", range(1, near)))
+    state_piece, *chip_sums = lax.optimization_barrier((state_piece, *chip_sums))
+    county_parts = [county_outs[0], from_core[0]] + [
         swap(x, "row", d) for x, d in zip(chip_sums, range(2, n_row, 2))
     ]
-    state_piece = total_of(gather_by(state_piece, "grp", range(1, near)))
     county_grad, precinct_grad, prior, nation_hot = pl.pallas_call(
         county_end_kernel,
         out_shape=[

time: 37.2 us -> 37.4 us (level)
  starting transfers between devices: 14 us -> 12.2 us
  Pallas kernels: 12.1 us -> 13 us
  local copies, waits for them, and re-layouts: 0.02 us -> 0.92 us
  other arithmetic: 0.96 us -> 1.72 us
  waiting for transfers between devices: 8.38 us -> 7.8 us
    ppermute x15 -> x13, starting transfers between devices: 14 us -> 12.2 us  [swap(): return lax.ppermute(x, axis, [(i, i ^ d) for i in range(n)])]
    pallas_call x1, Pallas kernels: 10.6 us -> 11.5 us  [on_device(): pl.pallas_call(functools.partial(main_kernel, 2 * n_row), in_specs=[pl.Bl...]
    unnamed x8 -> x10, local copies, waits for them, and re-layouts: 0.02 us -> 0.92 us
    add x0 -> x2, other arithmetic: none -> 0.77 us  [the longest x1 0.76 us: on_device(): own_sum = lax.optimization_barrier(outs[0] + swap(outs[1], 'row', 1))]
    ppermute x15 -> x13, waiting for transfers between devices: 8.38 us -> 7.8 us  [swap(): return lax.ppermute(x, axis, [(i, i ^ d) for i in range(n)])]
  transfers between devices with their start and end apart: 15 -> 13, of which waited for: 6 -> 6; matrix products, arithmetic and copies ran while one was open for 3% -> 5% of each run, Pallas kernels for 2% -> 2%
where the time goes in v11:
time: 37.4 us; the launch traced here: 37.1 us
  Pallas kernels  13 us (35%)
  starting transfers between devices  12.2 us (33%)
  waiting for transfers between devices  7.8 us (21%)
  other arithmetic  1.72 us (5%)
  between operations  1.43 us (4%)
  local copies, waits for them, and re-layouts  0.92 us (2%)
    ppermute x13, starting transfers between devices, swap(): return lax.ppermute(x, axis, [(i, i ^ d) for i in range(n)])  12.2 us
    pallas_call x1, Pallas kernels, on_device(): pl.pallas_call(functools.partial(main_kernel, 2 * n_row), in_specs=[pl.Bl...  11.5 us
    ppermute x13, waiting for transfers between devices, swap(): return lax.ppermute(x, axis, [(i, i ^ d) for i in range(n)])  7.8 us
    add x1, other arithmetic, on_device(): chip_sums = [county_outs[d] + from_core[d // 2] for d in range(2, n_row, 2)]  0.93 us
    unnamed x10, local copies, waits for them, and re-layouts  0.92 us
    pallas_call x1, Pallas kernels, on_device(): pl.pallas_call(end_kernel, out_shape=[jax.ShapeDtypeStruct(state_coef.sha...  0.79 us
    add x1, other arithmetic, on_device(): own_sum = lax.optimization_barrier(outs[0] + swap(outs[1], 'row', 1))  0.76 us
  transfers between devices with their start and end apart: 13, of which 6 were waited for; matrix products, arithmetic and copies ran while one was open for 5% of the time, Pallas kernels for 2%

profile of v11, /device:TPU:0, one launch (start us, length us, event | category | flops | bytes accessed | tf_op | source)
XLA Modules:
  0.0 37.1 jit_solution(12180697691656106795)
XLA Ops:
  1.4 11.5 %local_sums.1 = (f32[16,512]{1,0:T(8,128)}, f32[16,512]{1,0:T(8,128)}, f32[16,512]{1,0:T(8,128)}, f32[16,512]{1,0:T(8,128)}, f32[72,512]{1,0:T(8,128)}, /*index=...) custom-call(s32[1,1,1]{2,1,0:T(1,128)} %bitcast.10.count_ref, bf16[8192,512]{1,0:T(8,128)(2,1)} %features_ref.1, ...), custom_call_target="tpu_custom_call" | custom-call | tf_op jit(solution)/shard_map/local_sums/pallas_call | solution.py:306
  12.9 0.5 %collective-permute-start.2 = (f32[16,512]{1,0:T(8,128)}, f32[16,512]{1,0:T(8,128)S(1)}, u32[]{:S(2)}, u32[]{:S(2)}) collective-permute-start(f32[16,512]{1,0:T(8,128)} %get-tuple-element.29), channel_id=1, source_target_pairs={{0,1},{1,0},{2,3},{3,2},{4,5},{5,4},{6,7},{7,6},{8,9},{9,8},{10,11... | collective-permute-start | bytes 98312 | tf_op jit(solution)/shard_map/ppermute | solution.py:247
  13.4 2.6 %collective-permute-start = (f32[16,512]{1,0:T(8,128)}, f32[16,512]{1,0:T(8,128)S(1)}, u32[]{:S(2)}, u32[]{:S(2)}) collective-permute-start(f32[16,512]{1,0:T(8,128)} %get-tuple-element.26), channel_id=1, source_target_pairs={{0,2},{1,3},{2,0},{3,1},{4,6},{5,7},{6,4},{7,5},{8,10},{9,11},{10,... | collective-permute-start | bytes 98312 | tf_op jit(solution)/shard_map/ppermute | solution.py:247
  16.0 0.1 collective-permute-start.1
  16.0 0.1 collective-permute-start.3
  16.2 0.4 %collective-permute-start.4 = (f32[72,512]{1,0:T(8,128)}, f32[72,512]{1,0:T(8,128)S(1)}, u32[]{:S(2)}, u32[]{:S(2)}) collective-permute-start(f32[72,512]{1,0:T(8,128)} %get-tuple-element.31), channel_id=1, source_target_pairs={{0,1},{1,0},{2,3},{3,2},{4,5},{5,4},{6,7},{7,6},{8,9},{9,8},{10,11... | collective-permute-start | bytes 442376 | tf_op jit(solution)/shard_map/ppermute | solution.py:247
  16.5 0.0 collective-permute-done.2
  16.6 0.8 %add.25 = f32[16,512]{1,0:T(8,128)S(1)} add(f32[16,512]{1,0:T(8,128)} %get-tuple-element.28, f32[16,512]{1,0:T(8,128)S(1)} %collective-permute-done.2) | non-fusion elementwise | flops 8192 | bytes 98304 | tf_op jit(solution)/shard_map/add | solution.py:343
  17.3 0.8 %collective-permute-done = f32[16,512]{1,0:T(8,128)S(1)} collective-permute-done((f32[16,512]{1,0:T(8,128)}, f32[16,512]{1,0:T(8,128)S(1)}, u32[]{:S(2)}, u32[]{:S(2)}) %collective-permute-start) | collective-permute-done | bytes 32800 | tf_op jit(solution)/shard_map/ppermute | solution.py:247
  18.2 1.4 %collective-permute-done.1 = f32[16,512]{1,0:T(8,128)S(1)} collective-permute-done((f32[16,512]{1,0:T(8,128)}, f32[16,512]{1,0:T(8,128)S(1)}, u32[]{:S(2)}, u32[]{:S(2)}) %collective-permute-start.1) | collective-permute-done | bytes 32800 | tf_op jit(solution)/shard_map/ppermute | solution.py:247
  19.5 0.0 collective-permute-done.3.refs_1_
  19.5 0.0 collective-permute-done.4
  19.6 1.6 %collective-permute-start.5 = (f32[16,512]{1,0:T(8,128)S(1)}, f32[16,512]{1,0:T(8,128)S(1)}, u32[]{:S(2)}, u32[]{:S(2)}) collective-permute-start(f32[16,512]{1,0:T(8,128)S(1)} %add_add_fusion.1), channel_id=1, source_target_pairs={{0,4},{4,0},{8,12},{12,8},{16,20},{20,16},{24,28},{28,24},{1,5},{5... | collective-permute-start | bytes 98312 | tf_op jit(solution)/shard_map/ppermute | solution.py:247
  21.1 0.9 %add.28 = f32[72,512]{1,0:T(8,128)S(1)} add(f32[72,512]{1,0:T(8,128)} %get-tuple-element.34, f32[72,512]{1,0:T(8,128)S(1)} %collective-permute-done.4) | non-fusion elementwise | flops 36864 | bytes 442368 | tf_op jit(solution)/shard_map/add | solution.py:348
  22.1 1.5 %collective-permute-done.5 = f32[16,512]{1,0:T(8,128)S(1)} collective-permute-done((f32[16,512]{1,0:T(8,128)S(1)}, f32[16,512]{1,0:T(8,128)S(1)}, u32[]{:S(2)}, u32[]{:S(2)}) %collective-permute-start.5) | collective-permute-done | bytes 32800 | tf_op jit(solution)/shard_map/ppermute | solution.py:247
  23.5 2.6 %collective-permute-start.8 = (f32[16,512]{1,0:T(8,128)S(1)}, f32[16,512]{1,0:T(8,128)S(1)}, u32[]{:S(2)}, u32[]{:S(2)}) collective-permute-start(f32[16,512]{1,0:T(8,128)S(1)} %add.27), channel_id=1, source_target_pairs={{0,16},{4,20},{8,24},{12,28},{16,0},{20,4},{24,8},{28,12},{1,17},{... | collective-permute-start | bytes 98312 | tf_op jit(solution)/shard_map/ppermute | solution.py:247
  26.1 1.4 %collective-permute-start.9 = (f32[16,512]{1,0:T(8,128)S(1)}, f32[16,512]{1,0:T(8,128)S(1)}, u32[]{:S(2)}, u32[]{:S(2)}) collective-permute-start(f32[16,512]{1,0:T(8,128)S(1)} %add.27), channel_id=1, source_target_pairs={{0,24},{4,28},{8,16},{12,20},{16,8},{20,12},{24,0},{28,4},{1,25},{... | collective-permute-start | bytes 98312 | tf_op jit(solution)/shard_map/ppermute | solution.py:247
  27.5 0.2 collective-permute-start.7
  27.7 0.8 %collective-permute-start.6 = (f32[72,512]{1,0:T(8,128)S(1)}, f32[72,512]{1,0:T(8,128)S(1)}, u32[]{:S(2)}, u32[]{:S(2)}) collective-permute-start(f32[72,512]{1,0:T(8,128)S(1)} %add.28), channel_id=1, source_target_pairs={{0,2},{1,3},{2,0},{3,1},{4,6},{5,7},{6,4},{7,5},{8,10},{9,11},{10,... | collective-permute-start | bytes 442376 | tf_op jit(solution)/shard_map/ppermute | solution.py:247
  28.6 0.0 collective-permute-done.8
  28.6 3.3 %collective-permute-done.9 = f32[16,512]{1,0:T(8,128)S(1)} collective-permute-done((f32[16,512]{1,0:T(8,128)S(1)}, f32[16,512]{1,0:T(8,128)S(1)}, u32[]{:S(2)}, u32[]{:S(2)}) %collective-permute-start.9) | collective-permute-done | bytes 32800 | tf_op jit(solution)/shard_map/ppermute | solution.py:247
  31.8 0.0 collective-permute-done.7
  31.9 0.1 collective-permute-start.10
  31.9 1.0 %collective-permute-start.11 = (f32[16,512]{1,0:T(8,128)S(1)}, f32[16,512]{1,0:T(8,128)S(1)}, u32[]{:S(2)}, u32[]{:S(2)}) collective-permute-start(f32[16,512]{1,0:T(8,128)S(1)} %add_add_fusion.refs_0_), channel_id=1, source_target_pairs={{0,2},{1,3},{2,0},{3,1},{4,6},{5,7},{6,4},{7,5},{8,10},{9,11},{10,... | collective-permute-start | bytes 98312 | tf_op jit(solution)/shard_map/ppermute | solution.py:247
  32.9 0.9 %collective-permute-start.12 = (f32[16,512]{1,0:T(8,128)S(1)}, f32[16,512]{1,0:T(8,128)S(1)}, u32[]{:S(2)}, u32[]{:S(2)}) collective-permute-start(f32[16,512]{1,0:T(8,128)S(1)} %add_add_fusion.refs_0_), channel_id=1, source_target_pairs={{0,3},{1,2},{2,1},{3,0},{4,7},{5,6},{6,5},{7,4},{8,11},{9,10},{10,... | collective-permute-start | bytes 98312 | tf_op jit(solution)/shard_map/ppermute | solution.py:247
  33.8 0.0 collective-permute-done.6.refs_2_
  33.8 0.9 %copy-done.1 = f32[72,512]{1,0:T(8,128)S(1)} copy-done((f32[72,512]{1,0:T(8,128)S(1)}, f32[72,512]{1,0:T(8,128)}, u32[]{:S(2)}) %copy-start.1) | copy-done | bytes 147480
  34.7 0.7 %county_totals.1 = (f32[64,512]{1,0:T(8,128)}, f32[8,128]{1,0:T(8,128)}, f32[69,512]{1,0:T(8,128)S(1)}, f32[4,64]{1,0:T(4,128)S(1)}) custom-call(s32[1,64]{1,0:T(1,128)S(1)} %bitcast.14, f32[64,512]{1,0:T(8,128)S(1)} %copy-done, f32[4,512]{1,0:T(4,128)S(1)} %copy-done.2, f32[1,512]{1,0:T(1,128)S(1)} %bitcast.12, f32[72,512]{1,0:T(8,128)S(1)} %copy-done.1, ...), custom_call_target="tpu_custom_call" | custom-call | tf_op jit(solution)/shard_map/county_totals/pallas_call | solution.py:354
  35.4 0.0 collective-permute-done.10.refs_1_
  35.4 0.5 %collective-permute-done.11.refs_2_ = f32[16,512]{1,0:T(8,128)S(1)} collective-permute-done((f32[16,512]{1,0:T(8,128)S(1)}, f32[16,512]{1,0:T(8,128)S(1)}, u32[]{:S(2)}, u32[]{:S(2)}) %collective-permute-start.11) | collective-permute-done | bytes 32800 | tf_op jit(solution)/shard_map/ppermute | solution.py:247
  35.9 0.4 collective-permute-done.12.refs_3_
  36.3 0.8 %upper_totals.1 = (f32[64,512]{1,0:T(8,128)}, f32[4,512]{1,0:T(4,128)}, f32[1,512]{1,0:T(1,128)}) custom-call(f32[69,512]{1,0:T(8,128)S(1)} %get-tuple-element.39.prior_ref, f32[4,64]{1,0:T(4,128)S(1)} %get-tuple-element.40.hot_ref, f32[16,512]{1,0:T(8,128)S(1)} %add_add_fusion.refs_0_, f32[16,512]{1,0:T(8,128)S(1)} %collective-permute-done.10.refs_1_, ...), custom_call_target="tpu_custom_call" | custom-call | tf_op jit(solution)/shard_map/upper_totals/pallas_call | solution.py:368
  (12 shorter events, 0.0 us)
Async XLA Ops:
  0.6 33.2 %copy-start.4 = (s32[64]{0:T(128)S(1)}, s32[64]{0:T(128)}, u32[]{:S(2)}) copy-start(s32[64]{0:T(128)} %param.23) | copy-start | bytes 772
  0.6 33.2 %copy-start = (f32[64,512]{1,0:T(8,128)S(1)}, f32[64,512]{1,0:T(8,128)}, u32[]{:S(2)}) copy-start(f32[64,512]{1,0:T(8,128)} %state_ref.1) | copy-start | bytes 393220
  0.7 33.2 %copy-start.2 = (f32[4,512]{1,0:T(4,128)S(1)}, f32[4,512]{1,0:T(4,128)}, u32[]{:S(2)}) copy-start(f32[4,512]{1,0:T(4,128)} %nation_ref.1) | copy-start | bytes 24580
  0.7 33.2 %copy-start.3 = (f32[512]{0:T(512)S(1)}, f32[512]{0:T(512)}, u32[]{:S(2)}) copy-start(f32[512]{0:T(512)} %param.16) | copy-start | bytes 6148
  12.9 3.7 %collective-permute-start.2 = (f32[16,512]{1,0:T(8,128)}, f32[16,512]{1,0:T(8,128)S(1)}, u32[]{:S(2)}, u32[]{:S(2)}) collective-permute-start(f32[16,512]{1,0:T(8,128)} %get-tuple-element.29), channel_id=1, source_target_pairs={{0,1},{1,0},{2,3},{3,2},{4,5},{5,4},{6,7},{7,6},{8,9},{9,8},{10,11... | collective-permute-start | bytes 98312 | tf_op jit(solution)/shard_map/ppermute | solution.py:247
  13.4 4.8 %collective-permute-start = (f32[16,512]{1,0:T(8,128)}, f32[16,512]{1,0:T(8,128)S(1)}, u32[]{:S(2)}, u32[]{:S(2)}) collective-permute-start(f32[16,512]{1,0:T(8,128)} %get-tuple-element.26), channel_id=1, source_target_pairs={{0,2},{1,3},{2,0},{3,1},{4,6},{5,7},{6,4},{7,5},{8,10},{9,11},{10,... | collective-permute-start | bytes 98312 | tf_op jit(solution)/shard_map/ppermute | solution.py:247
  16.0 3.6 %collective-permute-start.1 = (f32[16,512]{1,0:T(8,128)}, f32[16,512]{1,0:T(8,128)S(1)}, u32[]{:S(2)}, u32[]{:S(2)}) collective-permute-start(f32[16,512]{1,0:T(8,128)} %get-tuple-element.27), channel_id=1, source_target_pairs={{0,3},{1,2},{2,1},{3,0},{4,7},{5,6},{6,5},{7,4},{8,11},{9,10},{10,... | collective-permute-start | bytes 98312 | tf_op jit(solution)/shard_map/ppermute | solution.py:247
  16.0 3.5 %collective-permute-start.3 = (f32[72,512]{1,0:T(8,128)}, f32[72,512]{1,0:T(8,128)S(1)}, u32[]{:S(2)}, u32[]{:S(2)}) collective-permute-start(f32[72,512]{1,0:T(8,128)} %get-tuple-element.30), channel_id=1, source_target_pairs={{0,1},{1,0},{2,3},{3,2},{4,5},{5,4},{6,7},{7,6},{8,9},{9,8},{10,11... | collective-permute-start | bytes 442376 | tf_op jit(solution)/shard_map/ppermute | solution.py:247
  16.2 3.4 %collective-permute-start.4 = (f32[72,512]{1,0:T(8,128)}, f32[72,512]{1,0:T(8,128)S(1)}, u32[]{:S(2)}, u32[]{:S(2)}) collective-permute-start(f32[72,512]{1,0:T(8,128)} %get-tuple-element.31), channel_id=1, source_target_pairs={{0,1},{1,0},{2,3},{3,2},{4,5},{5,4},{6,7},{7,6},{8,9},{9,8},{10,11... | collective-permute-start | bytes 442376 | tf_op jit(solution)/shard_map/ppermute | solution.py:247
  19.6 4.0 %collective-permute-start.5 = (f32[16,512]{1,0:T(8,128)S(1)}, f32[16,512]{1,0:T(8,128)S(1)}, u32[]{:S(2)}, u32[]{:S(2)}) collective-permute-start(f32[16,512]{1,0:T(8,128)S(1)} %add_add_fusion.1), channel_id=1, source_target_pairs={{0,4},{4,0},{8,12},{12,8},{16,20},{20,16},{24,28},{28,24},{1,5},{5... | collective-permute-start | bytes 98312 | tf_op jit(solution)/shard_map/ppermute | solution.py:247
  23.5 5.1 %collective-permute-start.8 = (f32[16,512]{1,0:T(8,128)S(1)}, f32[16,512]{1,0:T(8,128)S(1)}, u32[]{:S(2)}, u32[]{:S(2)}) collective-permute-start(f32[16,512]{1,0:T(8,128)S(1)} %add.27), channel_id=1, source_target_pairs={{0,16},{4,20},{8,24},{12,28},{16,0},{20,4},{24,8},{28,12},{1,17},{... | collective-permute-start | bytes 98312 | tf_op jit(solution)/shard_map/ppermute | solution.py:247
  26.1 5.7 %collective-permute-start.9 = (f32[16,512]{1,0:T(8,128)S(1)}, f32[16,512]{1,0:T(8,128)S(1)}, u32[]{:S(2)}, u32[]{:S(2)}) collective-permute-start(f32[16,512]{1,0:T(8,128)S(1)} %add.27), channel_id=1, source_target_pairs={{0,24},{4,28},{8,16},{12,20},{16,8},{20,12},{24,0},{28,4},{1,25},{... | collective-permute-start | bytes 98312 | tf_op jit(solution)/shard_map/ppermute | solution.py:247
  27.5 4.3 %collective-permute-start.7 = (f32[16,512]{1,0:T(8,128)S(1)}, f32[16,512]{1,0:T(8,128)S(1)}, u32[]{:S(2)}, u32[]{:S(2)}) collective-permute-start(f32[16,512]{1,0:T(8,128)S(1)} %add.27), channel_id=1, source_target_pairs={{0,8},{4,12},{8,0},{12,4},{16,24},{20,28},{24,16},{28,20},{1,9},{5... | collective-permute-start | bytes 98312 | tf_op jit(solution)/shard_map/ppermute | solution.py:247
  27.7 6.1 %collective-permute-start.6 = (f32[72,512]{1,0:T(8,128)S(1)}, f32[72,512]{1,0:T(8,128)S(1)}, u32[]{:S(2)}, u32[]{:S(2)}) collective-permute-start(f32[72,512]{1,0:T(8,128)S(1)} %add.28), channel_id=1, source_target_pairs={{0,2},{1,3},{2,0},{3,1},{4,6},{5,7},{6,4},{7,5},{8,10},{9,11},{10,... | collective-permute-start | bytes 442376 | tf_op jit(solution)/shard_map/ppermute | solution.py:247
  31.9 3.6 %collective-permute-start.10 = (f32[16,512]{1,0:T(8,128)S(1)}, f32[16,512]{1,0:T(8,128)S(1)}, u32[]{:S(2)}, u32[]{:S(2)}) collective-permute-start(f32[16,512]{1,0:T(8,128)S(1)} %add_add_fusion.refs_0_), channel_id=1, source_target_pairs={{0,1},{1,0},{2,3},{3,2},{4,5},{5,4},{6,7},{7,6},{8,9},{9,8},{10,11... | collective-permute-start | bytes 98312 | tf_op jit(solution)/shard_map/ppermute | solution.py:247
  31.9 4.0 %collective-permute-start.11 = (f32[16,512]{1,0:T(8,128)S(1)}, f32[16,512]{1,0:T(8,128)S(1)}, u32[]{:S(2)}, u32[]{:S(2)}) collective-permute-start(f32[16,512]{1,0:T(8,128)S(1)} %add_add_fusion.refs_0_), channel_id=1, source_target_pairs={{0,2},{1,3},{2,0},{3,1},{4,6},{5,7},{6,4},{7,5},{8,10},{9,11},{10,... | collective-permute-start | bytes 98312 | tf_op jit(solution)/shard_map/ppermute | solution.py:247
  32.9 3.4 %collective-permute-start.12 = (f32[16,512]{1,0:T(8,128)S(1)}, f32[16,512]{1,0:T(8,128)S(1)}, u32[]{:S(2)}, u32[]{:S(2)}) collective-permute-start(f32[16,512]{1,0:T(8,128)S(1)} %add_add_fusion.refs_0_), channel_id=1, source_target_pairs={{0,3},{1,2},{2,1},{3,0},{4,7},{5,6},{6,5},{7,4},{8,11},{9,10},{10,... | collective-permute-start | bytes 98312 | tf_op jit(solution)/shard_map/ppermute | solution.py:247
  33.8 0.9 %copy-start.1 = (f32[72,512]{1,0:T(8,128)S(1)}, f32[72,512]{1,0:T(8,128)}, u32[]{:S(2)}) copy-start(f32[72,512]{1,0:T(8,128)} %get-tuple-element.25.refs_0_) | copy-start | bytes 442372

commit v12 on v10

--- a/solution.py
+++ b/solution.py
@@ -325,16 +325,17 @@
     )(row_counts.reshape(1, 1, 1), features, *small)
 
     near = 1 << (n_grp.bit_length() // 2 - 1)
-    state_parts = [swap(outs[d], "row", d) for d in range(n_row)]
-    state_piece = total_of(state_parts)
+    own_sum = lax.optimization_barrier(outs[0] + swap(outs[1], "row", 1))
+    state_piece = total_of([swap(outs[d], "row", d) for d in range(2, n_row)]) + own_sum
     county_outs = outs[n_row:]
     from_core = [swap(county_outs[d ^ 1], "row", 1) for d in range(0, n_row, 2)]
     state_piece, *from_core = lax.optimization_barrier((state_piece, *from_core))
     chip_sums = [county_outs[d] + from_core[d // 2] for d in range(2, n_row, 2)]
-    county_parts = [swap(county_outs[0], "row", 0), from_core[0]] + [
+    state_piece = total_of(gather_by(state_piece, "grp", range(1, near)))
+    state_piece, *chip_sums = lax.optimization_barrier((state_piece, *chip_sums))
+    county_parts = [county_outs[0], from_core[0]] + [
         swap(x, "row", d) for x, d in zip(chip_sums, range(2, n_row, 2))
     ]
-    state_piece = total_of(gather_by(state_piece, "grp", range(1, near)))
     county_grad, precinct_grad, prior, nation_hot = pl.pallas_call(
         county_end_kernel,
         out_shape=[

time: 37.2 us -> 36.5 us (0.981)
  starting transfers between devices: 14 us -> 12.2 us
  local copies, waits for them, and re-layouts: 0.02 us -> 0.92 us
  other arithmetic: 0.96 us -> 1.72 us
  waiting for transfers between devices: 8.38 us -> 7.92 us
    ppermute x15 -> x13, starting transfers between devices: 14 us -> 12.2 us  [swap(): return lax.ppermute(x, axis, [(i, i ^ d) for i in range(n)])]
    unnamed x8 -> x10, local copies, waits for them, and re-layouts: 0.02 us -> 0.92 us
    add x0 -> x2, other arithmetic: none -> 0.77 us  [the longest x1 0.76 us: on_device(): own_sum = lax.optimization_barrier(outs[0] + swap(outs[1], 'row', 1))]
    ppermute x15 -> x13, waiting for transfers between devices: 8.38 us -> 7.92 us  [swap(): return lax.ppermute(x, axis, [(i, i ^ d) for i in range(n)])]
  transfers between devices with their start and end apart: 15 -> 13, of which waited for: 6 -> 6; matrix products, arithmetic and copies ran while one was open for 3% -> 5% of each run, Pallas kernels for 2% -> 2%
where the time goes in v12:
time: 36.5 us; the launch traced here: 36.2 us
  starting transfers between devices  12.2 us (33%)
  Pallas kernels  12 us (33%)
  waiting for transfers between devices  7.92 us (22%)
  other arithmetic  1.72 us (5%)
  between operations  1.43 us (4%)
  local copies, waits for them, and re-layouts  0.92 us (3%)
    ppermute x13, starting transfers between devices, swap(): return lax.ppermute(x, axis, [(i, i ^ d) for i in range(n)])  12.2 us
    pallas_call x1, Pallas kernels, on_device(): pl.pallas_call(functools.partial(main_kernel, 2 * n_row), in_specs=[pl.Bl...  10.6 us
    ppermute x13, waiting for transfers between devices, swap(): return lax.ppermute(x, axis, [(i, i ^ d) for i in range(n)])  7.92 us
    add x1, other arithmetic, on_device(): chip_sums = [county_outs[d] + from_core[d // 2] for d in range(2, n_row, 2)]  0.93 us
    unnamed x10, local copies, waits for them, and re-layouts  0.92 us
    pallas_call x1, Pallas kernels, on_device(): pl.pallas_call(end_kernel, out_shape=[jax.ShapeDtypeStruct(state_coef.sha...  0.79 us
    add x1, other arithmetic, on_device(): own_sum = lax.optimization_barrier(outs[0] + swap(outs[1], 'row', 1))  0.76 us
  transfers between devices with their start and end apart: 13, of which 6 were waited for; matrix products, arithmetic and copies ran while one was open for 5% of the time, Pallas kernels for 2%

profile of v12, /device:TPU:0, one launch (start us, length us, event | category | flops | bytes accessed | tf_op | source)
XLA Modules:
  0.0 36.2 jit_solution(4186678350491998212)
XLA Ops:
  1.4 10.6 %local_sums.1 = (f32[16,512]{1,0:T(8,128)}, f32[16,512]{1,0:T(8,128)}, f32[16,512]{1,0:T(8,128)}, f32[16,512]{1,0:T(8,128)}, f32[72,512]{1,0:T(8,128)}, /*index=...) custom-call(s32[1,1,1]{2,1,0:T(1,128)} %bitcast.10.count_ref, bf16[8192,512]{1,0:T(8,128)(2,1)} %features_ref.1, ...), custom_call_target="tpu_custom_call" | custom-call | tf_op jit(solution)/shard_map/local_sums/pallas_call | solution.py:291
  11.9 0.5 %collective-permute-start.2 = (f32[16,512]{1,0:T(8,128)}, f32[16,512]{1,0:T(8,128)S(1)}, u32[]{:S(2)}, u32[]{:S(2)}) collective-permute-start(f32[16,512]{1,0:T(8,128)} %get-tuple-element.29), channel_id=1, source_target_pairs={{0,1},{1,0},{2,3},{3,2},{4,5},{5,4},{6,7},{7,6},{8,9},{9,8},{10,11... | collective-permute-start | bytes 98312 | tf_op jit(solution)/shard_map/ppermute | solution.py:232
  12.5 2.6 %collective-permute-start = (f32[16,512]{1,0:T(8,128)}, f32[16,512]{1,0:T(8,128)S(1)}, u32[]{:S(2)}, u32[]{:S(2)}) collective-permute-start(f32[16,512]{1,0:T(8,128)} %get-tuple-element.26), channel_id=1, source_target_pairs={{0,2},{1,3},{2,0},{3,1},{4,6},{5,7},{6,4},{7,5},{8,10},{9,11},{10,... | collective-permute-start | bytes 98312 | tf_op jit(solution)/shard_map/ppermute | solution.py:232
  15.0 0.1 collective-permute-start.1
  15.1 0.1 collective-permute-start.3
  15.3 0.4 %collective-permute-start.4 = (f32[72,512]{1,0:T(8,128)}, f32[72,512]{1,0:T(8,128)S(1)}, u32[]{:S(2)}, u32[]{:S(2)}) collective-permute-start(f32[72,512]{1,0:T(8,128)} %get-tuple-element.31), channel_id=1, source_target_pairs={{0,1},{1,0},{2,3},{3,2},{4,5},{5,4},{6,7},{7,6},{8,9},{9,8},{10,11... | collective-permute-start | bytes 442376 | tf_op jit(solution)/shard_map/ppermute | solution.py:232
  15.6 0.0 collective-permute-done.2
  15.6 0.8 %add.25 = f32[16,512]{1,0:T(8,128)S(1)} add(f32[16,512]{1,0:T(8,128)} %get-tuple-element.28, f32[16,512]{1,0:T(8,128)S(1)} %collective-permute-done.2) | non-fusion elementwise | flops 8192 | bytes 98304 | tf_op jit(solution)/shard_map/add | solution.py:328
  16.4 0.8 %collective-permute-done = f32[16,512]{1,0:T(8,128)S(1)} collective-permute-done((f32[16,512]{1,0:T(8,128)}, f32[16,512]{1,0:T(8,128)S(1)}, u32[]{:S(2)}, u32[]{:S(2)}) %collective-permute-start) | collective-permute-done | bytes 32800 | tf_op jit(solution)/shard_map/ppermute | solution.py:232
  17.2 1.4 %collective-permute-done.1 = f32[16,512]{1,0:T(8,128)S(1)} collective-permute-done((f32[16,512]{1,0:T(8,128)}, f32[16,512]{1,0:T(8,128)S(1)}, u32[]{:S(2)}, u32[]{:S(2)}) %collective-permute-start.1) | collective-permute-done | bytes 32800 | tf_op jit(solution)/shard_map/ppermute | solution.py:232
  18.6 0.0 collective-permute-done.3.refs_1_
  18.6 0.0 collective-permute-done.4
  18.6 1.6 %collective-permute-start.5 = (f32[16,512]{1,0:T(8,128)S(1)}, f32[16,512]{1,0:T(8,128)S(1)}, u32[]{:S(2)}, u32[]{:S(2)}) collective-permute-start(f32[16,512]{1,0:T(8,128)S(1)} %add_add_fusion.1), channel_id=1, source_target_pairs={{0,4},{4,0},{8,12},{12,8},{16,20},{20,16},{24,28},{28,24},{1,5},{5... | collective-permute-start | bytes 98312 | tf_op jit(solution)/shard_map/ppermute | solution.py:232
  20.2 0.9 %add.28 = f32[72,512]{1,0:T(8,128)S(1)} add(f32[72,512]{1,0:T(8,128)} %get-tuple-element.34, f32[72,512]{1,0:T(8,128)S(1)} %collective-permute-done.4) | non-fusion elementwise | flops 36864 | bytes 442368 | tf_op jit(solution)/shard_map/add | solution.py:333
  21.1 1.5 %collective-permute-done.5 = f32[16,512]{1,0:T(8,128)S(1)} collective-permute-done((f32[16,512]{1,0:T(8,128)S(1)}, f32[16,512]{1,0:T(8,128)S(1)}, u32[]{:S(2)}, u32[]{:S(2)}) %collective-permute-start.5) | collective-permute-done | bytes 32800 | tf_op jit(solution)/shard_map/ppermute | solution.py:232
  22.6 2.6 %collective-permute-start.8 = (f32[16,512]{1,0:T(8,128)S(1)}, f32[16,512]{1,0:T(8,128)S(1)}, u32[]{:S(2)}, u32[]{:S(2)}) collective-permute-start(f32[16,512]{1,0:T(8,128)S(1)} %add.27), channel_id=1, source_target_pairs={{0,16},{4,20},{8,24},{12,28},{16,0},{20,4},{24,8},{28,12},{1,17},{... | collective-permute-start | bytes 98312 | tf_op jit(solution)/shard_map/ppermute | solution.py:232
  25.2 1.3 %collective-permute-start.9 = (f32[16,512]{1,0:T(8,128)S(1)}, f32[16,512]{1,0:T(8,128)S(1)}, u32[]{:S(2)}, u32[]{:S(2)}) collective-permute-start(f32[16,512]{1,0:T(8,128)S(1)} %add.27), channel_id=1, source_target_pairs={{0,24},{4,28},{8,16},{12,20},{16,8},{20,12},{24,0},{28,4},{1,25},{... | collective-permute-start | bytes 98312 | tf_op jit(solution)/shard_map/ppermute | solution.py:232
  26.6 0.2 collective-permute-start.7
  26.8 0.9 %collective-permute-start.6 = (f32[72,512]{1,0:T(8,128)S(1)}, f32[72,512]{1,0:T(8,128)S(1)}, u32[]{:S(2)}, u32[]{:S(2)}) collective-permute-start(f32[72,512]{1,0:T(8,128)S(1)} %add.28), channel_id=1, source_target_pairs={{0,2},{1,3},{2,0},{3,1},{4,6},{5,7},{6,4},{7,5},{8,10},{9,11},{10,... | collective-permute-start | bytes 442376 | tf_op jit(solution)/shard_map/ppermute | solution.py:232
  27.6 0.0 collective-permute-done.8
  27.6 3.3 %collective-permute-done.9 = f32[16,512]{1,0:T(8,128)S(1)} collective-permute-done((f32[16,512]{1,0:T(8,128)S(1)}, f32[16,512]{1,0:T(8,128)S(1)}, u32[]{:S(2)}, u32[]{:S(2)}) %collective-permute-start.9) | collective-permute-done | bytes 32800 | tf_op jit(solution)/shard_map/ppermute | solution.py:232
  30.9 0.0 collective-permute-done.7
  30.9 0.1 collective-permute-start.10
  31.0 0.9 %collective-permute-start.11 = (f32[16,512]{1,0:T(8,128)S(1)}, f32[16,512]{1,0:T(8,128)S(1)}, u32[]{:S(2)}, u32[]{:S(2)}) collective-permute-start(f32[16,512]{1,0:T(8,128)S(1)} %add_add_fusion.refs_0_), channel_id=1, source_target_pairs={{0,2},{1,3},{2,0},{3,1},{4,6},{5,7},{6,4},{7,5},{8,10},{9,11},{10,... | collective-permute-start | bytes 98312 | tf_op jit(solution)/shard_map/ppermute | solution.py:232
  31.9 1.0 %collective-permute-start.12 = (f32[16,512]{1,0:T(8,128)S(1)}, f32[16,512]{1,0:T(8,128)S(1)}, u32[]{:S(2)}, u32[]{:S(2)}) collective-permute-start(f32[16,512]{1,0:T(8,128)S(1)} %add_add_fusion.refs_0_), channel_id=1, source_target_pairs={{0,3},{1,2},{2,1},{3,0},{4,7},{5,6},{6,5},{7,4},{8,11},{9,10},{10,... | collective-permute-start | bytes 98312 | tf_op jit(solution)/shard_map/ppermute | solution.py:232
  32.9 0.0 collective-permute-done.6.refs_2_
  32.9 0.9 %copy-done.1 = f32[72,512]{1,0:T(8,128)S(1)} copy-done((f32[72,512]{1,0:T(8,128)S(1)}, f32[72,512]{1,0:T(8,128)}, u32[]{:S(2)}) %copy-start.1) | copy-done | bytes 147480
  33.8 0.7 %county_totals.1 = (f32[64,512]{1,0:T(8,128)}, f32[8,128]{1,0:T(8,128)}, f32[69,512]{1,0:T(8,128)S(1)}, f32[4,64]{1,0:T(4,128)S(1)}) custom-call(s32[1,64]{1,0:T(1,128)S(1)} %bitcast.14, f32[64,512]{1,0:T(8,128)S(1)} %copy-done, f32[4,512]{1,0:T(4,128)S(1)} %copy-done.2, f32[1,512]{1,0:T(1,128)S(1)} %bitcast.12, f32[72,512]{1,0:T(8,128)S(1)} %copy-done.1, ...), custom_call_target="tpu_custom_call" | custom-call | tf_op jit(solution)/shard_map/county_totals/pallas_call | solution.py:339
  34.5 0.0 collective-permute-done.10.refs_1_
  34.5 0.6 %collective-permute-done.11.refs_2_ = f32[16,512]{1,0:T(8,128)S(1)} collective-permute-done((f32[16,512]{1,0:T(8,128)S(1)}, f32[16,512]{1,0:T(8,128)S(1)}, u32[]{:S(2)}, u32[]{:S(2)}) %collective-permute-start.11) | collective-permute-done | bytes 32800 | tf_op jit(solution)/shard_map/ppermute | solution.py:232
  35.1 0.4 collective-permute-done.12.refs_3_
  35.4 0.8 %upper_totals.1 = (f32[64,512]{1,0:T(8,128)}, f32[4,512]{1,0:T(4,128)}, f32[1,512]{1,0:T(1,128)}) custom-call(f32[69,512]{1,0:T(8,128)S(1)} %get-tuple-element.39.prior_ref, f32[4,64]{1,0:T(4,128)S(1)} %get-tuple-element.40.hot_ref, f32[16,512]{1,0:T(8,128)S(1)} %add_add_fusion.refs_0_, f32[16,512]{1,0:T(8,128)S(1)} %collective-permute-done.10.refs_1_, ...), custom_call_target="tpu_custom_call" | custom-call | tf_op jit(solution)/shard_map/upper_totals/pallas_call | solution.py:353
  (12 shorter events, 0.0 us)
Async XLA Ops:
  0.6 32.3 %copy-start.4 = (s32[64]{0:T(128)S(1)}, s32[64]{0:T(128)}, u32[]{:S(2)}) copy-start(s32[64]{0:T(128)} %param.23) | copy-start | bytes 772
  0.6 32.2 %copy-start = (f32[64,512]{1,0:T(8,128)S(1)}, f32[64,512]{1,0:T(8,128)}, u32[]{:S(2)}) copy-start(f32[64,512]{1,0:T(8,128)} %state_ref.1) | copy-start | bytes 393220
  0.7 32.2 %copy-start.2 = (f32[4,512]{1,0:T(4,128)S(1)}, f32[4,512]{1,0:T(4,128)}, u32[]{:S(2)}) copy-start(f32[4,512]{1,0:T(4,128)} %nation_ref.1) | copy-start | bytes 24580
  0.7 32.2 %copy-start.3 = (f32[512]{0:T(512)S(1)}, f32[512]{0:T(512)}, u32[]{:S(2)}) copy-start(f32[512]{0:T(512)} %param.16) | copy-start | bytes 6148
  11.9 3.7 %collective-permute-start.2 = (f32[16,512]{1,0:T(8,128)}, f32[16,512]{1,0:T(8,128)S(1)}, u32[]{:S(2)}, u32[]{:S(2)}) collective-permute-start(f32[16,512]{1,0:T(8,128)} %get-tuple-element.29), channel_id=1, source_target_pairs={{0,1},{1,0},{2,3},{3,2},{4,5},{5,4},{6,7},{7,6},{8,9},{9,8},{10,11... | collective-permute-start | bytes 98312 | tf_op jit(solution)/shard_map/ppermute | solution.py:232
  12.5 4.8 %collective-permute-start = (f32[16,512]{1,0:T(8,128)}, f32[16,512]{1,0:T(8,128)S(1)}, u32[]{:S(2)}, u32[]{:S(2)}) collective-permute-start(f32[16,512]{1,0:T(8,128)} %get-tuple-element.26), channel_id=1, source_target_pairs={{0,2},{1,3},{2,0},{3,1},{4,6},{5,7},{6,4},{7,5},{8,10},{9,11},{10,... | collective-permute-start | bytes 98312 | tf_op jit(solution)/shard_map/ppermute | solution.py:232
  15.0 3.6 %collective-permute-start.1 = (f32[16,512]{1,0:T(8,128)}, f32[16,512]{1,0:T(8,128)S(1)}, u32[]{:S(2)}, u32[]{:S(2)}) collective-permute-start(f32[16,512]{1,0:T(8,128)} %get-tuple-element.27), channel_id=1, source_target_pairs={{0,3},{1,2},{2,1},{3,0},{4,7},{5,6},{6,5},{7,4},{8,11},{9,10},{10,... | collective-permute-start | bytes 98312 | tf_op jit(solution)/shard_map/ppermute | solution.py:232
  15.1 3.5 %collective-permute-start.3 = (f32[72,512]{1,0:T(8,128)}, f32[72,512]{1,0:T(8,128)S(1)}, u32[]{:S(2)}, u32[]{:S(2)}) collective-permute-start(f32[72,512]{1,0:T(8,128)} %get-tuple-element.30), channel_id=1, source_target_pairs={{0,1},{1,0},{2,3},{3,2},{4,5},{5,4},{6,7},{7,6},{8,9},{9,8},{10,11... | collective-permute-start | bytes 442376 | tf_op jit(solution)/shard_map/ppermute | solution.py:232
  15.3 3.4 %collective-permute-start.4 = (f32[72,512]{1,0:T(8,128)}, f32[72,512]{1,0:T(8,128)S(1)}, u32[]{:S(2)}, u32[]{:S(2)}) collective-permute-start(f32[72,512]{1,0:T(8,128)} %get-tuple-element.31), channel_id=1, source_target_pairs={{0,1},{1,0},{2,3},{3,2},{4,5},{5,4},{6,7},{7,6},{8,9},{9,8},{10,11... | collective-permute-start | bytes 442376 | tf_op jit(solution)/shard_map/ppermute | solution.py:232
  18.6 4.0 %collective-permute-start.5 = (f32[16,512]{1,0:T(8,128)S(1)}, f32[16,512]{1,0:T(8,128)S(1)}, u32[]{:S(2)}, u32[]{:S(2)}) collective-permute-start(f32[16,512]{1,0:T(8,128)S(1)} %add_add_fusion.1), channel_id=1, source_target_pairs={{0,4},{4,0},{8,12},{12,8},{16,20},{20,16},{24,28},{28,24},{1,5},{5... | collective-permute-start | bytes 98312 | tf_op jit(solution)/shard_map/ppermute | solution.py:232
  22.6 5.0 %collective-permute-start.8 = (f32[16,512]{1,0:T(8,128)S(1)}, f32[16,512]{1,0:T(8,128)S(1)}, u32[]{:S(2)}, u32[]{:S(2)}) collective-permute-start(f32[16,512]{1,0:T(8,128)S(1)} %add.27), channel_id=1, source_target_pairs={{0,16},{4,20},{8,24},{12,28},{16,0},{20,4},{24,8},{28,12},{1,17},{... | collective-permute-start | bytes 98312 | tf_op jit(solution)/shard_map/ppermute | solution.py:232
  25.2 5.7 %collective-permute-start.9 = (f32[16,512]{1,0:T(8,128)S(1)}, f32[16,512]{1,0:T(8,128)S(1)}, u32[]{:S(2)}, u32[]{:S(2)}) collective-permute-start(f32[16,512]{1,0:T(8,128)S(1)} %add.27), channel_id=1, source_target_pairs={{0,24},{4,28},{8,16},{12,20},{16,8},{20,12},{24,0},{28,4},{1,25},{... | collective-permute-start | bytes 98312 | tf_op jit(solution)/shard_map/ppermute | solution.py:232
  26.6 4.4 %collective-permute-start.7 = (f32[16,512]{1,0:T(8,128)S(1)}, f32[16,512]{1,0:T(8,128)S(1)}, u32[]{:S(2)}, u32[]{:S(2)}) collective-permute-start(f32[16,512]{1,0:T(8,128)S(1)} %add.27), channel_id=1, source_target_pairs={{0,8},{4,12},{8,0},{12,4},{16,24},{20,28},{24,16},{28,20},{1,9},{5... | collective-permute-start | bytes 98312 | tf_op jit(solution)/shard_map/ppermute | solution.py:232
  26.8 6.1 %collective-permute-start.6 = (f32[72,512]{1,0:T(8,128)S(1)}, f32[72,512]{1,0:T(8,128)S(1)}, u32[]{:S(2)}, u32[]{:S(2)}) collective-permute-start(f32[72,512]{1,0:T(8,128)S(1)} %add.28), channel_id=1, source_target_pairs={{0,2},{1,3},{2,0},{3,1},{4,6},{5,7},{6,4},{7,5},{8,10},{9,11},{10,... | collective-permute-start | bytes 442376 | tf_op jit(solution)/shard_map/ppermute | solution.py:232
  30.9 3.6 %collective-permute-start.10 = (f32[16,512]{1,0:T(8,128)S(1)}, f32[16,512]{1,0:T(8,128)S(1)}, u32[]{:S(2)}, u32[]{:S(2)}) collective-permute-start(f32[16,512]{1,0:T(8,128)S(1)} %add_add_fusion.refs_0_), channel_id=1, source_target_pairs={{0,1},{1,0},{2,3},{3,2},{4,5},{5,4},{6,7},{7,6},{8,9},{9,8},{10,11... | collective-permute-start | bytes 98312 | tf_op jit(solution)/shard_map/ppermute | solution.py:232
  31.0 4.1 %collective-permute-start.11 = (f32[16,512]{1,0:T(8,128)S(1)}, f32[16,512]{1,0:T(8,128)S(1)}, u32[]{:S(2)}, u32[]{:S(2)}) collective-permute-start(f32[16,512]{1,0:T(8,128)S(1)} %add_add_fusion.refs_0_), channel_id=1, source_target_pairs={{0,2},{1,3},{2,0},{3,1},{4,6},{5,7},{6,4},{7,5},{8,10},{9,11},{10,... | collective-permute-start | bytes 98312 | tf_op jit(solution)/shard_map/ppermute | solution.py:232
  31.9 3.5 %collective-permute-start.12 = (f32[16,512]{1,0:T(8,128)S(1)}, f32[16,512]{1,0:T(8,128)S(1)}, u32[]{:S(2)}, u32[]{:S(2)}) collective-permute-start(f32[16,512]{1,0:T(8,128)S(1)} %add_add_fusion.refs_0_), channel_id=1, source_target_pairs={{0,3},{1,2},{2,1},{3,0},{4,7},{5,6},{6,5},{7,4},{8,11},{9,10},{10,... | collective-permute-start | bytes 98312 | tf_op jit(solution)/shard_map/ppermute | solution.py:232
  32.9 0.9 %copy-start.1 = (f32[72,512]{1,0:T(8,128)S(1)}, f32[72,512]{1,0:T(8,128)}, u32[]{:S(2)}) copy-start(f32[72,512]{1,0:T(8,128)} %get-tuple-element.25.refs_0_) | copy-start | bytes 442372

commit v13 on v12

--- a/solution.py
+++ b/solution.py
@@ -89,12 +89,10 @@
     ]
     for copy in small_copies:
         copy.start()
-    for j in range(2):
-        fetch(j).start()
+    fetch(0).start()
     for copy in small_copies:
         copy.wait()
-    for j in range(2, 4):
-        fetch(j).start()
+    fetch(1).start()
 
     states = county_state_ref[lax.axis_index("grp")]
     state_hot = (iota_rows(n_states) == states).astype(F32).astype(BF16)
@@ -142,6 +140,8 @@
         )
 
     fetch(0).wait()
+    for j in range(2, 4):
+        fetch(j).start()
     score(0, 0)
     fetch(1).wait()
     score(1, 1)
@@ -176,24 +176,27 @@
     prec_sum = prec_acc[:n_hi] + prec_acc[n_hi:]
     own_rows = pl.ds(pl.multiple_of(me * share, share), share)
 
-    def send(k):
-        copy = pltpu.make_async_copy(outs[k], out_refs[k], out_sems.at[k])
+    def send(source, target):
+        copy = pltpu.make_async_copy(source, target, out_sems.at[len(copies)])
         copy.start()
-        return copy
+        copies.append(copy)
 
     copies = []
-    for d in range(n_row):
-        peer = jnp.bitwise_xor(me, d)
-        sums = county_acc[pl.ds(pl.multiple_of(peer * share, share), share), :]
-        county_outs[d][:share, :] = sums if d else sums - county_ref[own_rows, :]
+    for d in range(1, n_row):
+        rows = pl.ds(pl.multiple_of(jnp.bitwise_xor(me, d) * share, share), share)
+        send(county_acc.at[rows], out_refs[n_row + d].at[pl.ds(0, share)])
+    for d in range(2):
         county_outs[d][share:, :LANES] = prec_sum if d else prec_sum - prec_ref[...]
         county_outs[d][share:, LANES:] = jnp.zeros((n_hi, p_size - LANES), F32)
-        copies.append(send(n_row + d))
+    for d in range(1, n_row):
+        send(county_outs[1].at[pl.ds(share, n_hi)], out_refs[n_row + d].at[pl.ds(share, n_hi)])
+    county_outs[0][:share, :] = county_acc[own_rows, :] - county_ref[own_rows, :]
+    send(county_outs[0], out_refs[n_row])
     state_acc[...] = hot_dot(state_hot, county_acc[...], ((1,), (0,)))
     for d in range(n_row):
         peer = jnp.bitwise_xor(me, d)
         state_outs[d][...] = state_acc[pl.ds(pl.multiple_of(peer * per, per), per), :]
-        copies.append(send(d))
+        send(outs[d], out_refs[d])
     for copy in copies:
         copy.wait()
 
@@ -318,7 +321,7 @@
         + [
             pltpu.SemaphoreType.DMA((SMALL,)),
             pltpu.SemaphoreType.DMA((steps,)),
-            pltpu.SemaphoreType.DMA((2 * n_row,)),
+            pltpu.SemaphoreType.DMA((3 * n_row,)),
         ],
         compiler_params=pltpu.CompilerParams(vmem_limit_bytes=VMEM_LIMIT),
         name="local_sums",

time: 36.5 us -> 36.4 us (level)
  no operation moved by 1% of the time
where the time goes in v13:
time: 36.4 us; the launch traced here: 36.1 us
  starting transfers between devices  12.3 us (34%)
  Pallas kernels  11.9 us (33%)
  waiting for transfers between devices  7.82 us (21%)
  other arithmetic  1.72 us (5%)
  between operations  1.43 us (4%)
  local copies, waits for them, and re-layouts  0.92 us (3%)
    ppermute x13, starting transfers between devices, swap(): return lax.ppermute(x, axis, [(i, i ^ d) for i in range(n)])  12.3 us
    pallas_call x1, Pallas kernels, on_device(): pl.pallas_call(functools.partial(main_kernel, 2 * n_row), in_specs=[pl.Bl...  10.5 us
    ppermute x13, waiting for transfers between devices, swap(): return lax.ppermute(x, axis, [(i, i ^ d) for i in range(n)])  7.82 us
    add x1, other arithmetic, on_device(): chip_sums = [county_outs[d] + from_core[d // 2] for d in range(2, n_row, 2)]  0.93 us
    unnamed x10, local copies, waits for them, and re-layouts  0.92 us
    pallas_call x1, Pallas kernels, on_device(): pl.pallas_call(end_kernel, out_shape=[jax.ShapeDtypeStruct(state_coef.sha...  0.79 us
    add x1, other arithmetic, on_device(): own_sum = lax.optimization_barrier(outs[0] + swap(outs[1], 'row', 1))  0.76 us
  transfers between devices with their start and end apart: 13, of which 6 were waited for; matrix products, arithmetic and copies ran while one was open for 5% of the time, Pallas kernels for 2%

profile of v13, /device:TPU:0, one launch (start us, length us, event | category | flops | bytes accessed | tf_op | source)
XLA Modules:
  0.0 36.1 jit_solution(14834206657337840200)
XLA Ops:
  1.4 10.5 %local_sums.1 = (f32[16,512]{1,0:T(8,128)}, f32[16,512]{1,0:T(8,128)}, f32[16,512]{1,0:T(8,128)}, f32[16,512]{1,0:T(8,128)}, f32[72,512]{1,0:T(8,128)}, /*index=...) custom-call(s32[1,1,1]{2,1,0:T(1,128)} %bitcast.10.count_ref, bf16[8192,512]{1,0:T(8,128)(2,1)} %features_ref.1, ...), custom_call_target="tpu_custom_call" | custom-call | tf_op jit(solution)/shard_map/local_sums/pallas_call | solution.py:294
  11.8 0.5 %collective-permute-start.2 = (f32[16,512]{1,0:T(8,128)}, f32[16,512]{1,0:T(8,128)S(1)}, u32[]{:S(2)}, u32[]{:S(2)}) collective-permute-start(f32[16,512]{1,0:T(8,128)} %get-tuple-element.29), channel_id=1, source_target_pairs={{0,1},{1,0},{2,3},{3,2},{4,5},{5,4},{6,7},{7,6},{8,9},{9,8},{10,11... | collective-permute-start | bytes 98312 | tf_op jit(solution)/shard_map/ppermute | solution.py:235
  12.4 2.6 %collective-permute-start = (f32[16,512]{1,0:T(8,128)}, f32[16,512]{1,0:T(8,128)S(1)}, u32[]{:S(2)}, u32[]{:S(2)}) collective-permute-start(f32[16,512]{1,0:T(8,128)} %get-tuple-element.26), channel_id=1, source_target_pairs={{0,2},{1,3},{2,0},{3,1},{4,6},{5,7},{6,4},{7,5},{8,10},{9,11},{10,... | collective-permute-start | bytes 98312 | tf_op jit(solution)/shard_map/ppermute | solution.py:235
  14.9 0.1 collective-permute-start.1
  15.0 0.1 collective-permute-start.3
  15.2 0.4 %collective-permute-start.4 = (f32[72,512]{1,0:T(8,128)}, f32[72,512]{1,0:T(8,128)S(1)}, u32[]{:S(2)}, u32[]{:S(2)}) collective-permute-start(f32[72,512]{1,0:T(8,128)} %get-tuple-element.31), channel_id=1, source_target_pairs={{0,1},{1,0},{2,3},{3,2},{4,5},{5,4},{6,7},{7,6},{8,9},{9,8},{10,11... | collective-permute-start | bytes 442376 | tf_op jit(solution)/shard_map/ppermute | solution.py:235
  15.5 0.0 collective-permute-done.2
  15.5 0.8 %add.25 = f32[16,512]{1,0:T(8,128)S(1)} add(f32[16,512]{1,0:T(8,128)} %get-tuple-element.28, f32[16,512]{1,0:T(8,128)S(1)} %collective-permute-done.2) | non-fusion elementwise | flops 8192 | bytes 98304 | tf_op jit(solution)/shard_map/add | solution.py:331
  16.3 0.8 %collective-permute-done = f32[16,512]{1,0:T(8,128)S(1)} collective-permute-done((f32[16,512]{1,0:T(8,128)}, f32[16,512]{1,0:T(8,128)S(1)}, u32[]{:S(2)}, u32[]{:S(2)}) %collective-permute-start) | collective-permute-done | bytes 32800 | tf_op jit(solution)/shard_map/ppermute | solution.py:235
  17.1 1.4 %collective-permute-done.1 = f32[16,512]{1,0:T(8,128)S(1)} collective-permute-done((f32[16,512]{1,0:T(8,128)}, f32[16,512]{1,0:T(8,128)S(1)}, u32[]{:S(2)}, u32[]{:S(2)}) %collective-permute-start.1) | collective-permute-done | bytes 32800 | tf_op jit(solution)/shard_map/ppermute | solution.py:235
  18.5 0.0 collective-permute-done.3.refs_1_
  18.5 0.0 collective-permute-done.4
  18.5 1.6 %collective-permute-start.5 = (f32[16,512]{1,0:T(8,128)S(1)}, f32[16,512]{1,0:T(8,128)S(1)}, u32[]{:S(2)}, u32[]{:S(2)}) collective-permute-start(f32[16,512]{1,0:T(8,128)S(1)} %add_add_fusion.1), channel_id=1, source_target_pairs={{0,4},{4,0},{8,12},{12,8},{16,20},{20,16},{24,28},{28,24},{1,5},{5... | collective-permute-start | bytes 98312 | tf_op jit(solution)/shard_map/ppermute | solution.py:235
  20.1 0.9 %add.28 = f32[72,512]{1,0:T(8,128)S(1)} add(f32[72,512]{1,0:T(8,128)} %get-tuple-element.34, f32[72,512]{1,0:T(8,128)S(1)} %collective-permute-done.4) | non-fusion elementwise | flops 36864 | bytes 442368 | tf_op jit(solution)/shard_map/add | solution.py:336
  21.1 1.5 %collective-permute-done.5 = f32[16,512]{1,0:T(8,128)S(1)} collective-permute-done((f32[16,512]{1,0:T(8,128)S(1)}, f32[16,512]{1,0:T(8,128)S(1)}, u32[]{:S(2)}, u32[]{:S(2)}) %collective-permute-start.5) | collective-permute-done | bytes 32800 | tf_op jit(solution)/shard_map/ppermute | solution.py:235
  22.5 2.6 %collective-permute-start.8 = (f32[16,512]{1,0:T(8,128)S(1)}, f32[16,512]{1,0:T(8,128)S(1)}, u32[]{:S(2)}, u32[]{:S(2)}) collective-permute-start(f32[16,512]{1,0:T(8,128)S(1)} %add.27), channel_id=1, source_target_pairs={{0,16},{4,20},{8,24},{12,28},{16,0},{20,4},{24,8},{28,12},{1,17},{... | collective-permute-start | bytes 98312 | tf_op jit(solution)/shard_map/ppermute | solution.py:235
  25.1 1.3 %collective-permute-start.9 = (f32[16,512]{1,0:T(8,128)S(1)}, f32[16,512]{1,0:T(8,128)S(1)}, u32[]{:S(2)}, u32[]{:S(2)}) collective-permute-start(f32[16,512]{1,0:T(8,128)S(1)} %add.27), channel_id=1, source_target_pairs={{0,24},{4,28},{8,16},{12,20},{16,8},{20,12},{24,0},{28,4},{1,25},{... | collective-permute-start | bytes 98312 | tf_op jit(solution)/shard_map/ppermute | solution.py:235
  26.5 0.2 collective-permute-start.7
  26.7 0.9 %collective-permute-start.6 = (f32[72,512]{1,0:T(8,128)S(1)}, f32[72,512]{1,0:T(8,128)S(1)}, u32[]{:S(2)}, u32[]{:S(2)}) collective-permute-start(f32[72,512]{1,0:T(8,128)S(1)} %add.28), channel_id=1, source_target_pairs={{0,2},{1,3},{2,0},{3,1},{4,6},{5,7},{6,4},{7,5},{8,10},{9,11},{10,... | collective-permute-start | bytes 442376 | tf_op jit(solution)/shard_map/ppermute | solution.py:235
  27.6 0.0 collective-permute-done.8
  27.6 3.2 %collective-permute-done.9 = f32[16,512]{1,0:T(8,128)S(1)} collective-permute-done((f32[16,512]{1,0:T(8,128)S(1)}, f32[16,512]{1,0:T(8,128)S(1)}, u32[]{:S(2)}, u32[]{:S(2)}) %collective-permute-start.9) | collective-permute-done | bytes 32800 | tf_op jit(solution)/shard_map/ppermute | solution.py:235
  30.8 0.0 collective-permute-done.7
  30.8 0.1 collective-permute-start.10
  30.9 0.9 %collective-permute-start.11 = (f32[16,512]{1,0:T(8,128)S(1)}, f32[16,512]{1,0:T(8,128)S(1)}, u32[]{:S(2)}, u32[]{:S(2)}) collective-permute-start(f32[16,512]{1,0:T(8,128)S(1)} %add_add_fusion.refs_0_), channel_id=1, source_target_pairs={{0,2},{1,3},{2,0},{3,1},{4,6},{5,7},{6,4},{7,5},{8,10},{9,11},{10,... | collective-permute-start | bytes 98312 | tf_op jit(solution)/shard_map/ppermute | solution.py:235
  31.9 0.9 %collective-permute-start.12 = (f32[16,512]{1,0:T(8,128)S(1)}, f32[16,512]{1,0:T(8,128)S(1)}, u32[]{:S(2)}, u32[]{:S(2)}) collective-permute-start(f32[16,512]{1,0:T(8,128)S(1)} %add_add_fusion.refs_0_), channel_id=1, source_target_pairs={{0,3},{1,2},{2,1},{3,0},{4,7},{5,6},{6,5},{7,4},{8,11},{9,10},{10,... | collective-permute-start | bytes 98312 | tf_op jit(solution)/shard_map/ppermute | solution.py:235
  32.8 0.0 collective-permute-done.6.refs_2_
  32.8 0.9 %copy-done.1 = f32[72,512]{1,0:T(8,128)S(1)} copy-done((f32[72,512]{1,0:T(8,128)S(1)}, f32[72,512]{1,0:T(8,128)}, u32[]{:S(2)}) %copy-start.1) | copy-done | bytes 147480
  33.7 0.7 %county_totals.1 = (f32[64,512]{1,0:T(8,128)}, f32[8,128]{1,0:T(8,128)}, f32[69,512]{1,0:T(8,128)S(1)}, f32[4,64]{1,0:T(4,128)S(1)}) custom-call(s32[1,64]{1,0:T(1,128)S(1)} %bitcast.14, f32[64,512]{1,0:T(8,128)S(1)} %copy-done, f32[4,512]{1,0:T(4,128)S(1)} %copy-done.2, f32[1,512]{1,0:T(1,128)S(1)} %bitcast.12, f32[72,512]{1,0:T(8,128)S(1)} %copy-done.1, ...), custom_call_target="tpu_custom_call" | custom-call | tf_op jit(solution)/shard_map/county_totals/pallas_call | solution.py:342
  34.4 0.0 collective-permute-done.10.refs_1_
  34.4 0.5 %collective-permute-done.11.refs_2_ = f32[16,512]{1,0:T(8,128)S(1)} collective-permute-done((f32[16,512]{1,0:T(8,128)S(1)}, f32[16,512]{1,0:T(8,128)S(1)}, u32[]{:S(2)}, u32[]{:S(2)}) %collective-permute-start.11) | collective-permute-done | bytes 32800 | tf_op jit(solution)/shard_map/ppermute | solution.py:235
  35.0 0.4 collective-permute-done.12.refs_3_
  35.3 0.8 %upper_totals.1 = (f32[64,512]{1,0:T(8,128)}, f32[4,512]{1,0:T(4,128)}, f32[1,512]{1,0:T(1,128)}) custom-call(f32[69,512]{1,0:T(8,128)S(1)} %get-tuple-element.39.prior_ref, f32[4,64]{1,0:T(4,128)S(1)} %get-tuple-element.40.hot_ref, f32[16,512]{1,0:T(8,128)S(1)} %add_add_fusion.refs_0_, f32[16,512]{1,0:T(8,128)S(1)} %collective-permute-done.10.refs_1_, ...), custom_call_target="tpu_custom_call" | custom-call | tf_op jit(solution)/shard_map/upper_totals/pallas_call | solution.py:356
  (12 shorter events, 0.0 us)
Async XLA Ops:
  0.6 32.2 %copy-start.4 = (s32[64]{0:T(128)S(1)}, s32[64]{0:T(128)}, u32[]{:S(2)}) copy-start(s32[64]{0:T(128)} %param.23) | copy-start | bytes 772
  0.6 32.1 %copy-start = (f32[64,512]{1,0:T(8,128)S(1)}, f32[64,512]{1,0:T(8,128)}, u32[]{:S(2)}) copy-start(f32[64,512]{1,0:T(8,128)} %state_ref.1) | copy-start | bytes 393220
  0.7 32.1 %copy-start.2 = (f32[4,512]{1,0:T(4,128)S(1)}, f32[4,512]{1,0:T(4,128)}, u32[]{:S(2)}) copy-start(f32[4,512]{1,0:T(4,128)} %nation_ref.1) | copy-start | bytes 24580
  0.7 32.1 %copy-start.3 = (f32[512]{0:T(512)S(1)}, f32[512]{0:T(512)}, u32[]{:S(2)}) copy-start(f32[512]{0:T(512)} %param.16) | copy-start | bytes 6148
  11.8 3.7 %collective-permute-start.2 = (f32[16,512]{1,0:T(8,128)}, f32[16,512]{1,0:T(8,128)S(1)}, u32[]{:S(2)}, u32[]{:S(2)}) collective-permute-start(f32[16,512]{1,0:T(8,128)} %get-tuple-element.29), channel_id=1, source_target_pairs={{0,1},{1,0},{2,3},{3,2},{4,5},{5,4},{6,7},{7,6},{8,9},{9,8},{10,11... | collective-permute-start | bytes 98312 | tf_op jit(solution)/shard_map/ppermute | solution.py:235
  12.4 4.8 %collective-permute-start = (f32[16,512]{1,0:T(8,128)}, f32[16,512]{1,0:T(8,128)S(1)}, u32[]{:S(2)}, u32[]{:S(2)}) collective-permute-start(f32[16,512]{1,0:T(8,128)} %get-tuple-element.26), channel_id=1, source_target_pairs={{0,2},{1,3},{2,0},{3,1},{4,6},{5,7},{6,4},{7,5},{8,10},{9,11},{10,... | collective-permute-start | bytes 98312 | tf_op jit(solution)/shard_map/ppermute | solution.py:235
  14.9 3.6 %collective-permute-start.1 = (f32[16,512]{1,0:T(8,128)}, f32[16,512]{1,0:T(8,128)S(1)}, u32[]{:S(2)}, u32[]{:S(2)}) collective-permute-start(f32[16,512]{1,0:T(8,128)} %get-tuple-element.27), channel_id=1, source_target_pairs={{0,3},{1,2},{2,1},{3,0},{4,7},{5,6},{6,5},{7,4},{8,11},{9,10},{10,... | collective-permute-start | bytes 98312 | tf_op jit(solution)/shard_map/ppermute | solution.py:235
  15.0 3.5 %collective-permute-start.3 = (f32[72,512]{1,0:T(8,128)}, f32[72,512]{1,0:T(8,128)S(1)}, u32[]{:S(2)}, u32[]{:S(2)}) collective-permute-start(f32[72,512]{1,0:T(8,128)} %get-tuple-element.30), channel_id=1, source_target_pairs={{0,1},{1,0},{2,3},{3,2},{4,5},{5,4},{6,7},{7,6},{8,9},{9,8},{10,11... | collective-permute-start | bytes 442376 | tf_op jit(solution)/shard_map/ppermute | solution.py:235
  15.2 3.4 %collective-permute-start.4 = (f32[72,512]{1,0:T(8,128)}, f32[72,512]{1,0:T(8,128)S(1)}, u32[]{:S(2)}, u32[]{:S(2)}) collective-permute-start(f32[72,512]{1,0:T(8,128)} %get-tuple-element.31), channel_id=1, source_target_pairs={{0,1},{1,0},{2,3},{3,2},{4,5},{5,4},{6,7},{7,6},{8,9},{9,8},{10,11... | collective-permute-start | bytes 442376 | tf_op jit(solution)/shard_map/ppermute | solution.py:235
  18.5 4.0 %collective-permute-start.5 = (f32[16,512]{1,0:T(8,128)S(1)}, f32[16,512]{1,0:T(8,128)S(1)}, u32[]{:S(2)}, u32[]{:S(2)}) collective-permute-start(f32[16,512]{1,0:T(8,128)S(1)} %add_add_fusion.1), channel_id=1, source_target_pairs={{0,4},{4,0},{8,12},{12,8},{16,20},{20,16},{24,28},{28,24},{1,5},{5... | collective-permute-start | bytes 98312 | tf_op jit(solution)/shard_map/ppermute | solution.py:235
  22.5 5.1 %collective-permute-start.8 = (f32[16,512]{1,0:T(8,128)S(1)}, f32[16,512]{1,0:T(8,128)S(1)}, u32[]{:S(2)}, u32[]{:S(2)}) collective-permute-start(f32[16,512]{1,0:T(8,128)S(1)} %add.27), channel_id=1, source_target_pairs={{0,16},{4,20},{8,24},{12,28},{16,0},{20,4},{24,8},{28,12},{1,17},{... | collective-permute-start | bytes 98312 | tf_op jit(solution)/shard_map/ppermute | solution.py:235
  25.1 5.7 %collective-permute-start.9 = (f32[16,512]{1,0:T(8,128)S(1)}, f32[16,512]{1,0:T(8,128)S(1)}, u32[]{:S(2)}, u32[]{:S(2)}) collective-permute-start(f32[16,512]{1,0:T(8,128)S(1)} %add.27), channel_id=1, source_target_pairs={{0,24},{4,28},{8,16},{12,20},{16,8},{20,12},{24,0},{28,4},{1,25},{... | collective-permute-start | bytes 98312 | tf_op jit(solution)/shard_map/ppermute | solution.py:235
  26.5 4.4 %collective-permute-start.7 = (f32[16,512]{1,0:T(8,128)S(1)}, f32[16,512]{1,0:T(8,128)S(1)}, u32[]{:S(2)}, u32[]{:S(2)}) collective-permute-start(f32[16,512]{1,0:T(8,128)S(1)} %add.27), channel_id=1, source_target_pairs={{0,8},{4,12},{8,0},{12,4},{16,24},{20,28},{24,16},{28,20},{1,9},{5... | collective-permute-start | bytes 98312 | tf_op jit(solution)/shard_map/ppermute | solution.py:235
  26.7 6.1 %collective-permute-start.6 = (f32[72,512]{1,0:T(8,128)S(1)}, f32[72,512]{1,0:T(8,128)S(1)}, u32[]{:S(2)}, u32[]{:S(2)}) collective-permute-start(f32[72,512]{1,0:T(8,128)S(1)} %add.28), channel_id=1, source_target_pairs={{0,2},{1,3},{2,0},{3,1},{4,6},{5,7},{6,4},{7,5},{8,10},{9,11},{10,... | collective-permute-start | bytes 442376 | tf_op jit(solution)/shard_map/ppermute | solution.py:235
  30.8 3.6 %collective-permute-start.10 = (f32[16,512]{1,0:T(8,128)S(1)}, f32[16,512]{1,0:T(8,128)S(1)}, u32[]{:S(2)}, u32[]{:S(2)}) collective-permute-start(f32[16,512]{1,0:T(8,128)S(1)} %add_add_fusion.refs_0_), channel_id=1, source_target_pairs={{0,1},{1,0},{2,3},{3,2},{4,5},{5,4},{6,7},{7,6},{8,9},{9,8},{10,11... | collective-permute-start | bytes 98312 | tf_op jit(solution)/shard_map/ppermute | solution.py:235
  30.9 4.0 %collective-permute-start.11 = (f32[16,512]{1,0:T(8,128)S(1)}, f32[16,512]{1,0:T(8,128)S(1)}, u32[]{:S(2)}, u32[]{:S(2)}) collective-permute-start(f32[16,512]{1,0:T(8,128)S(1)} %add_add_fusion.refs_0_), channel_id=1, source_target_pairs={{0,2},{1,3},{2,0},{3,1},{4,6},{5,7},{6,4},{7,5},{8,10},{9,11},{10,... | collective-permute-start | bytes 98312 | tf_op jit(solution)/shard_map/ppermute | solution.py:235
  31.9 3.5 %collective-permute-start.12 = (f32[16,512]{1,0:T(8,128)S(1)}, f32[16,512]{1,0:T(8,128)S(1)}, u32[]{:S(2)}, u32[]{:S(2)}) collective-permute-start(f32[16,512]{1,0:T(8,128)S(1)} %add_add_fusion.refs_0_), channel_id=1, source_target_pairs={{0,3},{1,2},{2,1},{3,0},{4,7},{5,6},{6,5},{7,4},{8,11},{9,10},{10,... | collective-permute-start | bytes 98312 | tf_op jit(solution)/shard_map/ppermute | solution.py:235
  32.8 0.9 %copy-start.1 = (f32[72,512]{1,0:T(8,128)S(1)}, f32[72,512]{1,0:T(8,128)}, u32[]{:S(2)}) copy-start(f32[72,512]{1,0:T(8,128)} %get-tuple-element.25.refs_0_) | copy-start | bytes 442372

commit v14 on v13

--- a/solution.py
+++ b/solution.py
@@ -89,10 +89,12 @@
     ]
     for copy in small_copies:
         copy.start()
-    fetch(0).start()
+    for j in range(2):
+        fetch(j).start()
     for copy in small_copies:
         copy.wait()
-    fetch(1).start()
+    for j in range(2, 4):
+        fetch(j).start()
 
     states = county_state_ref[lax.axis_index("grp")]
     state_hot = (iota_rows(n_states) == states).astype(F32).astype(BF16)
@@ -140,8 +142,6 @@
         )
 
     fetch(0).wait()
-    for j in range(2, 4):
-        fetch(j).start()
     score(0, 0)
     fetch(1).wait()
     score(1, 1)

time: 36.4 us -> 36.4 us (level)
  no operation moved by 1% of the time
where the time goes in v14:
time: 36.4 us; the launch traced here: 36.2 us
  starting transfers between devices  12.2 us (34%)
  Pallas kernels  12 us (33%)
  waiting for transfers between devices  7.92 us (22%)
  other arithmetic  1.72 us (5%)
  between operations  1.43 us (4%)
  local copies, waits for them, and re-layouts  0.92 us (3%)
    ppermute x13, starting transfers between devices, swap(): return lax.ppermute(x, axis, [(i, i ^ d) for i in range(n)])  12.2 us
    pallas_call x1, Pallas kernels, on_device(): pl.pallas_call(functools.partial(main_kernel, 2 * n_row), in_specs=[pl.Bl...  10.5 us
    ppermute x13, waiting for transfers between devices, swap(): return lax.ppermute(x, axis, [(i, i ^ d) for i in range(n)])  7.92 us
    add x1, other arithmetic, on_device(): chip_sums = [county_outs[d] + from_core[d // 2] for d in range(2, n_row, 2)]  0.93 us
    unnamed x10, local copies, waits for them, and re-layouts  0.92 us
    pallas_call x1, Pallas kernels, on_device(): pl.pallas_call(end_kernel, out_shape=[jax.ShapeDtypeStruct(state_coef.sha...  0.79 us
    add x1, other arithmetic, on_device(): own_sum = lax.optimization_barrier(outs[0] + swap(outs[1], 'row', 1))  0.76 us
  transfers between devices with their start and end apart: 13, of which 6 were waited for; matrix products, arithmetic and copies ran while one was open for 5% of the time, Pallas kernels for 2%

profile of v14, /device:TPU:0, one launch (start us, length us, event | category | flops | bytes accessed | tf_op | source)
XLA Modules:
  0.0 36.2 jit_solution(14010779692649717914)
XLA Ops:
  1.4 10.5 %local_sums.1 = (f32[16,512]{1,0:T(8,128)}, f32[16,512]{1,0:T(8,128)}, f32[16,512]{1,0:T(8,128)}, f32[16,512]{1,0:T(8,128)}, f32[72,512]{1,0:T(8,128)}, /*index=...) custom-call(s32[1,1,1]{2,1,0:T(1,128)} %bitcast.10.count_ref, bf16[8192,512]{1,0:T(8,128)(2,1)} %features_ref.1, ...), custom_call_target="tpu_custom_call" | custom-call | tf_op jit(solution)/shard_map/local_sums/pallas_call | solution.py:294
  11.9 0.5 %collective-permute-start.2 = (f32[16,512]{1,0:T(8,128)}, f32[16,512]{1,0:T(8,128)S(1)}, u32[]{:S(2)}, u32[]{:S(2)}) collective-permute-start(f32[16,512]{1,0:T(8,128)} %get-tuple-element.29), channel_id=1, source_target_pairs={{0,1},{1,0},{2,3},{3,2},{4,5},{5,4},{6,7},{7,6},{8,9},{9,8},{10,11... | collective-permute-start | bytes 98312 | tf_op jit(solution)/shard_map/ppermute | solution.py:235
  12.4 2.6 %collective-permute-start = (f32[16,512]{1,0:T(8,128)}, f32[16,512]{1,0:T(8,128)S(1)}, u32[]{:S(2)}, u32[]{:S(2)}) collective-permute-start(f32[16,512]{1,0:T(8,128)} %get-tuple-element.26), channel_id=1, source_target_pairs={{0,2},{1,3},{2,0},{3,1},{4,6},{5,7},{6,4},{7,5},{8,10},{9,11},{10,... | collective-permute-start | bytes 98312 | tf_op jit(solution)/shard_map/ppermute | solution.py:235
  15.0 0.1 collective-permute-start.1
  15.1 0.1 collective-permute-start.3
  15.2 0.4 %collective-permute-start.4 = (f32[72,512]{1,0:T(8,128)}, f32[72,512]{1,0:T(8,128)S(1)}, u32[]{:S(2)}, u32[]{:S(2)}) collective-permute-start(f32[72,512]{1,0:T(8,128)} %get-tuple-element.31), channel_id=1, source_target_pairs={{0,1},{1,0},{2,3},{3,2},{4,5},{5,4},{6,7},{7,6},{8,9},{9,8},{10,11... | collective-permute-start | bytes 442376 | tf_op jit(solution)/shard_map/ppermute | solution.py:235
  15.6 0.0 collective-permute-done.2
  15.6 0.8 %add.25 = f32[16,512]{1,0:T(8,128)S(1)} add(f32[16,512]{1,0:T(8,128)} %get-tuple-element.28, f32[16,512]{1,0:T(8,128)S(1)} %collective-permute-done.2) | non-fusion elementwise | flops 8192 | bytes 98304 | tf_op jit(solution)/shard_map/add | solution.py:331
  16.3 0.8 %collective-permute-done = f32[16,512]{1,0:T(8,128)S(1)} collective-permute-done((f32[16,512]{1,0:T(8,128)}, f32[16,512]{1,0:T(8,128)S(1)}, u32[]{:S(2)}, u32[]{:S(2)}) %collective-permute-start) | collective-permute-done | bytes 32800 | tf_op jit(solution)/shard_map/ppermute | solution.py:235
  17.2 1.4 %collective-permute-done.1 = f32[16,512]{1,0:T(8,128)S(1)} collective-permute-done((f32[16,512]{1,0:T(8,128)}, f32[16,512]{1,0:T(8,128)S(1)}, u32[]{:S(2)}, u32[]{:S(2)}) %collective-permute-start.1) | collective-permute-done | bytes 32800 | tf_op jit(solution)/shard_map/ppermute | solution.py:235
  18.5 0.0 collective-permute-done.3.refs_1_
  18.6 0.0 collective-permute-done.4
  18.6 1.6 %collective-permute-start.5 = (f32[16,512]{1,0:T(8,128)S(1)}, f32[16,512]{1,0:T(8,128)S(1)}, u32[]{:S(2)}, u32[]{:S(2)}) collective-permute-start(f32[16,512]{1,0:T(8,128)S(1)} %add_add_fusion.1), channel_id=1, source_target_pairs={{0,4},{4,0},{8,12},{12,8},{16,20},{20,16},{24,28},{28,24},{1,5},{5... | collective-permute-start | bytes 98312 | tf_op jit(solution)/shard_map/ppermute | solution.py:235
  20.1 0.9 %add.28 = f32[72,512]{1,0:T(8,128)S(1)} add(f32[72,512]{1,0:T(8,128)} %get-tuple-element.34, f32[72,512]{1,0:T(8,128)S(1)} %collective-permute-done.4) | non-fusion elementwise | flops 36864 | bytes 442368 | tf_op jit(solution)/shard_map/add | solution.py:336
  21.1 1.5 %collective-permute-done.5 = f32[16,512]{1,0:T(8,128)S(1)} collective-permute-done((f32[16,512]{1,0:T(8,128)S(1)}, f32[16,512]{1,0:T(8,128)S(1)}, u32[]{:S(2)}, u32[]{:S(2)}) %collective-permute-start.5) | collective-permute-done | bytes 32800 | tf_op jit(solution)/shard_map/ppermute | solution.py:235
  22.6 2.6 %collective-permute-start.8 = (f32[16,512]{1,0:T(8,128)S(1)}, f32[16,512]{1,0:T(8,128)S(1)}, u32[]{:S(2)}, u32[]{:S(2)}) collective-permute-start(f32[16,512]{1,0:T(8,128)S(1)} %add.27), channel_id=1, source_target_pairs={{0,16},{4,20},{8,24},{12,28},{16,0},{20,4},{24,8},{28,12},{1,17},{... | collective-permute-start | bytes 98312 | tf_op jit(solution)/shard_map/ppermute | solution.py:235
  25.1 1.3 %collective-permute-start.9 = (f32[16,512]{1,0:T(8,128)S(1)}, f32[16,512]{1,0:T(8,128)S(1)}, u32[]{:S(2)}, u32[]{:S(2)}) collective-permute-start(f32[16,512]{1,0:T(8,128)S(1)} %add.27), channel_id=1, source_target_pairs={{0,24},{4,28},{8,16},{12,20},{16,8},{20,12},{24,0},{28,4},{1,25},{... | collective-permute-start | bytes 98312 | tf_op jit(solution)/shard_map/ppermute | solution.py:235
  26.5 0.2 collective-permute-start.7
  26.7 0.8 %collective-permute-start.6 = (f32[72,512]{1,0:T(8,128)S(1)}, f32[72,512]{1,0:T(8,128)S(1)}, u32[]{:S(2)}, u32[]{:S(2)}) collective-permute-start(f32[72,512]{1,0:T(8,128)S(1)} %add.28), channel_id=1, source_target_pairs={{0,2},{1,3},{2,0},{3,1},{4,6},{5,7},{6,4},{7,5},{8,10},{9,11},{10,... | collective-permute-start | bytes 442376 | tf_op jit(solution)/shard_map/ppermute | solution.py:235
  27.6 0.0 collective-permute-done.8
  27.6 3.3 %collective-permute-done.9 = f32[16,512]{1,0:T(8,128)S(1)} collective-permute-done((f32[16,512]{1,0:T(8,128)S(1)}, f32[16,512]{1,0:T(8,128)S(1)}, u32[]{:S(2)}, u32[]{:S(2)}) %collective-permute-start.9) | collective-permute-done | bytes 32800 | tf_op jit(solution)/shard_map/ppermute | solution.py:235
  30.9 0.0 collective-permute-done.7
  30.9 0.1 collective-permute-start.10
  31.0 0.9 %collective-permute-start.11 = (f32[16,512]{1,0:T(8,128)S(1)}, f32[16,512]{1,0:T(8,128)S(1)}, u32[]{:S(2)}, u32[]{:S(2)}) collective-permute-start(f32[16,512]{1,0:T(8,128)S(1)} %add_add_fusion.refs_0_), channel_id=1, source_target_pairs={{0,2},{1,3},{2,0},{3,1},{4,6},{5,7},{6,4},{7,5},{8,10},{9,11},{10,... | collective-permute-start | bytes 98312 | tf_op jit(solution)/shard_map/ppermute | solution.py:235
  31.9 1.0 %collective-permute-start.12 = (f32[16,512]{1,0:T(8,128)S(1)}, f32[16,512]{1,0:T(8,128)S(1)}, u32[]{:S(2)}, u32[]{:S(2)}) collective-permute-start(f32[16,512]{1,0:T(8,128)S(1)} %add_add_fusion.refs_0_), channel_id=1, source_target_pairs={{0,3},{1,2},{2,1},{3,0},{4,7},{5,6},{6,5},{7,4},{8,11},{9,10},{10,... | collective-permute-start | bytes 98312 | tf_op jit(solution)/shard_map/ppermute | solution.py:235
  32.8 0.0 collective-permute-done.6.refs_2_
  32.9 0.9 %copy-done.1 = f32[72,512]{1,0:T(8,128)S(1)} copy-done((f32[72,512]{1,0:T(8,128)S(1)}, f32[72,512]{1,0:T(8,128)}, u32[]{:S(2)}) %copy-start.1) | copy-done | bytes 147480
  33.8 0.7 %county_totals.1 = (f32[64,512]{1,0:T(8,128)}, f32[8,128]{1,0:T(8,128)}, f32[69,512]{1,0:T(8,128)S(1)}, f32[4,64]{1,0:T(4,128)S(1)}) custom-call(s32[1,64]{1,0:T(1,128)S(1)} %bitcast.14, f32[64,512]{1,0:T(8,128)S(1)} %copy-done, f32[4,512]{1,0:T(4,128)S(1)} %copy-done.2, f32[1,512]{1,0:T(1,128)S(1)} %bitcast.12, f32[72,512]{1,0:T(8,128)S(1)} %copy-done.1, ...), custom_call_target="tpu_custom_call" | custom-call | tf_op jit(solution)/shard_map/county_totals/pallas_call | solution.py:342
  34.5 0.0 collective-permute-done.10.refs_1_
  34.5 0.6 %collective-permute-done.11.refs_2_ = f32[16,512]{1,0:T(8,128)S(1)} collective-permute-done((f32[16,512]{1,0:T(8,128)S(1)}, f32[16,512]{1,0:T(8,128)S(1)}, u32[]{:S(2)}, u32[]{:S(2)}) %collective-permute-start.11) | collective-permute-done | bytes 32800 | tf_op jit(solution)/shard_map/ppermute | solution.py:235
  35.0 0.4 collective-permute-done.12.refs_3_
  35.4 0.8 %upper_totals.1 = (f32[64,512]{1,0:T(8,128)}, f32[4,512]{1,0:T(4,128)}, f32[1,512]{1,0:T(1,128)}) custom-call(f32[69,512]{1,0:T(8,128)S(1)} %get-tuple-element.39.prior_ref, f32[4,64]{1,0:T(4,128)S(1)} %get-tuple-element.40.hot_ref, f32[16,512]{1,0:T(8,128)S(1)} %add_add_fusion.refs_0_, f32[16,512]{1,0:T(8,128)S(1)} %collective-permute-done.10.refs_1_, ...), custom_call_target="tpu_custom_call" | custom-call | tf_op jit(solution)/shard_map/upper_totals/pallas_call | solution.py:356
  (12 shorter events, 0.0 us)
Async XLA Ops:
  0.6 32.2 %copy-start.4 = (s32[64]{0:T(128)S(1)}, s32[64]{0:T(128)}, u32[]{:S(2)}) copy-start(s32[64]{0:T(128)} %param.23) | copy-start | bytes 772
  0.6 32.2 %copy-start = (f32[64,512]{1,0:T(8,128)S(1)}, f32[64,512]{1,0:T(8,128)}, u32[]{:S(2)}) copy-start(f32[64,512]{1,0:T(8,128)} %state_ref.1) | copy-start | bytes 393220
  0.7 32.2 %copy-start.2 = (f32[4,512]{1,0:T(4,128)S(1)}, f32[4,512]{1,0:T(4,128)}, u32[]{:S(2)}) copy-start(f32[4,512]{1,0:T(4,128)} %nation_ref.1) | copy-start | bytes 24580
  0.7 32.2 %copy-start.3 = (f32[512]{0:T(512)S(1)}, f32[512]{0:T(512)}, u32[]{:S(2)}) copy-start(f32[512]{0:T(512)} %param.16) | copy-start | bytes 6148
  11.9 3.7 %collective-permute-start.2 = (f32[16,512]{1,0:T(8,128)}, f32[16,512]{1,0:T(8,128)S(1)}, u32[]{:S(2)}, u32[]{:S(2)}) collective-permute-start(f32[16,512]{1,0:T(8,128)} %get-tuple-element.29), channel_id=1, source_target_pairs={{0,1},{1,0},{2,3},{3,2},{4,5},{5,4},{6,7},{7,6},{8,9},{9,8},{10,11... | collective-permute-start | bytes 98312 | tf_op jit(solution)/shard_map/ppermute | solution.py:235
  12.4 4.8 %collective-permute-start = (f32[16,512]{1,0:T(8,128)}, f32[16,512]{1,0:T(8,128)S(1)}, u32[]{:S(2)}, u32[]{:S(2)}) collective-permute-start(f32[16,512]{1,0:T(8,128)} %get-tuple-element.26), channel_id=1, source_target_pairs={{0,2},{1,3},{2,0},{3,1},{4,6},{5,7},{6,4},{7,5},{8,10},{9,11},{10,... | collective-permute-start | bytes 98312 | tf_op jit(solution)/shard_map/ppermute | solution.py:235
  15.0 3.6 %collective-permute-start.1 = (f32[16,512]{1,0:T(8,128)}, f32[16,512]{1,0:T(8,128)S(1)}, u32[]{:S(2)}, u32[]{:S(2)}) collective-permute-start(f32[16,512]{1,0:T(8,128)} %get-tuple-element.27), channel_id=1, source_target_pairs={{0,3},{1,2},{2,1},{3,0},{4,7},{5,6},{6,5},{7,4},{8,11},{9,10},{10,... | collective-permute-start | bytes 98312 | tf_op jit(solution)/shard_map/ppermute | solution.py:235
  15.1 3.5 %collective-permute-start.3 = (f32[72,512]{1,0:T(8,128)}, f32[72,512]{1,0:T(8,128)S(1)}, u32[]{:S(2)}, u32[]{:S(2)}) collective-permute-start(f32[72,512]{1,0:T(8,128)} %get-tuple-element.30), channel_id=1, source_target_pairs={{0,1},{1,0},{2,3},{3,2},{4,5},{5,4},{6,7},{7,6},{8,9},{9,8},{10,11... | collective-permute-start | bytes 442376 | tf_op jit(solution)/shard_map/ppermute | solution.py:235
  15.2 3.4 %collective-permute-start.4 = (f32[72,512]{1,0:T(8,128)}, f32[72,512]{1,0:T(8,128)S(1)}, u32[]{:S(2)}, u32[]{:S(2)}) collective-permute-start(f32[72,512]{1,0:T(8,128)} %get-tuple-element.31), channel_id=1, source_target_pairs={{0,1},{1,0},{2,3},{3,2},{4,5},{5,4},{6,7},{7,6},{8,9},{9,8},{10,11... | collective-permute-start | bytes 442376 | tf_op jit(solution)/shard_map/ppermute | solution.py:235
  18.6 4.0 %collective-permute-start.5 = (f32[16,512]{1,0:T(8,128)S(1)}, f32[16,512]{1,0:T(8,128)S(1)}, u32[]{:S(2)}, u32[]{:S(2)}) collective-permute-start(f32[16,512]{1,0:T(8,128)S(1)} %add_add_fusion.1), channel_id=1, source_target_pairs={{0,4},{4,0},{8,12},{12,8},{16,20},{20,16},{24,28},{28,24},{1,5},{5... | collective-permute-start | bytes 98312 | tf_op jit(solution)/shard_map/ppermute | solution.py:235
  22.6 5.0 %collective-permute-start.8 = (f32[16,512]{1,0:T(8,128)S(1)}, f32[16,512]{1,0:T(8,128)S(1)}, u32[]{:S(2)}, u32[]{:S(2)}) collective-permute-start(f32[16,512]{1,0:T(8,128)S(1)} %add.27), channel_id=1, source_target_pairs={{0,16},{4,20},{8,24},{12,28},{16,0},{20,4},{24,8},{28,12},{1,17},{... | collective-permute-start | bytes 98312 | tf_op jit(solution)/shard_map/ppermute | solution.py:235
  25.1 5.7 %collective-permute-start.9 = (f32[16,512]{1,0:T(8,128)S(1)}, f32[16,512]{1,0:T(8,128)S(1)}, u32[]{:S(2)}, u32[]{:S(2)}) collective-permute-start(f32[16,512]{1,0:T(8,128)S(1)} %add.27), channel_id=1, source_target_pairs={{0,24},{4,28},{8,16},{12,20},{16,8},{20,12},{24,0},{28,4},{1,25},{... | collective-permute-start | bytes 98312 | tf_op jit(solution)/shard_map/ppermute | solution.py:235
  26.5 4.4 %collective-permute-start.7 = (f32[16,512]{1,0:T(8,128)S(1)}, f32[16,512]{1,0:T(8,128)S(1)}, u32[]{:S(2)}, u32[]{:S(2)}) collective-permute-start(f32[16,512]{1,0:T(8,128)S(1)} %add.27), channel_id=1, source_target_pairs={{0,8},{4,12},{8,0},{12,4},{16,24},{20,28},{24,16},{28,20},{1,9},{5... | collective-permute-start | bytes 98312 | tf_op jit(solution)/shard_map/ppermute | solution.py:235
  26.7 6.1 %collective-permute-start.6 = (f32[72,512]{1,0:T(8,128)S(1)}, f32[72,512]{1,0:T(8,128)S(1)}, u32[]{:S(2)}, u32[]{:S(2)}) collective-permute-start(f32[72,512]{1,0:T(8,128)S(1)} %add.28), channel_id=1, source_target_pairs={{0,2},{1,3},{2,0},{3,1},{4,6},{5,7},{6,4},{7,5},{8,10},{9,11},{10,... | collective-permute-start | bytes 442376 | tf_op jit(solution)/shard_map/ppermute | solution.py:235
  30.9 3.6 %collective-permute-start.10 = (f32[16,512]{1,0:T(8,128)S(1)}, f32[16,512]{1,0:T(8,128)S(1)}, u32[]{:S(2)}, u32[]{:S(2)}) collective-permute-start(f32[16,512]{1,0:T(8,128)S(1)} %add_add_fusion.refs_0_), channel_id=1, source_target_pairs={{0,1},{1,0},{2,3},{3,2},{4,5},{5,4},{6,7},{7,6},{8,9},{9,8},{10,11... | collective-permute-start | bytes 98312 | tf_op jit(solution)/shard_map/ppermute | solution.py:235
  31.0 4.1 %collective-permute-start.11 = (f32[16,512]{1,0:T(8,128)S(1)}, f32[16,512]{1,0:T(8,128)S(1)}, u32[]{:S(2)}, u32[]{:S(2)}) collective-permute-start(f32[16,512]{1,0:T(8,128)S(1)} %add_add_fusion.refs_0_), channel_id=1, source_target_pairs={{0,2},{1,3},{2,0},{3,1},{4,6},{5,7},{6,4},{7,5},{8,10},{9,11},{10,... | collective-permute-start | bytes 98312 | tf_op jit(solution)/shard_map/ppermute | solution.py:235
  31.9 3.5 %collective-permute-start.12 = (f32[16,512]{1,0:T(8,128)S(1)}, f32[16,512]{1,0:T(8,128)S(1)}, u32[]{:S(2)}, u32[]{:S(2)}) collective-permute-start(f32[16,512]{1,0:T(8,128)S(1)} %add_add_fusion.refs_0_), channel_id=1, source_target_pairs={{0,3},{1,2},{2,1},{3,0},{4,7},{5,6},{6,5},{7,4},{8,11},{9,10},{10,... | collective-permute-start | bytes 98312 | tf_op jit(solution)/shard_map/ppermute | solution.py:235
  32.8 0.9 %copy-start.1 = (f32[72,512]{1,0:T(8,128)S(1)}, f32[72,512]{1,0:T(8,128)}, u32[]{:S(2)}) copy-start(f32[72,512]{1,0:T(8,128)} %get-tuple-element.25.refs_0_) | copy-start | bytes 442372
